TPU v7x, 32 devices: a whole 2x2x4 slice. The times are simulated.
32 devices in a mesh: pipe: 4 (over y, core), req: 2 (over x), tp: 4 (over z).
Axes of the slice: x: 2, y: 2, z: 4, core: 2. Of those that a mesh axis runs over, the one named last changes fastest.
Arguments:
- hidden: bfloat16 [256, 8192], P('req', 'tp'), may hold values from -64 to 64
- queries: bfloat16 [4, 256, 4096], P('pipe', 'req', 'tp'), may hold values from -32 to 32
- norm_gain: bfloat16 [4, 8192], P('pipe'), may hold values from 0.5 to 1.5
- kv_weight: bfloat16 [4, 8192, 2, 512], P('pipe', None, None, 'tp'), may hold values from -0.0625 to 0.0625
- adapter_in: bfloat16 [4, 8, 64, 4096], P('pipe', 'req', None, 'tp'), may hold values from -0.09375 to 0.09375
- adapter_out: bfloat16 [4, 8, 64, 8192], P('pipe', 'req', None, 'tp'), may hold values from -3 to 3
- kv_pages: bfloat16 [4, 256, 2, 64, 512], P('pipe', 'req', None, None, 'tp'), may hold values from -4 to 4
- adapter_ids: int32 [64], P('req'), may hold values from 0 to 7, as said below
- owner_rows: int32 [8], replicated, may hold values from 0 to 7, as said below
- page_table: int32 [64, 4], P('req'), may hold values from 0 to 127, as said below
- lengths: int32 [64], P('req'), may hold values from 1 to 252, as said below
- moves: int32 [32, 3], P('req'), may hold values from 0 to 127, as said below
Outputs:
- section_out: bfloat16 [4, 256, 8192], P('pipe', 'req', 'tp')
- new_kv: bfloat16 [4, 256, 2, 512], P('pipe', 'req', None, 'tp')
- arrived: bfloat16 [4, 32, 2, 64, 512], P('pipe', 'req', None, None, 'tp')
Inputs may be any that keep to these rules, and one draw needn't show every extreme that they name: `adapter_ids`: adapter a is stored at row owner_rows[a], on request device owner_rows[a] // 4. In each aligned block of 16 requests at most 16 requests have adapters stored on one request device, and in every block some device stores exactly 16 of them. `owner_rows`: each storage row once. `page_table`: the 128 slots of one request device are each named once by its requests. `lengths`: every request device has a request of length 252. `moves`: row i * 16 + k belongs to request device i. Its destination differs from i; its source slots are distinct; at most 16 of its rows name one destination, exactly 16 for some; destination slots are below 16 and distinct among all rows that name one destination.
All inputs are finite; a program needn't handle non-finite values.
Results may differ from a plain program's by a relative error of at most 0.02.
Values may be sent and summed in bfloat16 or wider, within the bound.
No kernel may reach another device: no remote copies, remote signals or barrier semaphores. Data moves between devices by JAX's collectives and lax.ppermute only.
A program may use at most 128 MiB of HBM per device.

v0:
```python
import math

import jax
import jax.numpy as jnp
from jax import lax
from jax.sharding import PartitionSpec as P

D = 8192
HD = 128
R = 64
ADP_DEV = 4
RQ = 32
S = 4
MICRO = 2
PAGE = 64
MOVES = 16
RQ_MB = 16
CTX = 256


def passed_along(block, axis, distance):
    devices = range(lax.axis_size(axis))
    route = [(i - distance, i) for i in devices if i - distance in devices]
    return lax.ppermute(block, axis, route)


def rotate(key_vecs, positions):
    half_dim = key_vecs.shape[-1] // 2
    inv_freq = jnp.exp(
        -math.log(500000.0) * (2.0 * jnp.arange(half_dim, dtype=jnp.float32) / key_vecs.shape[-1])
    )
    angles = positions.astype(jnp.float32)[..., None, None] * inv_freq
    cos_vals = jnp.cos(angles)
    sin_vals = jnp.sin(angles)
    front_half = key_vecs[..., :half_dim]
    back_half = key_vecs[..., half_dim:]
    return jnp.concatenate(
        [
            front_half * cos_vals - back_half * sin_vals,
            back_half * cos_vals + front_half * sin_vals,
        ],
        axis=-1,
    )


def body(
    hidden,
    queries,
    norm_gain,
    kv_weight,
    adapter_in,
    adapter_out,
    kv_pages,
    adapter_ids,
    owner_rows,
    page_table,
    lengths,
    moves,
):
    section_count = lax.axis_size("pipe")
    req_count = lax.axis_size("req")
    section_id = lax.axis_index("pipe")
    my_req = lax.axis_index("req")
    width_loc = hidden.shape[1]
    q_width = queries.shape[2]
    kv_width = kv_weight.shape[3]
    kv_heads = kv_width // HD
    group_size = q_width // HD // kv_heads
    batches = 1
    per_batch = RQ // batches
    rows_per = per_batch * S
    block_cap = min(RQ_MB, max(2, 2 * RQ_MB // req_count))
    batch_cap = block_cap * (MICRO // batches)
    pair_cap = (MOVES + req_count - 2) // (req_count - 1)
    free_slots = (req_count - 1) * pair_cap
    token_ids = jnp.arange(S, dtype=jnp.int32)
    store_rows = owner_rows[adapter_ids]
    dest_all = store_rows // ADP_DEV
    pick_all = store_rows % ADP_DEV
    req_ids = jnp.arange(RQ, dtype=jnp.int32)
    earlier = (
        (req_ids[None, :] < req_ids[:, None])
        & (req_ids[None, :] // per_batch == req_ids[:, None] // per_batch)
        & (dest_all[None, :] == dest_all[:, None])
    )
    slot_all = jnp.sum(earlier.astype(jnp.int32), axis=1)
    positions = (lengths[:, None] + token_ids[None, :]).reshape(RQ * S)
    gain_full = norm_gain[0].astype(jnp.float32)
    weight_flat = kv_weight[0].reshape(D, 2 * kv_width)
    layer_pages = kv_pages[0]
    adapters_in = adapter_in[0]
    adapters_out = adapter_out[0].reshape(ADP_DEV * R, width_loc)
    key_pos = jnp.arange(CTX, dtype=jnp.int32)
    causal = token_ids[None, :] <= token_ids[:, None]
    adapter_slots = jnp.arange(ADP_DEV, dtype=jnp.int32)
    carried = jnp.zeros((rows_per, width_loc), jnp.bfloat16)
    section_rows = jnp.zeros((RQ * S, width_loc), jnp.bfloat16)
    fresh_rows = jnp.zeros((RQ * S, 2, kv_width), jnp.bfloat16)
    for tick_id in range(batches + section_count - 1):
        offset_batch = tick_id - section_id
        active = (offset_batch >= 0) & (offset_batch < batches)
        hstate = jnp.where(section_id == 0, hidden, carried)
        whole_rows = lax.all_gather(hstate, "tp", axis=1, tiled=True)
        widened = whole_rows.astype(jnp.float32)
        inv_rms = lax.rsqrt(jnp.mean(widened * widened, axis=-1, keepdims=True) + 1e-05)
        normed = (widened * inv_rms * gain_full).astype(jnp.bfloat16)
        projected = jnp.dot(normed, weight_flat, preferred_element_type=jnp.float32).reshape(
            rows_per, 2, kv_heads, HD
        )
        new_keys = rotate(projected[:, 0], positions).astype(jnp.bfloat16)
        new_values = projected[:, 1].astype(jnp.bfloat16)
        fresh_kv = jnp.stack(
            [new_keys.reshape(rows_per, kv_width), new_values.reshape(rows_per, kv_width)], axis=1
        )
        gathered = layer_pages[page_table]
        cached = jnp.swapaxes(gathered, 1, 2).reshape(per_batch, 2, CTX, kv_heads, HD)
        fresh_heads = fresh_kv.reshape(per_batch, S, 2, kv_heads, HD)
        query_heads = queries[0].reshape(per_batch, S, kv_heads, group_size, HD)
        score_old = jnp.einsum(
            "bskgd,btkd->bskgt", query_heads, cached[:, 0], preferred_element_type=jnp.float32
        ) * HD ** (-0.5)
        score_new = jnp.einsum(
            "bskgd,btkd->bskgt",
            query_heads,
            fresh_heads[:, :, 0],
            preferred_element_type=jnp.float32,
        ) * HD ** (-0.5)
        old_ok = key_pos[None, :] < lengths[:, None]
        score_old = jnp.where(old_ok[:, None, None, None, :], score_old, -jnp.inf)
        score_new = jnp.where(causal[None, :, None, None, :], score_new, -jnp.inf)
        row_max = jnp.maximum(jnp.max(score_old, axis=-1), jnp.max(score_new, axis=-1))[..., None]
        exp_old = jnp.exp(score_old - row_max)
        exp_new = jnp.exp(score_new - row_max)
        denominator = (jnp.sum(exp_old, axis=-1) + jnp.sum(exp_new, axis=-1))[..., None]
        weight_old = (exp_old / denominator).astype(jnp.bfloat16)
        weight_new = (exp_new / denominator).astype(jnp.bfloat16)
        mixed = jnp.einsum(
            "bskgt,btkd->bskgd", weight_old, cached[:, 1], preferred_element_type=jnp.float32
        )
        mixed = mixed + jnp.einsum(
            "bskgt,btkd->bskgd",
            weight_new,
            fresh_heads[:, :, 1],
            preferred_element_type=jnp.float32,
        )
        attended = mixed.reshape(per_batch, S, q_width).astype(jnp.bfloat16)
        outgoing = (
            jnp.zeros((req_count, batch_cap, S, q_width), jnp.bfloat16)
            .at[dest_all, slot_all]
            .set(attended)
        )
        picks_out = (
            jnp.zeros((req_count, batch_cap), jnp.int32).at[dest_all, slot_all].set(pick_all)
        )
        rows_in = lax.all_to_all(outgoing, "req", split_axis=0, concat_axis=0, tiled=True)
        picks_in = lax.all_to_all(picks_out, "req", split_axis=0, concat_axis=0, tiled=True)
        sources = rows_in.shape[0]
        item_count = rows_in.shape[1]
        flat_rows = rows_in.reshape(sources * item_count * S, q_width)
        all_low = jnp.einsum(
            "nf,arf->nar", flat_rows, adapters_in, preferred_element_type=jnp.float32
        )
        picks_rows = jnp.broadcast_to(picks_in[:, :, None], (sources, item_count, S)).reshape(
            sources * item_count * S
        )
        one_hot = (picks_rows[:, None] == adapter_slots[None, :]).astype(jnp.float32)
        partial_low = jnp.sum(all_low * one_hot[:, :, None], axis=1)
        rank_low = lax.psum(partial_low, "tp").astype(jnp.bfloat16)
        spread = (rank_low.astype(jnp.float32)[:, None, :] * one_hot[:, :, None]).astype(
            jnp.bfloat16
        )
        deltas = jnp.dot(
            spread.reshape(sources * item_count * S, ADP_DEV * R),
            adapters_out,
            preferred_element_type=jnp.float32,
        ).astype(jnp.bfloat16)
        deltas = deltas.reshape(sources, item_count, S, width_loc)
        returned = lax.all_to_all(deltas, "req", split_axis=0, concat_axis=0, tiled=True)
        delta_rows = returned[dest_all, slot_all].reshape(rows_per, width_loc)
        new_state = (hstate.astype(jnp.float32) + delta_rows.astype(jnp.float32)).astype(
            jnp.bfloat16
        )
        section_rows = jnp.where(active, new_state, section_rows)
        fresh_rows = jnp.where(active, fresh_kv, fresh_rows)
        carried = passed_along(new_state, "pipe", 1)
    page_slot = jnp.take_along_axis(page_table, (positions // PAGE).reshape(RQ, S), axis=1).reshape(
        RQ * S
    )
    written = layer_pages.at[page_slot, :, positions % PAGE, :].set(fresh_rows)
    leaving = written[moves[:, 1]]
    empty_pages = jnp.zeros((free_slots, 2, PAGE, kv_width), jnp.bfloat16)
    received, dest_in, spots_in = (
        lax.all_gather(leaving, "req", axis=0, tiled=True),
        lax.all_gather(moves[:, 0], "req", axis=0, tiled=True),
        lax.all_gather(moves[:, 2], "req", axis=0, tiled=True),
    )
    target = jnp.where(dest_in == my_req, spots_in, free_slots)
    arrived = empty_pages.at[target].set(received, mode="drop")
    return (section_rows[None], fresh_rows[None], arrived[None])


def solution(mesh):
    in_specs = (
        P("req", "tp"),
        P("pipe", "req", "tp"),
        P("pipe", None),
        P("pipe", None, None, "tp"),
        P("pipe", "req", None, "tp"),
        P("pipe", "req", None, "tp"),
        P("pipe", "req", None, None, "tp"),
        P("req"),
        P(),
        P("req", None),
        P("req"),
        P("req", None),
    )
    out_specs = (
        P("pipe", "req", "tp"),
        P("pipe", "req", None, "tp"),
        P("pipe", "req", None, None, "tp"),
    )
    return jax.shard_map(body, mesh=mesh, in_specs=in_specs, out_specs=out_specs, check_vma=False)
```

profile of v0, /device:TPU:0, one launch (start us, length us, event | category | flops | bytes accessed | tf_op | source)
XLA Modules:
  0.0 547.3 jit_solution(7893575389813634621)
XLA Ops:
  12.0 5.3 scatter_fusion.1
  17.3 4.2 all-to-all-start.1
  21.5 4.7 copy.110
  26.2 6.5 %copy.78 = bf16[256,8192]{1,0:T(8,128)(2,1)} copy(bf16[256,8192]{0,1:T(8,128)(2,1)} %bitcast.357) | data formatting | bytes 8388608 | tf_op jit(solution)/shard_map/dot_general | solution.py:107
  33.0 12.7 %copy.111 = bf16[1,128,2,64,128]{4,2,3,1,0:T(2,128)(2,1)} copy(bf16[1,128,2,64,128]{4,3,2,1,0:T(8,128)(2,1)} %param.18) | data formatting | bytes 8388608 | tf_op args[6]
  45.9 14.5 %gather_fusion.1 = bf16[128,2,64,128]{3,1,2,0:T(2,128)(2,1)} fusion(bf16[128,2,64,128]{3,1,2,0:T(2,128)(2,1)} %bitcast.354, s32[1024]{0:T(1024)S(1)} %pad_clamp_fusion.1), kind=kCustom, calls=%fused_computation.1 | custom fusion | bytes 8389120 | tf_op jit(solution)/shard_map/gather | solution.py:115
  60.4 3.3 copy.77
  68.7 4.2 fusion.22
  75.5 2.9 fusion.38
  80.9 4.6 scatter_fusion
  85.6 3.5 all-to-all-start
  89.3 7.3 %all-to-all-done = bf16[2,32,4,1024]{3,2,1,0:T(4,128)(2,1)S(1)} async-done(((bf16[2,32,4,1024]{3,2,1,0:T(4,128)(2,1)}), bf16[2,32,4,1024]{3,2,1,0:T(4,128)(2,1)S(1)}, u32[]{:S(2)}, u32[]{:S(2)}) %all-to-all-start) | async-done | bytes 524320 | tf_op jit(solution)/shard_map/all_to_all | solution.py:155
  98.1 20.1 %psum.28 = bf16[256,64]{0,1:T(8,128)(2,1)S(1)} all-reduce(f32[256,64]{0,1:T(8,128)S(1)} %fusion.53), channel_id=1, replica_groups=mesh['pipe'=4,'req'=2,'tp'=4] {'tp'}, use_global_device_ids=true, to_apply=%region_9.10 | all-reduce | flops 16384 | bytes 98304 | tf_op jit(solution)/shard_map/psum | solution.py:168
  119.8 2.3 reshape.1462
  122.0 13.8 %all_to_all.52 = bf16[2,32,4,2048]{3,2,1,0:T(4,128)(2,1)} all-to-all(bf16[2,32,4,2048]{3,2,1,0:T(4,128)(2,1)} %reshape.1462), channel_id=1, replica_groups=mesh['pipe'=4,'req'=2,'tp'=4] {'req'}, dimensions={0} | all-to-all | bytes 2097152 | tf_op jit(solution)/shard_map/all_to_all | solution.py:178
  135.9 2.3 gather_fusion.2
  145.4 50.9 %all-gather.11.cloned.1.call-done = bf16[128,8192]{1,0:T(8,128)(2,1)} async-done(((bf16[128,2048]{1,0:T(8,128)(2,1)}), bf16[128,8192]{1,0:T(8,128)(2,1)}) %all-gather.11.cloned.1.call-update) | async-done | bytes 2097168 | tf_op jit(solution)/shard_map/all_gather | solution.py:103
  198.4 4.2 fusion.57
  206.6 3.0 fusion.37
  213.2 11.3 %all_to_all.53 = bf16[2,32,4,1024]{3,2,1,0:T(4,128)(2,1)} all-to-all(bf16[2,32,4,1024]{3,2,1,0:T(4,128)(2,1)S(1)} %scatter_fusion.2), channel_id=1, replica_groups=mesh['pipe'=4,'req'=2,'tp'=4] {'req'}, dimensions={0} | all-to-all | bytes 1048576 | tf_op jit(solution)/shard_map/all_to_all | solution.py:155
  227.1 17.7 %psum.29 = bf16[256,64]{0,1:T(8,128)(2,1)S(1)} all-reduce(f32[256,64]{0,1:T(8,128)S(1)} %fusion.54), channel_id=1, replica_groups=mesh['pipe'=4,'req'=2,'tp'=4] {'tp'}, use_global_device_ids=true, to_apply=%region_16.17 | all-reduce | flops 16384 | bytes 98304 | tf_op jit(solution)/shard_map/psum | solution.py:168
  246.3 2.3 reshape.1466
  248.6 14.1 %all_to_all.54 = bf16[2,32,4,2048]{3,2,1,0:T(4,128)(2,1)} all-to-all(bf16[2,32,4,2048]{3,2,1,0:T(4,128)(2,1)} %reshape.1466), channel_id=1, replica_groups=mesh['pipe'=4,'req'=2,'tp'=4] {'req'}, dimensions={0} | all-to-all | bytes 2097152 | tf_op jit(solution)/shard_map/all_to_all | solution.py:178
  262.6 3.0 gather_fusion.3
  265.7 2.2 reshape.1477
  273.9 51.1 %all-gather.13.cloned.1.call-done = bf16[128,8192]{1,0:T(8,128)(2,1)} async-done(((bf16[128,2048]{1,0:T(8,128)(2,1)}), bf16[128,8192]{1,0:T(8,128)(2,1)}) %all-gather.13.cloned.1.call-update) | async-done | bytes 2097168 | tf_op jit(solution)/shard_map/all_gather | solution.py:103
  327.2 4.2 fusion.60
  331.9 2.3 fusion.163
  334.9 2.9 fusion.36
  338.0 2.1 fusion.46
  343.1 11.3 %all_to_all.55 = bf16[2,32,4,1024]{3,2,1,0:T(4,128)(2,1)} all-to-all(bf16[2,32,4,1024]{3,2,1,0:T(4,128)(2,1)S(1)} %scatter_fusion.3), channel_id=1, replica_groups=mesh['pipe'=4,'req'=2,'tp'=4] {'req'}, dimensions={0} | all-to-all | bytes 1048576 | tf_op jit(solution)/shard_map/all_to_all | solution.py:155
  357.0 17.7 %psum.30 = bf16[256,64]{0,1:T(8,128)(2,1)S(1)} all-reduce(f32[256,64]{0,1:T(8,128)S(1)} %fusion.55), channel_id=1, replica_groups=mesh['pipe'=4,'req'=2,'tp'=4] {'tp'}, use_global_device_ids=true, to_apply=%region_23.24 | all-reduce | flops 16384 | bytes 98304 | tf_op jit(solution)/shard_map/psum | solution.py:168
  376.2 2.3 reshape.1470
  378.5 14.2 %all_to_all.56 = bf16[2,32,4,2048]{3,2,1,0:T(4,128)(2,1)} all-to-all(bf16[2,32,4,2048]{3,2,1,0:T(4,128)(2,1)} %reshape.1470), channel_id=1, replica_groups=mesh['pipe'=4,'req'=2,'tp'=4] {'req'}, dimensions={0} | all-to-all | bytes 2097152 | tf_op jit(solution)/shard_map/all_to_all | solution.py:178
  392.7 3.0 gather_fusion.4
  395.7 2.2 reshape.1478
  407.4 4.5 all-reduce.2
  415.6 39.5 %all-gather.15.cloned.1.call-done = bf16[128,8192]{1,0:T(8,128)(2,1)} async-done(((bf16[128,2048]{1,0:T(8,128)(2,1)}), bf16[128,8192]{1,0:T(8,128)(2,1)}) %all-gather.15.cloned.1.call-update) | async-done | bytes 2097168 | tf_op jit(solution)/shard_map/all_gather | solution.py:103
  457.2 4.2 fusion.63
  464.0 2.9 fusion.35
  469.5 4.6 scatter_fusion.4
  474.1 3.5 all-to-all-start.7
  477.9 15.4 %scatter_fusion.5 = bf16[128,2,64,128]{3,1,2,0:T(2,128)(2,1)} fusion(bf16[128,2,64,128]{3,1,2,0:T(2,128)(2,1)} %bitcast.355, s32[128]{0:T(128)S(1)} %fusion.154, bf16[128,2,128]{2,1,0:T(2,128)(2,1)S(1)} %copy.93), kind=kCustom, calls=%fused_computation.13 | custom fusion | bytes 197632 | tf_op jit(solution)/shard_map/scatter | solution.py:189
  493.3 3.8 gather_fusion.6
  498.6 17.6 %psum.31 = bf16[256,64]{0,1:T(8,128)(2,1)S(1)} all-reduce(f32[256,64]{0,1:T(8,128)S(1)} %fusion.56), channel_id=1, replica_groups=mesh['pipe'=4,'req'=2,'tp'=4] {'tp'}, use_global_device_ids=true, to_apply=%region_30.31 | all-reduce | flops 16384 | bytes 98304 | tf_op jit(solution)/shard_map/psum | solution.py:168
  517.9 3.6 all-to-all-start.8
  522.4 9.4 %all-to-all-done.8 = bf16[2,32,4,2048]{3,2,1,0:T(4,128)(2,1)S(1)} async-done(((bf16[2,32,4,2048]{3,2,1,0:T(4,128)(2,1)}), bf16[2,32,4,2048]{3,2,1,0:T(4,128)(2,1)S(1)}, u32[]{:S(2)}, u32[]{:S(2)}) %all-to-all-start.8) | async-done | bytes 1048608 | tf_op jit(solution)/shard_map/all_to_all | solution.py:178
  535.9 3.6 scatter_fusion.6
  (282 shorter events, 84.3 us)
Async XLA Ops:
  7.2 111.1 %copy-start = (bf16[1,4,64,2048]{3,2,1,0:T(8,128)(2,1)S(1)}, bf16[1,4,64,2048]{3,2,1,0:T(8,128)(2,1)}, u32[]{:S(2)}) copy-start(bf16[1,4,64,2048]{3,2,1,0:T(8,128)(2,1)} %param.17) | copy-start | bytes 3145732
  7.2 59.4 %all-gather.9.cloned.1.call-start = ((), (), s32[]{:S(2)}) async-start(), calls=%async_computation.9 | async-start | bytes 2621440 | tf_op jit(solution)/shard_map/all_gather | solution.py:103
  17.3 68.3 %all-to-all-start.1 = ((s32[2,1,32]{2,1,0:T(1,128)}), s32[2,1,32]{2,1,0:T(1,128)S(1)}, u32[]{:S(2)}, u32[]{:S(2)}) async-start(s32[2,1,32]{2,1,0:T(1,128)} %bitcast.38), calls=%async_computation.1 | async-start | bytes 2048 | tf_op jit(solution)/shard_map/all_to_all | solution.py:156
  26.2 6.5 %copy-start.32 = (bf16[1,8192]{1,0:T(2,128)(2,1)S(1)}, bf16[1,8192]{1,0:T(2,128)(2,1)}, u32[]{:S(2)}) copy-start(bf16[1,8192]{1,0:T(2,128)(2,1)} %param.14) | copy-start | bytes 49156
  26.2 6.5 %copy-start.44 = (s32[32]{0:T(128)S(1)}, s32[32]{0:T(128)}, u32[]{:S(2)}) copy-start(s32[32]{0:T(128)} %param.22) | copy-start | bytes 388
  26.2 6.7 %copy-start.16 = (bf16[1,128,1024]{2,1,0:T(8,128)(2,1)S(1)}, bf16[1,128,1024]{2,1,0:T(8,128)(2,1)}, u32[]{:S(2)}) copy-start(bf16[1,128,1024]{2,1,0:T(8,128)(2,1)} %param.13) | copy-start | bytes 786436
  32.7 165.7 %copy-start.33 = (f32[1,8192]{1,0:T(1,128)}, f32[1,8192]{1,0:T(1,128)S(1)}, u32[]{:S(2)}) copy-start(f32[1,8192]{1,0:T(1,128)S(1)} %mul.401) | copy-start | bytes 98308
  32.9 40.0 %copy-start.36 = (f32[128]{0:T(128)}, f32[128]{0:T(128)S(1)}, u32[]{:S(2)}) copy-start(f32[128]{0:T(128)S(1)} %convert_element_type.449) | copy-start | bytes 1540
  33.0 40.4 %copy-start.17 = (bf16[16,8,8,128]{3,2,1,0:T(8,128)(2,1)}, bf16[16,8,8,128]{3,2,1,0:T(8,128)(2,1)S(1)}, u32[]{:S(2)}) copy-start(bf16[16,8,8,128]{3,2,1,0:T(8,128)(2,1)S(1)} %copy.106) | copy-start | bytes 786436
  33.0 12.7 %copy-start.1 = (s32[32,4]{0,1:T(4,128)S(1)}, s32[32,4]{0,1:T(4,128)}, u32[]{:S(2)}) copy-start(s32[32,4]{0,1:T(4,128)} %param.21) | copy-start | bytes 1540
  63.7 9.2 %copy-start.40 = (f32[64]{0:T(128)}, f32[64]{0:T(128)S(1)}, u32[]{:S(2)}) copy-start(f32[64]{0:T(128)S(1)} %multiply_exponential_fusion) | copy-start | bytes 772
  63.8 9.6 %copy-start.51 = (pred[4,4]{1,0:T(4,128)(4,1)}, pred[4,4]{1,0:T(4,128)(4,1)S(1)}, u32[]{:S(2)}) copy-start(pred[4,4]{1,0:T(4,128)(4,1)S(1)} %iota_compare_fusion.3) | copy-start | bytes 52
  72.9 5.5 %copy-start.20 = (f32[128,2,128]{0,2,1:T(8,128)}, f32[128,2,128]{0,2,1:T(8,128)S(1)}, u32[]{:S(2)}) copy-start(f32[128,2,128]{0,2,1:T(8,128)S(1)} %fusion.22) | copy-start | bytes 393220
  85.6 11.0 %all-to-all-start = ((bf16[2,32,4,1024]{3,2,1,0:T(4,128)(2,1)}), bf16[2,32,4,1024]{3,2,1,0:T(4,128)(2,1)S(1)}, u32[]{:S(2)}, u32[]{:S(2)}) async-start(bf16[2,32,4,1024]{3,2,1,0:T(4,128)(2,1)} %scatter_fusion), calls=%async_computation | async-start | bytes 1048576 | tf_op jit(solution)/shard_map/all_to_all | solution.py:155
  89.1 107.2 %all-gather.11.cloned.1.call-start = ((), (), s32[]{:S(2)}) async-start(), calls=%async_computation.10 | async-start | bytes 2621440 | tf_op jit(solution)/shard_map/all_gather | solution.py:103
  118.3 20.9 %copy-start.2 = (bf16[128,2048]{1,0:T(8,128)(2,1)S(1)}, bf16[128,2048]{1,0:T(8,128)(2,1)}, u32[]{:S(2)}) copy-start(bf16[128,2048]{1,0:T(8,128)(2,1)} %param.12) | copy-start | bytes 1572868
  141.5 2.8 collective-permute-start
  145.1 179.9 %all-gather.13.cloned.1.call-start = ((), (), s32[]{:S(2)}) async-start(), calls=%async_computation.11 | async-start | bytes 2621440 | tf_op jit(solution)/shard_map/all_gather | solution.py:103
  198.4 5.3 copy-start.18
  202.6 7.0 %copy-start.22 = (f32[128,2,1,128]{0,3,2,1:T(8,128)}, f32[128,2,1,128]{0,3,2,1:T(8,128)S(1)}, u32[]{:S(2)}) copy-start(f32[128,2,1,128]{0,3,2,1:T(8,128)S(1)} %fusion.57) | copy-start | bytes 393220
  244.8 23.0 %copy-start.5 = (bf16[128,2048]{1,0:T(8,128)(2,1)S(1)}, bf16[128,2048]{1,0:T(8,128)(2,1)}, u32[]{:S(2)}) copy-start(bf16[128,2048]{1,0:T(8,128)(2,1)} %broadcast_select_fusion.2) | copy-start | bytes 1572868
  265.7 61.5 %copy-start.34 = (f32[1,8192]{1,0:T(1,128)S(1)}, f32[1,8192]{1,0:T(1,128)}, u32[]{:S(2)}) copy-start(f32[1,8192]{1,0:T(1,128)} %copy-done.33) | copy-start | bytes 98308
  270.0 2.8 collective-permute-start.1
  273.7 181.4 %all-gather.15.cloned.1.call-start = ((), (), s32[]{:S(2)}) async-start(), calls=%async_computation.12 | async-start | bytes 2621440 | tf_op jit(solution)/shard_map/all_gather | solution.py:103
  331.3 6.5 %copy-start.24 = (f32[128,2,1,128]{0,3,2,1:T(8,128)}, f32[128,2,1,128]{0,3,2,1:T(8,128)S(1)}, u32[]{:S(2)}) copy-start(f32[128,2,1,128]{0,3,2,1:T(8,128)S(1)} %fusion.60) | copy-start | bytes 393220
  331.6 6.3 %copy-start.12 = (bf16[128,1,64]{0,2,1:T(8,128)(2,1)}, bf16[128,1,64]{0,2,1:T(8,128)(2,1)S(1)}, u32[]{:S(2)}) copy-start(bf16[128,1,64]{0,2,1:T(8,128)(2,1)S(1)} %get-tuple-element.19) | copy-start | bytes 49156
  331.6 6.3 %copy-start.14 = (bf16[128,1,64]{0,2,1:T(8,128)(2,1)}, bf16[128,1,64]{0,2,1:T(8,128)(2,1)S(1)}, u32[]{:S(2)}) copy-start(bf16[128,1,64]{0,2,1:T(8,128)(2,1)S(1)} %get-tuple-element.20) | copy-start | bytes 49156
  374.8 23.1 %copy-start.6 = (bf16[128,2048]{1,0:T(8,128)(2,1)S(1)}, bf16[128,2048]{1,0:T(8,128)(2,1)}, u32[]{:S(2)}) copy-start(bf16[128,2048]{1,0:T(8,128)(2,1)} %broadcast_select_fusion.1) | copy-start | bytes 1572868
  378.5 25.2 %copy-start.45 = (s32[32]{0:T(128)S(1)}, s32[32]{0:T(128)}, u32[]{:S(2)}) copy-start(s32[32]{0:T(128)} %param.22) | copy-start | bytes 388
  400.0 2.8 collective-permute-start.2
  404.0 9.2 %copy-start.21 = (f32[128,2,128]{0,2,1:T(8,128)S(1)}, f32[128,2,128]{0,2,1:T(8,128)}, u32[]{:S(2)}) copy-start(f32[128,2,128]{0,2,1:T(8,128)} %copy-done.20) | copy-start | bytes 393220
  404.0 10.4 %copy-start.23 = (f32[128,2,1,128]{0,3,2,1:T(8,128)S(1)}, f32[128,2,1,128]{0,3,2,1:T(8,128)}, u32[]{:S(2)}) copy-start(f32[128,2,1,128]{0,3,2,1:T(8,128)} %copy-done.22) | copy-start | bytes 393220
  404.0 11.0 %copy-start.25 = (f32[128,2,1,128]{0,3,2,1:T(8,128)S(1)}, f32[128,2,1,128]{0,3,2,1:T(8,128)}, u32[]{:S(2)}) copy-start(f32[128,2,1,128]{0,3,2,1:T(8,128)} %copy-done.24) | copy-start | bytes 393220
  404.0 53.2 %copy-start.35 = (f32[1,8192]{1,0:T(1,128)S(1)}, f32[1,8192]{1,0:T(1,128)}, u32[]{:S(2)}) copy-start(f32[1,8192]{1,0:T(1,128)} %copy-done.33) | copy-start | bytes 98308
  467.0 10.7 %copy-start.13 = (bf16[128,1,64]{0,2,1:T(8,128)(2,1)S(1)}, bf16[128,1,64]{0,2,1:T(8,128)(2,1)}, u32[]{:S(2)}) copy-start(bf16[128,1,64]{0,2,1:T(8,128)(2,1)} %copy-done.12) | copy-start | bytes 49156
  467.0 10.8 %copy-start.15 = (bf16[128,1,64]{0,2,1:T(8,128)(2,1)S(1)}, bf16[128,1,64]{0,2,1:T(8,128)(2,1)}, u32[]{:S(2)}) copy-start(bf16[128,1,64]{0,2,1:T(8,128)(2,1)} %copy-done.14) | copy-start | bytes 49156
  468.6 29.6 %copy-start.48 = (bf16[1,4,64,1024]{3,2,1,0:T(8,128)(2,1)S(1)}, bf16[1,4,64,1024]{3,2,1,0:T(8,128)(2,1)}, u32[]{:S(2)}) copy-start(bf16[1,4,64,1024]{3,2,1,0:T(8,128)(2,1)} %param.16) | copy-start | bytes 1572868
  474.1 23.9 %all-to-all-start.7 = ((bf16[2,32,4,1024]{3,2,1,0:T(4,128)(2,1)}), bf16[2,32,4,1024]{3,2,1,0:T(4,128)(2,1)S(1)}, u32[]{:S(2)}, u32[]{:S(2)}) async-start(bf16[2,32,4,1024]{3,2,1,0:T(4,128)(2,1)} %scatter_fusion.4), calls=%async_computation.7 | async-start | bytes 1048576 | tf_op jit(solution)/shard_map/all_to_all | solution.py:155
  477.6 58.1 %all-gather.17.cloned.1.call-start = ((), (), s32[]{:S(2)}) async-start(), calls=%async_computation.13 | async-start | bytes 1572864 | tf_op jit(solution)/shard_map/all_gather | solution.py:193
  498.2 23.4 %copy-start.26 = (bf16[1,128,1,128]{1,3,2,0:T(8,128)(2,1)S(1)}, bf16[1,128,1,128]{1,3,2,0:T(8,128)(2,1)}, u32[]{:S(2)}) copy-start(bf16[1,128,1,128]{1,3,2,0:T(8,128)(2,1)} %maximum_bitcast_fusion.11) | copy-start | bytes 98308
  498.2 23.4 %copy-start.27 = (bf16[1,128,1,128]{1,3,2,0:T(8,128)(2,1)S(1)}, bf16[1,128,1,128]{1,3,2,0:T(8,128)(2,1)}, u32[]{:S(2)}) copy-start(bf16[1,128,1,128]{1,3,2,0:T(8,128)(2,1)} %slice_bitcast_fusion.20) | copy-start | bytes 98308
  498.2 23.4 %copy-start.28 = (bf16[1,128,1,128]{1,3,2,0:T(8,128)(2,1)S(1)}, bf16[1,128,1,128]{1,3,2,0:T(8,128)(2,1)}, u32[]{:S(2)}) copy-start(bf16[1,128,1,128]{1,3,2,0:T(8,128)(2,1)} %maximum_bitcast_fusion.10) | copy-start | bytes 98308
  498.2 23.4 %copy-start.29 = (bf16[1,128,1,128]{1,3,2,0:T(8,128)(2,1)S(1)}, bf16[1,128,1,128]{1,3,2,0:T(8,128)(2,1)}, u32[]{:S(2)}) copy-start(bf16[1,128,1,128]{1,3,2,0:T(8,128)(2,1)} %slice_bitcast_fusion.22) | copy-start | bytes 98308
  498.2 23.4 %copy-start.30 = (bf16[1,128,1,128]{1,3,2,0:T(8,128)(2,1)S(1)}, bf16[1,128,1,128]{1,3,2,0:T(8,128)(2,1)}, u32[]{:S(2)}) copy-start(bf16[1,128,1,128]{1,3,2,0:T(8,128)(2,1)} %slice_bitcast_fusion.24) | copy-start | bytes 98308
  516.7 18.0 %copy-start.3 = (bf16[128,2048]{1,0:T(8,128)(2,1)S(1)}, bf16[128,2048]{1,0:T(8,128)(2,1)}, u32[]{:S(2)}) copy-start(bf16[128,2048]{1,0:T(8,128)(2,1)} %broadcast_select_fusion) | copy-start | bytes 1572868
  516.7 18.0 %copy-start.9 = (bf16[128,2048]{1,0:T(8,128)(2,1)S(1)}, bf16[128,2048]{1,0:T(8,128)(2,1)}, u32[]{:S(2)}) copy-start(bf16[128,2048]{1,0:T(8,128)(2,1)} %copy-done.8) | copy-start | bytes 1572868
  517.9 13.8 %all-to-all-start.8 = ((bf16[2,32,4,2048]{3,2,1,0:T(4,128)(2,1)}), bf16[2,32,4,2048]{3,2,1,0:T(4,128)(2,1)S(1)}, u32[]{:S(2)}, u32[]{:S(2)}) async-start(bf16[2,32,4,2048]{3,2,1,0:T(4,128)(2,1)} %reshape.1474), calls=%async_computation.8 | async-start | bytes 2097152 | tf_op jit(solution)/shard_map/all_to_all | solution.py:178
  521.5 14.4 %copy-start.47 = (s32[32]{0:T(128)S(1)}, s32[32]{0:T(128)}, u32[]{:S(2)}) copy-start(s32[32]{0:T(128)} %compare_select_fusion.6) | copy-start | bytes 388
  (18 other events, 55.1 us)
Sparse Core Ops, SparseCore 0:
  10.2 48.6 all-gather.8
  145.3 50.9 all-gather.10
  273.8 51.2 all-gather.12
  403.8 51.2 all-gather.14
  498.1 20.5 all-gather.16
where the time goes:
time: 558 us; the launch traced here: 547 us
  waiting for transfers between devices  163 us (29%)
  blocking collectives  142 us (25%)
  local copies, waits for them, and re-layouts  130 us (23%)
  matrix products  52 us (9%)
  other arithmetic  24.9 us (4%)
  starting transfers between devices  19.3 us (3%)
  between operations  16.5 us (3%)
    all_gather x4, waiting for transfers between devices, body(): whole_rows = lax.all_gather(hstate, 'tp', axis=1, tiled=True)  142 us
    psum x4, blocking collectives, body(): rank_low = lax.psum(partial_low, 'tp').astype(jnp.bfloat16)  73.1 us
    all_to_all x3, blocking collectives, body(): lax.all_to_all(deltas, 'req', split_axis=0, concat_axis=0, tiled=True)  42.1 us
    unnamed x115, local copies, waits for them, and re-layouts  24.2 us
    all_to_all x2, blocking collectives, body(): lax.all_to_all(outgoing, 'req', split_axis=0, concat_axis=0, tiled=True)  22.7 us
    gather x2, local copies, waits for them, and re-layouts, body(): gathered = layer_pages[page_table]  17.8 us
    dot_general x4, matrix products, body(): jnp.dot(normed, weight_flat, preferred_element_type=jnp.float32)  16.7 us
    scatter x1, local copies, waits for them, and re-layouts, body(): written = layer_pages.at[page_slot, :, positions % PAGE, :].set(fresh_rows)  15.4 us
  transfers between devices with their start and end apart: 12, of which 8 were waited for; matrix products, arithmetic and copies ran while one was open for 19% of the time, Pallas kernels for 0%

commit v1 on v0

v1 whole, which is shorter than its diff:
```python
import functools
import math

import jax
import jax.numpy as jnp
from jax import lax
from jax.experimental import pallas as pl
from jax.experimental.pallas import tpu as pltpu
from jax.sharding import PartitionSpec as P

HD = 128
R = 64
S = 4
PAGE = 64
MAXP = 4
EPS = 1e-05
BIG = -1e30
SCALE = HD ** (-0.5)
VM = pl.BlockSpec(memory_space=pltpu.VMEM)
SM = pl.BlockSpec(memory_space=pltpu.SMEM)
ANY = pl.BlockSpec(memory_space=pl.ANY)
NT = (((1,), (1,)), ((), ()))


def params(mib):
    return pltpu.CompilerParams(vmem_limit_bytes=mib << 20)


def sds(shape, dtype):
    return jax.ShapeDtypeStruct(shape, dtype)


def halves_of(rows):
    return rows // 2


def split_parts_kernel(raw_ref, out_ref, wide):
    wide[...] = raw_ref[...].astype(jnp.float32)
    rows = out_ref.shape[0]
    out_ref[:, :HD] = wide[pl.ds(0, rows, stride=2), :].astype(jnp.bfloat16)
    out_ref[:, HD:] = wide[pl.ds(1, rows, stride=2), :].astype(jnp.bfloat16)


def split_parts(raw):
    rows = raw.shape[0] // 2
    step = 1024
    return pl.pallas_call(
        split_parts_kernel,
        grid=(rows // step,),
        in_specs=[pl.BlockSpec((2 * step, HD), lambda i: (i, 0))],
        out_specs=pl.BlockSpec((step, 2 * HD), lambda i: (i, 0)),
        out_shape=sds((rows, 2 * HD), jnp.bfloat16),
        scratch_shapes=[pltpu.VMEM((2 * step, HD), jnp.float32)],
        compiler_params=params(16),
        name="split_parts",
    )(raw)


def cached_kernel(table_ref, len_ref, q_ref, pages_ref, acc_ref, lse_ref, buf, wide_q, sems):
    heads = acc_ref.shape[0]
    reqs = len_ref.shape[0]
    per = 8 // S
    ctx = MAXP * PAGE
    pages = per * MAXP

    def start(i, _):
        pltpu.make_async_copy(
            pages_ref.at[table_ref[i]], buf.at[i], sems.at[i // pages]
        ).start()
        return 0

    lax.fori_loop(0, reqs * MAXP, start, 0)
    wide_q[...] = q_ref[...].astype(jnp.float32)
    shape = (heads * 8, per * ctx)
    rows = lax.broadcasted_iota(jnp.int32, shape, 0)
    cols = lax.broadcasted_iota(jnp.int32, shape, 1)
    own = (rows % 8) // S == cols // ctx
    at = jnp.where(own, cols % ctx, 2 * ctx)
    second = cols >= ctx
    lanes = lax.broadcasted_iota(jnp.int32, (8, HD), 1)

    def group(g, _):
        first = pl.multiple_of(g * pages, pages)
        block = buf.at[pl.ds(first, pages)]
        pltpu.make_async_copy(block, block, sems.at[g]).wait()
        row = pl.multiple_of(g * 8, 8)
        q = jnp.concatenate(
            [wide_q[pl.ds(row, 8), h * HD : (h + 1) * HD] for h in range(heads)], axis=0
        ).astype(jnp.bfloat16)
        keys = buf[pl.ds(first, pages), 0].reshape(per * ctx, HD)
        values = buf[pl.ds(first, pages), 1].reshape(per * ctx, HD)
        scores = lax.dot_general(q, keys, NT, preferred_element_type=jnp.float32) * SCALE
        limit = jnp.where(second, len_ref[g * per + 1], len_ref[g * per])
        scores = jnp.where(at < limit, scores, BIG)
        top = jnp.max(scores, axis=1, keepdims=True)
        weights = jnp.exp(scores - top)
        total = jnp.sum(weights, axis=1, keepdims=True)
        mixed = jnp.dot(weights.astype(jnp.bfloat16), values, preferred_element_type=jnp.float32)
        mixed = mixed / total
        lse = top + jnp.log(total)
        packed = jnp.zeros((8, HD), jnp.float32)
        for h in range(heads):
            acc_ref[h, pl.ds(row, 8), :] = mixed[h * 8 : (h + 1) * 8]
            packed = jnp.where(lanes == h, lse[h * 8 : (h + 1) * 8], packed)
        lse_ref[pl.ds(row, 8), :] = packed
        return 0

    lax.fori_loop(0, reqs // per, group, 0)


def cached_attention(table, lengths, queries, pages):
    tokens, width = queries.shape
    heads = width // HD
    return pl.pallas_call(
        cached_kernel,
        in_specs=[SM, SM, VM, ANY],
        out_specs=(VM, VM),
        out_shape=(sds((heads, tokens, HD), jnp.float32), sds((tokens, HD), jnp.float32)),
        scratch_shapes=[
            pltpu.VMEM(pages.shape, pages.dtype),
            pltpu.VMEM(queries.shape, jnp.float32),
            pltpu.SemaphoreType.DMA((lengths.shape[0] * S // 8,)),
        ],
        compiler_params=params(24),
        name="cached_attention",
    )(table, lengths, queries, pages)


def attend_new(proj_k, proj_v, refs, new_k, new_v, low_ref, mixed_all):
    q_ref, cos_ref, sin_ref, acc_ref, lse_ref, slot_ref, a_refs = refs
    tokens = proj_k.shape[0]
    heads = q_ref.shape[1] // HD
    keys = (proj_k * cos_ref[...] + pltpu.roll(proj_k, HD // 2, 1) * sin_ref[...]).astype(
        jnp.bfloat16
    )
    values = proj_v.astype(jnp.bfloat16)
    new_k[...] = keys
    new_v[...] = values
    rows = lax.broadcasted_iota(jnp.int32, (tokens, tokens), 0)
    cols = lax.broadcasted_iota(jnp.int32, (tokens, tokens), 1)
    allowed = (rows // S == cols // S) & (cols <= rows)
    for h in range(heads):
        span = slice(h * HD, (h + 1) * HD)
        scores = lax.dot_general(q_ref[:, span], keys, NT, preferred_element_type=jnp.float32)
        scores = jnp.where(allowed, scores * SCALE, BIG)
        lse = lse_ref[:, h : h + 1]
        top = jnp.maximum(jnp.max(scores, axis=1, keepdims=True), lse)
        weights = jnp.exp(scores - top)
        old = jnp.exp(lse - top)
        total = jnp.sum(weights, axis=1, keepdims=True) + old
        mixed = jnp.dot(weights.astype(jnp.bfloat16), values, preferred_element_type=jnp.float32)
        mixed_all[:, span] = ((mixed + old * acc_ref[h]) / total).astype(jnp.bfloat16)
    slots = slot_ref[...]
    half = lax.broadcasted_iota(jnp.int32, (tokens, HD), 1) // R
    folded = jnp.zeros((tokens, HD), jnp.float32)
    base = 0
    for a_ref in a_refs:
        low = lax.dot_general(
            mixed_all[...], a_ref[...], NT, preferred_element_type=jnp.float32
        )
        for j in range(a_ref.shape[0] // HD):
            folded = folded + jnp.where(
                slots == base + 2 * j + half, low[:, j * HD : (j + 1) * HD], 0.0
            )
        base += a_ref.shape[0] // R
    folded = folded + pltpu.roll(folded, R, 1)
    low_ref[...] = jnp.where(
        half[: tokens // 2] == 0, folded[: tokens // 2], folded[tokens // 2 :]
    ).astype(jnp.bfloat16)


def first_kernel(n_tp, n_a, sec_ref, *refs):
    h_refs, (w_ref, gain_ref) = refs[:n_tp], refs[n_tp : n_tp + 2]
    shared = refs[n_tp + 2 : n_tp + 8]
    a_refs = refs[n_tp + 8 : n_tp + 8 + n_a]
    new_k, new_v, low_ref, mixed_all = refs[n_tp + 8 + n_a :]
    width = h_refs[0].shape[1]

    @pl.when(sec_ref[0] == 0)
    def _():
        tokens = h_refs[0].shape[0]
        proj = jnp.zeros((tokens, 2 * HD), jnp.float32)
        square = jnp.zeros((tokens, 1), jnp.float32)
        for s in range(n_tp):
            place = lax.rem(sec_ref[1] + n_tp - s, n_tp)
            row = pl.multiple_of(place * width, width)
            h = h_refs[s][...].astype(jnp.float32)
            square = square + jnp.sum(h * h, axis=1, keepdims=True)
            x = (h * gain_ref[pl.ds(place, 1), :]).astype(jnp.bfloat16)
            proj = proj + jnp.dot(
                x, w_ref[pl.ds(row, width), :], preferred_element_type=jnp.float32
            )
        proj = proj * lax.rsqrt(square / (n_tp * width) + EPS)
        attend_new(
            proj[:, :HD], proj[:, HD:], (*shared, a_refs), new_k, new_v, low_ref, mixed_all
        )

    @pl.when(sec_ref[0] != 0)
    def _():
        new_k[...] = jnp.zeros_like(new_k)
        new_v[...] = jnp.zeros_like(new_v)


def later_kernel(section, n_tp, n_a, total_width, sec_ref, *refs):
    m_refs = refs[:n_tp]
    shared = refs[n_tp : n_tp + 6]
    a_refs = refs[n_tp + 6 : n_tp + 6 + n_a]
    prev_k, prev_v, new_k, new_v, low_ref, mixed_all = refs[n_tp + 6 + n_a :]

    @pl.when(sec_ref[0] == section)
    def _():
        tokens = prev_k.shape[0]
        proj = jnp.zeros((tokens, 2 * HD), jnp.float32)
        square = jnp.zeros((1, HD), jnp.float32)
        for m_ref in m_refs:
            proj = proj + m_ref[:tokens, :].astype(jnp.float32)
            tail = m_ref[tokens : tokens + 16, :HD].astype(jnp.float32)
            square = square + jnp.sum(tail, axis=0, keepdims=True) * 0.125
        inv = lax.rsqrt(square / total_width + EPS)
        inv = jnp.transpose(jnp.broadcast_to(inv, (tokens, HD)))
        attend_new(
            proj[:, :HD] * inv,
            proj[:, HD:] * inv,
            (*shared, a_refs),
            new_k,
            new_v,
            low_ref,
            mixed_all,
        )

    @pl.when(sec_ref[0] != section)
    def _():
        new_k[...] = prev_k[...]
        new_v[...] = prev_v[...]


def attend_call(kernel, operands, tokens, q_width, name):
    return pl.pallas_call(
        kernel,
        in_specs=[SM] + [VM] * (len(operands) - 1),
        out_specs=(VM, VM, VM),
        out_shape=(
            sds((tokens, HD), jnp.bfloat16),
            sds((tokens, HD), jnp.bfloat16),
            sds((tokens // 2, HD), jnp.bfloat16),
        ),
        scratch_shapes=[pltpu.VMEM((tokens, q_width), jnp.bfloat16)],
        compiler_params=params(32),
        name=name,
    )(*operands)


def unfold_low(packed, slots, base, rows):
    count = packed.shape[0]
    half = lax.broadcasted_iota(jnp.int32, (count, HD), 1) // R
    turned = pltpu.roll(packed, R, 1)
    low = jnp.concatenate(
        [jnp.where(half == 0, packed, turned), jnp.where(half == 1, packed, turned)], axis=0
    )
    half = lax.broadcasted_iota(jnp.int32, (2 * count, HD), 1) // R
    return jnp.concatenate(
        [
            jnp.where(slots == base + 2 * j + half, low, 0.0).astype(jnp.bfloat16)
            for j in range(rows // HD)
        ],
        axis=1,
    )


def add_delta(low, slots, b_refs, h_ref, span):
    delta = None
    base = 0
    for b_ref, spread in zip(b_refs, low):
        part = jnp.dot(spread, b_ref[:, span], preferred_element_type=jnp.float32)
        delta = part if delta is None else delta + part
    delta = delta.astype(jnp.bfloat16).astype(jnp.float32)
    return (h_ref[:, span].astype(jnp.float32) + delta).astype(jnp.bfloat16)


def spreads(packed, slots, b_refs):
    out = []
    base = 0
    for b_ref in b_refs:
        out.append(unfold_low(packed, slots, base, b_ref.shape[0]))
        base += b_ref.shape[0] // R
    return out


def slice_kernel(section, n_tp, n_b, sec_ref, *refs):
    low_refs = refs[:n_tp]
    slot_ref, h_ref, gain_ref, w_ref = refs[n_tp : n_tp + 4]
    b_refs = refs[n_tp + 4 : n_tp + 4 + n_b]
    rest = refs[n_tp + 4 + n_b :]
    mine, other = rest[: n_tp - 1], rest[n_tp - 1 : 2 * n_tp - 2]
    h_out, low_out = rest[2 * n_tp - 2 : 2 * n_tp]
    m_refs = rest[2 * n_tp : 3 * n_tp]
    x_all = rest[3 * n_tp]
    tokens, width = h_ref.shape
    part = width // 4
    split = width // 2

    @pl.when(sec_ref[0] == section)
    def _():
        packed = low_refs[0][...].astype(jnp.float32)
        for low_ref in low_refs[1:]:
            packed = packed + low_ref[...].astype(jnp.float32)
        rounded = packed.astype(jnp.bfloat16)
        low_out[...] = rounded
        slots = slot_ref[...]
        low = spreads(rounded.astype(jnp.float32), slots, b_refs)
        square = jnp.zeros((tokens, 1), jnp.float32)
        for c in range(4):
            span = slice(c * part, (c + 1) * part)
            h = add_delta(low, slots, b_refs, h_ref, span)
            h_out[:, span] = h
            h = h.astype(jnp.float32)
            square = square + jnp.sum(h * h, axis=1, keepdims=True)
            x_all[:, span] = (h * gain_ref[:, span]).astype(jnp.bfloat16)
        square = jnp.transpose(jnp.broadcast_to(square, (tokens, HD)))[:16]
        high = square.astype(jnp.bfloat16).astype(jnp.float32)
        upper = lax.broadcasted_iota(jnp.int32, (16, HD), 0) < 8
        tail = jnp.where(upper, high, square - high).astype(jnp.bfloat16)
        row = pl.multiple_of(sec_ref[1] * width, width)
        here = pl.multiple_of(sec_ref[2] * split, split)
        there = pl.multiple_of((1 - sec_ref[2]) * split, split)
        for s in range(n_tp):
            if s == 0:
                proj = jnp.dot(
                    x_all[...], w_ref[pl.ds(row, width), :], preferred_element_type=jnp.float32
                )
            else:
                proj = jnp.dot(
                    x_all[:, pl.ds(here, split)],
                    mine[s - 1][...],
                    preferred_element_type=jnp.float32,
                ) + jnp.dot(
                    x_all[:, pl.ds(there, split)],
                    other[s - 1][...],
                    preferred_element_type=jnp.float32,
                )
            m_refs[s][:tokens, :] = proj.astype(jnp.bfloat16)
            m_refs[s][tokens:, :HD] = tail
            m_refs[s][tokens:, HD:] = jnp.zeros_like(tail)


def section_slice(section, n_tp, sec, lows, slots, h_prev, gain, weights, b_blocks, mine, other):
    tokens, width = h_prev.shape
    operands = [sec, *lows, slots, h_prev, gain, weights, *b_blocks, *mine, *other]
    return pl.pallas_call(
        functools.partial(slice_kernel, section, n_tp, len(b_blocks)),
        in_specs=[SM] + [VM] * (len(operands) - 1),
        out_specs=(VM,) * (2 + n_tp),
        out_shape=(
            sds((tokens, width), jnp.bfloat16),
            sds((tokens // 2, HD), jnp.bfloat16),
            *[sds((tokens + 16, 2 * HD), jnp.bfloat16)] * n_tp,
        ),
        scratch_shapes=[pltpu.VMEM((tokens, width), jnp.bfloat16)],
        compiler_params=params(48),
        name="section_slice_%d" % section,
    )(*operands)


def result_kernel(n_sec, n_tp, n_b, sec_ref, back_ref, *refs):
    low_refs = refs[:n_tp]
    slot_ref = refs[n_tp]
    h_refs = refs[n_tp + 1 : n_tp + 1 + n_sec]
    b_refs = refs[n_tp + 1 + n_sec : n_tp + 1 + n_sec + n_b]
    out_ref, h_buf, sem = refs[n_tp + 1 + n_sec + n_b :]
    for l in range(n_sec):

        @pl.when(sec_ref[0] == l)
        def _(l=l):
            copy = pltpu.make_async_copy(h_refs[l], h_buf, sem)
            copy.start()
            copy.wait()

    packed = low_refs[0][...].astype(jnp.float32)
    for low_ref in low_refs[1:]:
        packed = packed + low_ref[...].astype(jnp.float32)
    packed = jnp.where(sec_ref[0] == n_sec - 1, packed, back_ref[...].astype(jnp.float32))
    rounded = packed.astype(jnp.bfloat16).astype(jnp.float32)
    slots = slot_ref[...]
    low = spreads(rounded, slots, b_refs)
    part = h_buf.shape[1] // 4
    for c in range(4):
        span = slice(c * part, (c + 1) * part)
        out_ref[:, span] = add_delta(low, slots, b_refs, h_buf, span)


def section_result(n_sec, n_tp, sec, back, lows, slots, hs, b_blocks):
    tokens, width = hs[0].shape
    return pl.pallas_call(
        functools.partial(result_kernel, n_sec, n_tp, len(b_blocks)),
        in_specs=[SM] + [VM] * (2 + n_tp) + [ANY] * n_sec + [VM] * len(b_blocks),
        out_specs=VM,
        out_shape=sds((tokens, width), jnp.bfloat16),
        scratch_shapes=[
            pltpu.VMEM((tokens, width), jnp.bfloat16),
            pltpu.SemaphoreType.DMA,
        ],
        compiler_params=params(32),
        name="section_result",
    )(sec, back, *lows, slots, *hs, *b_blocks)


def leaving_kernel(src_ref, keep_ref, page_ref, at_ref, k_ref, v_ref, pages_ref, out_ref, sem):
    count = out_ref.shape[0]
    tokens = k_ref.shape[0]

    def start(i, _):
        pltpu.make_async_copy(pages_ref.at[src_ref[i]], out_ref.at[i], sem).start()
        return 0

    lax.fori_loop(0, count, start, 0)
    pltpu.make_async_copy(out_ref, out_ref, sem).wait()
    rows = lax.broadcasted_iota(jnp.int32, (PAGE, tokens), 0)
    spot = jnp.where(at_ref[...] == rows, page_ref[...], -1)

    def insert(i, _):
        hit = jnp.where(spot == src_ref[i], 1.0, 0.0)
        fresh = jnp.sum(hit, axis=1, keepdims=True) > 0.0
        hit = hit.astype(jnp.bfloat16)
        keep = keep_ref[i] > 0
        for part, new in enumerate((k_ref, v_ref)):
            value = jnp.dot(hit, new[...], preferred_element_type=jnp.float32)
            old = out_ref[i, part].astype(jnp.float32)
            value = jnp.where(keep, jnp.where(fresh, value, old), 0.0)
            out_ref[i, part] = value.astype(jnp.bfloat16)
        return 0

    lax.fori_loop(0, count, insert, 0)


def leaving_pages(src, keep, page_of, at, new_k, new_v, pages):
    count = src.shape[0]
    return pl.pallas_call(
        leaving_kernel,
        in_specs=[SM, SM, VM, VM, VM, VM, ANY],
        out_specs=VM,
        out_shape=sds((count, *pages.shape[1:]), jnp.bfloat16),
        scratch_shapes=[pltpu.SemaphoreType.DMA],
        compiler_params=params(16),
        name="leaving_pages",
    )(src, keep, page_of, at, new_k, new_v, pages)


def turn_tables(positions):
    half = HD // 2
    freq = jnp.exp(-math.log(500000.0) * (2.0 * jnp.arange(half, dtype=jnp.float32) / HD))
    angles = positions.astype(jnp.float32)[:, None] * freq
    cos, sin = jnp.cos(angles), jnp.sin(angles)
    return jnp.concatenate([cos, cos], axis=1), jnp.concatenate([-sin, sin], axis=1)


def body(
    hidden,
    queries,
    norm_gain,
    kv_weight,
    adapter_in,
    adapter_out,
    kv_pages,
    adapter_ids,
    owner_rows,
    page_table,
    lengths,
    moves,
):
    n_sec, n_req, n_tp = (lax.axis_size(a) for a in ("pipe", "req", "tp"))
    section, my_req, my_tp = (lax.axis_index(a) for a in ("pipe", "req", "tp"))
    tokens, width = hidden.shape
    depth = width * n_tp
    adapters = adapter_in.shape[1]
    q_width = queries.shape[2]
    half = width // 2

    def across(x, shift, sections):
        pairs = [
            (l * n_tp + t, l * n_tp + (t + shift) % n_tp) for l in sections for t in range(n_tp)
        ]
        return lax.ppermute(x, ("pipe", "tp"), pairs)

    def onward(x, shift, l):
        pairs = [((l - 1) * n_tp + t, l * n_tp + (t + shift) % n_tp) for t in range(n_tp)]
        return lax.ppermute(x, ("pipe", "tp"), pairs)

    def partner(x):
        return lax.ppermute(x, "req", [(i, i ^ 1) for i in range(n_req)])

    later = list(range(1, n_sec))
    sec = jnp.stack([section, my_tp, my_req % 2]).astype(jnp.int32)
    a_own = adapter_in[0].reshape(adapters * R, q_width)
    b_own = adapter_out[0].reshape(adapters * R, width)
    store = owner_rows[adapter_ids]
    if n_req == 2:
        slot = jnp.where(store // adapters == my_req, 0, adapters) + store % adapters
        gather_a = lambda x: [x, partner(x)]
    else:
        slot = store
        gather_a = lambda x: [lax.all_gather(x, "req", axis=0, tiled=True)]
    slots = jnp.repeat(slot, S)[:, None]
    positions = (lengths[:, None] + jnp.arange(S, dtype=jnp.int32)[None, :]).reshape(tokens)
    cos, sin = turn_tables(positions)
    page_of = jnp.take_along_axis(
        page_table, positions.reshape(-1, S) // PAGE, axis=1
    ).reshape(1, tokens)
    at = (positions % PAGE).reshape(1, tokens)
    gains = norm_gain[0].astype(jnp.float32).reshape(n_tp, width)
    gain = lax.dynamic_slice_in_dim(gains, my_tp, 1, axis=0)

    rows_in = [hidden] + [across(hidden, s, [0]) for s in range(1, n_tp)]
    a_blocks = gather_a(a_own)
    b_blocks = gather_a(b_own)
    weights = split_parts(kv_weight[0].reshape(2 * depth, HD))
    acc, lse = cached_attention(page_table.reshape(-1), lengths, queries[0], kv_pages[0])

    mine, other = [], []
    for s in range(1, n_tp):
        row = ((my_tp + s) % n_tp) * width + (my_req % 2) * half
        piece = lax.dynamic_slice_in_dim(weights, row, half, axis=0)
        mine.append(across(piece, s, later))
        other.append(partner(mine[-1]))
    before = [
        lax.ppermute(b, "pipe", [(l, l + 1) for l in range(n_sec - 1)]) for b in b_blocks
    ]

    shared = [queries[0], cos, sin, acc, lse, slots, *a_blocks]
    n_a = len(a_blocks)
    new_k, new_v, low = attend_call(
        functools.partial(first_kernel, n_tp, n_a),
        [sec, *rows_in, weights, gains, *shared],
        tokens,
        q_width,
        "first_section",
    )
    hs = [hidden]
    h_prev = hidden
    sums = []
    for l in later:
        lows = [onward(low, s, l) for s in range(n_tp)]
        h_new, low_sum, *parts = section_slice(
            l, n_tp, sec, lows, slots, h_prev, gain, weights, before, mine, other
        )
        hs.append(h_new)
        sums.append(low_sum)
        parts = [parts[0]] + [across(parts[s], -s, [l]) for s in range(1, n_tp)]
        if l + 1 < n_sec:
            h_prev = lax.ppermute(h_new, "pipe", [(l, l + 1)])
        new_k, new_v, low = attend_call(
            functools.partial(later_kernel, l, n_tp, n_a, depth),
            [sec, *parts, *shared, new_k, new_v],
            tokens,
            q_width,
            "section_%d" % l,
        )
    lows = [low] + [across(low, s, [n_sec - 1]) for s in range(1, n_tp)]
    back = sums[0]
    for l in later[1:]:
        back = jnp.where(section == l, sums[l - 1], back)
    back = lax.ppermute(back, "pipe", [(l, l - 1) for l in later])
    section_out = section_result(n_sec, n_tp, sec, back, lows, slots, hs, b_blocks)

    count = moves.shape[0]
    if n_req == 2:
        match = moves[:, 2][None, :] == jnp.arange(count, dtype=jnp.int32)[:, None]
        src = jnp.sum(jnp.where(match, moves[:, 1][None, :], 0), axis=1)
        keep = jnp.sum(match.astype(jnp.int32), axis=1)
        leaving = leaving_pages(src, keep, page_of, at, new_k, new_v, kv_pages[0])
        arrived = partner(leaving)
    else:
        keep = jnp.ones((count,), jnp.int32)
        leaving = leaving_pages(moves[:, 1], keep, page_of, at, new_k, new_v, kv_pages[0])
        free_slots = (n_req - 1) * ((count + n_req - 2) // (n_req - 1))
        received, dest_in, spots_in = (
            lax.all_gather(x, "req", axis=0, tiled=True)
            for x in (leaving, moves[:, 0], moves[:, 2])
        )
        target = jnp.where(dest_in == my_req, spots_in, free_slots)
        empty = jnp.zeros((free_slots, *leaving.shape[1:]), jnp.bfloat16)
        arrived = empty.at[target].set(received, mode="drop")
    new_kv = jnp.stack([new_k, new_v], axis=1)
    return (section_out[None], new_kv[None], arrived[None])


def solution(mesh):
    in_specs = (
        P("req", "tp"),
        P("pipe", "req", "tp"),
        P("pipe", None),
        P("pipe", None, None, "tp"),
        P("pipe", "req", None, "tp"),
        P("pipe", "req", None, "tp"),
        P("pipe", "req", None, None, "tp"),
        P("req"),
        P(),
        P("req", None),
        P("req"),
        P("req", None),
    )
    out_specs = (
        P("pipe", "req", "tp"),
        P("pipe", "req", None, "tp"),
        P("pipe", "req", None, None, "tp"),
    )
    return jax.shard_map(body, mesh=mesh, in_specs=in_specs, out_specs=out_specs, check_vma=False)
```

time: 558 us -> 239 us (0.43)
  the two profiles are of different devices: /device:TPU:0 before, /device:TPU:13 now
where the time goes in v1:
time: 239 us; the launch traced here: 237 us
  waiting for transfers between devices  91.6 us (38%)
  starting transfers between devices  59.9 us (25%)
  Pallas kernels  40.8 us (17%)
  local copies, waits for them, and re-layouts  40.1 us (17%)
  other arithmetic  2.85 us (1%)
    ppermute x6, waiting for transfers between devices, partner(): return lax.ppermute(x, 'req', [(i, i ^ 1) for i in range(n_req)])  44.5 us
    ppermute x18, starting transfers between devices, across(): return lax.ppermute(x, ('pipe', 'tp'), pairs)  38.1 us
    ppermute x12, waiting for transfers between devices, onward(): return lax.ppermute(x, ('pipe', 'tp'), pairs)  36.1 us
    unnamed x115, local copies, waits for them, and re-layouts  24.3 us
    pallas_call x1, Pallas kernels, cached_attention(): pl.pallas_call(cached_kernel, in_specs=[SM, SM, VM, ANY], out_specs=(VM,...  13.8 us
    pallas_call x3, Pallas kernels, section_slice(): pl.pallas_call(functools.partial(slice_kernel, section, n_tp, len(b_block...  12.6 us
    ppermute x18, waiting for transfers between devices, across(): return lax.ppermute(x, ('pipe', 'tp'), pairs)  11 us
    ppermute x12, starting transfers between devices, onward(): return lax.ppermute(x, ('pipe', 'tp'), pairs)  10.5 us
  transfers between devices with their start and end apart: 41, of which 14 were waited for; matrix products, arithmetic and copies ran while one was open for 8% of the time, Pallas kernels for 9%

profile of v1, /device:TPU:13, one launch (start us, length us, event | category | flops | bytes accessed | tf_op | source)
XLA Modules:
  0.0 237.0 jit_solution(6894956329726011236)
XLA Ops:
  1.3 1.5 collective-permute-start.1
  2.8 1.4 collective-permute-start.2
  5.7 2.2 copy-done.8
  7.9 1.3 split_parts.1.refs_4_.refs_7_
  9.3 2.0 copy-done.1
  12.0 2.6 %constant_dynamic-slice_fusion = (bf16[1024,256]{1,0:T(8,128)(2,1)}, bf16[1024,256]{1,0:T(8,128)(2,1)}, bf16[1024,256]{1,0:T(8,128)(2,1)}) fusion(bf16[8192,256]{1,0:T(8,128)(2,1)} %copy-done.1, s32[]{:T(128)S(6)} %select_n.154, s32[]{:T(128)S(6)} %select_n.152, s32[]{:T(128)S(6)} %select_n.150), kind=kLoop, calls=%fused_computation.44 | loop fusion | bytes 3145740 | tf_op jit(solution)/shard_map/dynamic_slice | solution.py:521
  14.8 2.4 %collective-permute-done.3.refs_13_.refs_11_ = bf16[256,1024]{1,0:T(8,128)(2,1)S(1)} collective-permute-done((bf16[256,1024]{1,0:T(8,128)(2,1)}, bf16[256,1024]{1,0:T(8,128)(2,1)S(1)}, u32[]{:S(2)}, u32[]{:S(2)}) %collective-permute-start.3) | collective-permute-done | bytes 524320 | tf_op jit(solution)/shard_map/ppermute | solution.py:489
  17.3 1.3 collective-permute-start.8
  19.4 3.2 %collective-permute-start.11 = (bf16[1024,256]{1,0:T(8,128)(2,1)}, bf16[1024,256]{1,0:T(8,128)(2,1)}, u32[]{:S(2)}, u32[]{:S(2)}) collective-permute-start(bf16[1024,256]{1,0:T(8,128)(2,1)} %get-tuple-element.80), channel_id=1, source_target_pairs={{8,9},{9,10},{10,11},{11,8},{16,17},{17,18},{18,19},{19,16},{24,25... | collective-permute-start | bytes 1572872 | tf_op jit(solution)/shard_map/ppermute | solution.py:482
  22.6 2.9 %collective-permute-start.12 = (bf16[1024,256]{1,0:T(8,128)(2,1)}, bf16[1024,256]{1,0:T(8,128)(2,1)}, u32[]{:S(2)}, u32[]{:S(2)}) collective-permute-start(bf16[1024,256]{1,0:T(8,128)(2,1)} %get-tuple-element.79), channel_id=1, source_target_pairs={{8,10},{9,11},{10,8},{11,9},{16,18},{17,19},{18,16},{19,17},{24,26... | collective-permute-start | bytes 1572872 | tf_op jit(solution)/shard_map/ppermute | solution.py:482
  25.5 3.4 %collective-permute-start.13 = (bf16[1024,256]{1,0:T(8,128)(2,1)}, bf16[1024,256]{1,0:T(8,128)(2,1)}, u32[]{:S(2)}, u32[]{:S(2)}) collective-permute-start(bf16[1024,256]{1,0:T(8,128)(2,1)} %get-tuple-element.78), channel_id=1, source_target_pairs={{8,11},{9,8},{10,9},{11,10},{16,19},{17,16},{18,17},{19,18},{24,27... | collective-permute-start | bytes 1572872 | tf_op jit(solution)/shard_map/ppermute | solution.py:482
  28.9 10.9 %collective-permute-done.9.refs_10_ = bf16[256,2048]{1,0:T(8,128)(2,1)} collective-permute-done((bf16[256,2048]{1,0:T(8,128)(2,1)}, bf16[256,2048]{1,0:T(8,128)(2,1)}, u32[]{:S(2)}, u32[]{:S(2)}) %collective-permute-start.9) | collective-permute-done | bytes 1048608 | tf_op jit(solution)/shard_map/ppermute | solution.py:489
  42.2 2.3 copy-done.3
  44.6 13.8 %cached_attention.1 = (f32[8,128,128]{2,1,0:T(8,128)S(1)}, f32[128,128]{1,0:T(8,128)S(1)}) custom-call(s32[128]{0:T(128)S(1)} %reshape.275.table_ref, s32[32]{0:T(128)S(1)} %copy-done.48, bf16[128,1024]{1,0:T(8,128)(2,1)S(1)} %bitcast.33, bf16[128,2,64,128]{3,2,1,0:T(8,128)(2,1)S(1)} %bitcast.26), custom_call_target="tpu_custom_call" | custom-call | tf_op jit(solution)/shard_map/cached_attention/pallas_call | solution.py:114
  62.1 2.3 collective-permute-done.12.refs_11_
  65.1 4.9 %collective-permute-done.13.refs_12_ = bf16[1024,256]{1,0:T(8,128)(2,1)} collective-permute-done((bf16[1024,256]{1,0:T(8,128)(2,1)}, bf16[1024,256]{1,0:T(8,128)(2,1)}, u32[]{:S(2)}, u32[]{:S(2)}) %collective-permute-start.13) | collective-permute-done | bytes 524320 | tf_op jit(solution)/shard_map/ppermute | solution.py:482
  77.2 8.6 %collective-permute-done.14.refs_13_ = bf16[1024,256]{1,0:T(8,128)(2,1)} collective-permute-done((bf16[1024,256]{1,0:T(8,128)(2,1)}, bf16[1024,256]{1,0:T(8,128)(2,1)}, u32[]{:S(2)}, u32[]{:S(2)}) %collective-permute-start.14) | collective-permute-done | bytes 524320 | tf_op jit(solution)/shard_map/ppermute | solution.py:489
  85.9 11.2 %collective-permute-done.15.refs_14_ = bf16[1024,256]{1,0:T(8,128)(2,1)} collective-permute-done((bf16[1024,256]{1,0:T(8,128)(2,1)}, bf16[1024,256]{1,0:T(8,128)(2,1)}, u32[]{:S(2)}, u32[]{:S(2)}) %collective-permute-start.15) | collective-permute-done | bytes 524320 | tf_op jit(solution)/shard_map/ppermute | solution.py:489
  97.1 11.2 %collective-permute-done.16.refs_15_ = bf16[1024,256]{1,0:T(8,128)(2,1)} collective-permute-done((bf16[1024,256]{1,0:T(8,128)(2,1)}, bf16[1024,256]{1,0:T(8,128)(2,1)}, u32[]{:S(2)}, u32[]{:S(2)}) %collective-permute-start.16) | collective-permute-done | bytes 524320 | tf_op jit(solution)/shard_map/ppermute | solution.py:489
  111.2 3.4 %section_slice_1.1 = (bf16[128,2048]{1,0:T(8,128)(2,1)S(1)}, bf16[64,128]{1,0:T(8,128)(2,1)S(1)}, bf16[144,256]{1,0:T(8,128)(2,1)S(1)}, bf16[144,256]{1,0:T(8,12...) custom-call(s32[3]{0:T(128)S(1)} %pad_add_fusion.sec_ref, bf16[64,128]{1,0:T(8,128)(2,1)S(1)} %copy-done.36, ...), custom_call_target="tpu_custom_call" | custom-call | tf_op jit(solution)/shard_map/section_slice_1/pallas_call | solution.py:349
  122.1 4.3 %section_slice_2.1 = (bf16[128,2048]{1,0:T(8,128)(2,1)}, bf16[64,128]{1,0:T(8,128)(2,1)S(1)}, bf16[144,256]{1,0:T(8,128)(2,1)S(1)}, bf16[144,256]{1,0:T(8,128)(2...) custom-call(s32[3]{0:T(128)S(1)} %pad_add_fusion.sec_ref, bf16[64,128]{1,0:T(8,128)(2,1)S(1)} %collective-permute-done.20.refs_0_, ...), custom_call_target="tpu_custom_call" | custom-call | tf_op jit(solution)/shard_map/section_slice_2/pallas_call | solution.py:349
  130.9 1.3 collective-permute-start.26
  132.2 1.3 collective-permute-start.27
  134.0 1.3 reshape.285
  135.3 2.5 %gather_fusion.1 = s32[128]{0:T(128)} fusion(s32[32,4]{0,1:T(4,128)} %param.21, s32[128]{0:T(128)} %reshape.285), kind=kCustom, calls=%fused_computation.1 | custom fusion | bytes 2048 | tf_op jit(solution)/shard_map/jit(take_along_axis)/gather | solution.py:505
  137.7 1.3 add.183
  139.1 1.3 add.203
  141.0 1.3 add.205
  142.9 1.3 add.215
  149.5 1.3 collective-permute-start.28
  150.8 1.3 collective-permute-start.29
  152.1 1.3 collective-permute-start.30
  153.4 1.3 collective-permute-start.31
  155.4 31.8 %collective-permute-done.28.refs_0_ = bf16[64,128]{1,0:T(8,128)(2,1)S(1)} collective-permute-done((bf16[64,128]{1,0:T(8,128)(2,1)S(1)}, bf16[64,128]{1,0:T(8,128)(2,1)S(1)}, u32[]{:S(2)}, u32[]{:S(2)}) %collective-permute-start.28) | collective-permute-done | bytes 16416 | tf_op jit(solution)/shard_map/ppermute | solution.py:486
  187.9 3.1 %collective-permute-done.30.refs_2_ = bf16[64,128]{1,0:T(8,128)(2,1)S(1)} collective-permute-done((bf16[64,128]{1,0:T(8,128)(2,1)S(1)}, bf16[64,128]{1,0:T(8,128)(2,1)S(1)}, u32[]{:S(2)}, u32[]{:S(2)}) %collective-permute-start.30) | collective-permute-done | bytes 16416 | tf_op jit(solution)/shard_map/ppermute | solution.py:486
  191.4 4.9 %section_slice_3.1 = (bf16[128,2048]{1,0:T(8,128)(2,1)S(1)}, bf16[64,128]{1,0:T(8,128)(2,1)S(1)}, bf16[144,256]{1,0:T(8,128)(2,1)S(1)}, bf16[144,256]{1,0:T(8,12...) custom-call(s32[3]{0:T(128)S(1)} %pad_add_fusion.sec_ref, ...), custom_call_target="tpu_custom_call" | custom-call | tf_op jit(solution)/shard_map/section_slice_3/pallas_call | solution.py:349
  196.4 3.8 %collective-permute-start.34 = (bf16[144,256]{1,0:T(8,128)(2,1)S(1)}, bf16[144,256]{1,0:T(8,128)(2,1)S(1)}, u32[]{:S(2)}, u32[]{:S(2)}) collective-permute-start(bf16[144,256]{1,0:T(8,128)(2,1)S(1)} %get-tuple-element.58), channel_id=1, source_target_pairs={{24,27},{25,24},{26,25},{27,26},{28,31},{29,28},{30,29},{31,30}} | collective-permute-start | bytes 221192 | tf_op jit(solution)/shard_map/ppermute | solution.py:482
  200.2 2.5 %collective-permute-start.35 = (bf16[144,256]{1,0:T(8,128)(2,1)S(1)}, bf16[144,256]{1,0:T(8,128)(2,1)S(1)}, u32[]{:S(2)}, u32[]{:S(2)}) collective-permute-start(bf16[144,256]{1,0:T(8,128)(2,1)S(1)} %get-tuple-element.59), channel_id=1, source_target_pairs={{24,26},{25,27},{26,24},{27,25},{28,30},{29,31},{30,28},{31,29}} | collective-permute-start | bytes 221192 | tf_op jit(solution)/shard_map/ppermute | solution.py:482
  202.7 3.3 %collective-permute-start.36 = (bf16[144,256]{1,0:T(8,128)(2,1)S(1)}, bf16[144,256]{1,0:T(8,128)(2,1)S(1)}, u32[]{:S(2)}, u32[]{:S(2)}) collective-permute-start(bf16[144,256]{1,0:T(8,128)(2,1)S(1)} %get-tuple-element.60), channel_id=1, source_target_pairs={{24,25},{25,26},{26,27},{27,24},{28,29},{29,30},{30,31},{31,28}} | collective-permute-start | bytes 221192 | tf_op jit(solution)/shard_map/ppermute | solution.py:482
  206.3 1.8 collective-permute-done.36.refs_3_
  208.1 3.9 %section_3.1 = (bf16[128,128]{1,0:T(8,128)(2,1)S(1)}, bf16[128,128]{1,0:T(8,128)(2,1)S(1)}, bf16[64,128]{1,0:T(8,128)(2,1)S(1)}) custom-call(s32[3]{0:T(128)S(1)} %pad_add_fusion.sec_ref, bf16[144,256]{1,0:T(8,128)(2,1)S(1)} %get-tuple-element.57.refs_0_, bf16[144,256]{1,0:T(8,128)(2,1)S(1)} %collective-permute-done.34.refs_1_, ...), custom_call_target="tpu_custom_call" | custom-call | tf_op jit(solution)/shard_map/section_3/pallas_call | solution.py:238
  212.1 3.6 %leaving_pages.1 = bf16[16,2,64,128]{3,2,1,0:T(8,128)(2,1)S(1)} custom-call(s32[16]{0:T(128)S(1)} %get-tuple-element.77.src_ref, s32[16]{0:T(128)S(1)} %get-tuple-element.76.keep_ref, s32[1,128]{1,0:T(1,128)S(1)} %get-tuple-element.87.page_ref, s32[1,128]{1,0:T(1,128)S(1)} %get-tuple-element.86.at_ref, bf16[128,128]{1,0:T(8,128)(2,1)S(1)} %get-tuple-element.65.k_ref, ...), custom_call_target="tpu_custom_call" | custom-call | tf_op jit(solution)/shard_map/leaving_pages/pallas_call | solution.py:437
  215.7 1.3 collective-permute-start.40
  219.0 3.3 %collective-permute-start.37 = (bf16[64,128]{1,0:T(8,128)(2,1)S(1)}, bf16[64,128]{1,0:T(8,128)(2,1)S(1)}, u32[]{:S(2)}, u32[]{:S(2)}) collective-permute-start(bf16[64,128]{1,0:T(8,128)(2,1)S(1)} %get-tuple-element.63.refs_0_), channel_id=1, source_target_pairs={{24,25},{25,26},{26,27},{27,24},{28,29},{29,30},{30,31},{31,28}} | collective-permute-start | bytes 49160 | tf_op jit(solution)/shard_map/ppermute | solution.py:482
  222.3 4.4 %collective-permute-start.38 = (bf16[64,128]{1,0:T(8,128)(2,1)S(1)}, bf16[64,128]{1,0:T(8,128)(2,1)S(1)}, u32[]{:S(2)}, u32[]{:S(2)}) collective-permute-start(bf16[64,128]{1,0:T(8,128)(2,1)S(1)} %get-tuple-element.63.refs_0_), channel_id=1, source_target_pairs={{24,26},{25,27},{26,24},{27,25},{28,30},{29,31},{30,28},{31,29}} | collective-permute-start | bytes 49160 | tf_op jit(solution)/shard_map/ppermute | solution.py:482
  226.8 1.9 collective-permute-start.39
  229.4 1.8 collective-permute-done.39.refs_3_
  233.5 2.6 %section_result.1 = bf16[128,2048]{1,0:T(8,128)(2,1)} custom-call(s32[3]{0:T(128)S(1)} %pad_add_fusion.sec_ref, bf16[64,128]{1,0:T(8,128)(2,1)S(1)} %collective-permute-done.33.back_ref, bf16[64,128]{1,0:T(8,128)(2,1)S(1)} %get-tuple-element.63.refs_0_, bf16[64,128]{1,0:T(8,128)(2,1)S(1)} %collective-permute-done.37.refs_1_, ...), custom_call_target="tpu_custom_call" | custom-call | tf_op jit(solution)/shard_map/section_result/pallas_call | solution.py:393
  (191 shorter events, 47.1 us)
Async XLA Ops:
  0.6 17.9 %collective-permute-start = (bf16[128,2048]{1,0:T(8,128)(2,1)}, bf16[128,2048]{1,0:T(8,128)(2,1)S(1)}, u32[]{:S(2)}, u32[]{:S(2)}) collective-permute-start(bf16[128,2048]{1,0:T(8,128)(2,1)} %refs_5_.3), channel_id=1, source_target_pairs={{0,1},{1,2},{2,3},{3,0},{4,5},{5,6},{6,7},{7,4}} | collective-permute-start | bytes 1572872 | tf_op jit(solution)/shard_map/ppermute | solution.py:482
  1.3 21.2 %collective-permute-start.1 = (bf16[128,2048]{1,0:T(8,128)(2,1)}, bf16[128,2048]{1,0:T(8,128)(2,1)}, u32[]{:S(2)}, u32[]{:S(2)}) collective-permute-start(bf16[128,2048]{1,0:T(8,128)(2,1)} %refs_5_.3), channel_id=1, source_target_pairs={{0,2},{1,3},{2,0},{3,1},{4,6},{5,7},{6,4},{7,5}} | collective-permute-start | bytes 1572872 | tf_op jit(solution)/shard_map/ppermute | solution.py:482
  2.8 22.7 %collective-permute-start.2 = (bf16[128,2048]{1,0:T(8,128)(2,1)}, bf16[128,2048]{1,0:T(8,128)(2,1)}, u32[]{:S(2)}, u32[]{:S(2)}) collective-permute-start(bf16[128,2048]{1,0:T(8,128)(2,1)} %refs_5_.3), channel_id=1, source_target_pairs={{0,3},{1,0},{2,1},{3,2},{4,7},{5,4},{6,5},{7,6}} | collective-permute-start | bytes 1572872 | tf_op jit(solution)/shard_map/ppermute | solution.py:482
  4.3 13.0 %collective-permute-start.3 = (bf16[256,1024]{1,0:T(8,128)(2,1)}, bf16[256,1024]{1,0:T(8,128)(2,1)S(1)}, u32[]{:S(2)}, u32[]{:S(2)}) collective-permute-start(bf16[256,1024]{1,0:T(8,128)(2,1)} %bitcast.28), channel_id=1, source_target_pairs={{0,4},{4,0},{1,5},{5,1},{2,6},{6,2},{3,7},{7,3},{8,12},{12,8},{9,1... | collective-permute-start | bytes 1572872 | tf_op jit(solution)/shard_map/ppermute | solution.py:489
  5.5 34.4 %collective-permute-start.9 = (bf16[256,2048]{1,0:T(8,128)(2,1)}, bf16[256,2048]{1,0:T(8,128)(2,1)}, u32[]{:S(2)}, u32[]{:S(2)}) collective-permute-start(bf16[256,2048]{1,0:T(8,128)(2,1)} %bitcast.39), channel_id=1, source_target_pairs={{0,4},{4,0},{1,5},{5,1},{2,6},{6,2},{3,7},{7,3},{8,12},{12,8},{9,1... | collective-permute-start | bytes 3145736 | tf_op jit(solution)/shard_map/ppermute | solution.py:489
  12.0 46.9 %copy-start.5 = (bf16[1,4,64,1024]{3,2,1,0:T(8,128)(2,1)S(1)}, bf16[1,4,64,1024]{3,2,1,0:T(8,128)(2,1)}, u32[]{:S(2)}) copy-start(bf16[1,4,64,1024]{3,2,1,0:T(8,128)(2,1)} %param.16) | copy-start | bytes 1572868
  12.0 46.9 %copy-start.7 = (bf16[128,2048]{1,0:T(8,128)(2,1)S(1)}, bf16[128,2048]{1,0:T(8,128)(2,1)}, u32[]{:S(2)}) copy-start(bf16[128,2048]{1,0:T(8,128)(2,1)} %refs_5_.3) | copy-start | bytes 1572868
  17.3 91.1 %collective-permute-start.8 = (bf16[256,2048]{1,0:T(8,128)(2,1)}, bf16[256,2048]{1,0:T(8,128)(2,1)S(1)}, u32[]{:S(2)}, u32[]{:S(2)}) collective-permute-start(bf16[256,2048]{1,0:T(8,128)(2,1)} %bitcast.40), channel_id=1, source_target_pairs={{0,8},{8,16},{16,24},{1,9},{9,17},{17,25},{2,10},{10,18},{18,26},{... | collective-permute-start | bytes 3145736 | tf_op jit(solution)/shard_map/ppermute | solution.py:525
  19.4 42.1 %collective-permute-start.11 = (bf16[1024,256]{1,0:T(8,128)(2,1)}, bf16[1024,256]{1,0:T(8,128)(2,1)}, u32[]{:S(2)}, u32[]{:S(2)}) collective-permute-start(bf16[1024,256]{1,0:T(8,128)(2,1)} %get-tuple-element.80), channel_id=1, source_target_pairs={{8,9},{9,10},{10,11},{11,8},{16,17},{17,18},{18,19},{19,16},{24,25... | collective-permute-start | bytes 1572872 | tf_op jit(solution)/shard_map/ppermute | solution.py:482
  22.6 41.9 %collective-permute-start.12 = (bf16[1024,256]{1,0:T(8,128)(2,1)}, bf16[1024,256]{1,0:T(8,128)(2,1)}, u32[]{:S(2)}, u32[]{:S(2)}) collective-permute-start(bf16[1024,256]{1,0:T(8,128)(2,1)} %get-tuple-element.79), channel_id=1, source_target_pairs={{8,10},{9,11},{10,8},{11,9},{16,18},{17,19},{18,16},{19,17},{24,26... | collective-permute-start | bytes 1572872 | tf_op jit(solution)/shard_map/ppermute | solution.py:482
  25.5 44.5 %collective-permute-start.13 = (bf16[1024,256]{1,0:T(8,128)(2,1)}, bf16[1024,256]{1,0:T(8,128)(2,1)}, u32[]{:S(2)}, u32[]{:S(2)}) collective-permute-start(bf16[1024,256]{1,0:T(8,128)(2,1)} %get-tuple-element.78), channel_id=1, source_target_pairs={{8,11},{9,8},{10,9},{11,10},{16,19},{17,16},{18,17},{19,18},{24,27... | collective-permute-start | bytes 1572872 | tf_op jit(solution)/shard_map/ppermute | solution.py:482
  39.8 68.5 %collective-permute-start.10 = (bf16[256,2048]{1,0:T(8,128)(2,1)}, bf16[256,2048]{1,0:T(8,128)(2,1)}, u32[]{:S(2)}, u32[]{:S(2)}) collective-permute-start(bf16[256,2048]{1,0:T(8,128)(2,1)} %collective-permute-done.9.refs_10_), channel_id=1, source_target_pairs={{0,8},{8,16},{16,24},{1,9},{9,17},{17,25},{2,10},{10,18},{18,26},{... | collective-permute-start | bytes 3145736 | tf_op jit(solution)/shard_map/ppermute | solution.py:525
  61.5 9.2 %collective-permute-start.4 = (bf16[64,128]{1,0:T(8,128)(2,1)S(1)}, bf16[64,128]{1,0:T(8,128)(2,1)S(1)}, u32[]{:S(2)}, u32[]{:S(2)}) collective-permute-start(bf16[64,128]{1,0:T(8,128)(2,1)S(1)} %get-tuple-element.37), channel_id=1, source_target_pairs={{0,8},{1,9},{2,10},{3,11},{4,12},{5,13},{6,14},{7,15}} | collective-permute-start | bytes 49160 | tf_op jit(solution)/shard_map/ppermute | solution.py:486
  64.4 7.5 %collective-permute-start.5 = (bf16[64,128]{1,0:T(8,128)(2,1)S(1)}, bf16[64,128]{1,0:T(8,128)(2,1)S(1)}, u32[]{:S(2)}, u32[]{:S(2)}) collective-permute-start(bf16[64,128]{1,0:T(8,128)(2,1)S(1)} %get-tuple-element.37), channel_id=1, source_target_pairs={{0,9},{1,10},{2,11},{3,8},{4,13},{5,14},{6,15},{7,12}} | collective-permute-start | bytes 49160 | tf_op jit(solution)/shard_map/ppermute | solution.py:486
  70.0 3.8 %collective-permute-start.6 = (bf16[64,128]{1,0:T(8,128)(2,1)S(1)}, bf16[64,128]{1,0:T(8,128)(2,1)S(1)}, u32[]{:S(2)}, u32[]{:S(2)}) collective-permute-start(bf16[64,128]{1,0:T(8,128)(2,1)S(1)} %get-tuple-element.37), channel_id=1, source_target_pairs={{0,10},{1,11},{2,8},{3,9},{4,14},{5,15},{6,12},{7,13}} | collective-permute-start | bytes 49160 | tf_op jit(solution)/shard_map/ppermute | solution.py:486
  71.3 3.3 %collective-permute-start.7 = (bf16[64,128]{1,0:T(8,128)(2,1)S(1)}, bf16[64,128]{1,0:T(8,128)(2,1)S(1)}, u32[]{:S(2)}, u32[]{:S(2)}) collective-permute-start(bf16[64,128]{1,0:T(8,128)(2,1)S(1)} %get-tuple-element.37), channel_id=1, source_target_pairs={{0,11},{1,8},{2,9},{3,10},{4,15},{5,12},{6,13},{7,14}} | collective-permute-start | bytes 49160 | tf_op jit(solution)/shard_map/ppermute | solution.py:486
  72.5 13.3 %collective-permute-start.14 = (bf16[1024,256]{1,0:T(8,128)(2,1)}, bf16[1024,256]{1,0:T(8,128)(2,1)}, u32[]{:S(2)}, u32[]{:S(2)}) collective-permute-start(bf16[1024,256]{1,0:T(8,128)(2,1)} %collective-permute-done.11.refs_10_), channel_id=1, source_target_pairs={{0,4},{4,0},{1,5},{5,1},{2,6},{6,2},{3,7},{7,3},{8,12},{12,8},{9,1... | collective-permute-start | bytes 1572872 | tf_op jit(solution)/shard_map/ppermute | solution.py:489
  74.4 22.7 %collective-permute-start.15 = (bf16[1024,256]{1,0:T(8,128)(2,1)}, bf16[1024,256]{1,0:T(8,128)(2,1)}, u32[]{:S(2)}, u32[]{:S(2)}) collective-permute-start(bf16[1024,256]{1,0:T(8,128)(2,1)} %collective-permute-done.12.refs_11_), channel_id=1, source_target_pairs={{0,4},{4,0},{1,5},{5,1},{2,6},{6,2},{3,7},{7,3},{8,12},{12,8},{9,1... | collective-permute-start | bytes 1572872 | tf_op jit(solution)/shard_map/ppermute | solution.py:489
  75.2 33.1 %collective-permute-start.16 = (bf16[1024,256]{1,0:T(8,128)(2,1)}, bf16[1024,256]{1,0:T(8,128)(2,1)}, u32[]{:S(2)}, u32[]{:S(2)}) collective-permute-start(bf16[1024,256]{1,0:T(8,128)(2,1)} %collective-permute-done.13.refs_12_), channel_id=1, source_target_pairs={{0,4},{4,0},{1,5},{5,1},{2,6},{6,2},{3,7},{7,3},{8,12},{12,8},{9,1... | collective-permute-start | bytes 1572872 | tf_op jit(solution)/shard_map/ppermute | solution.py:489
  114.7 7.4 %collective-permute-start.24 = (bf16[128,2048]{1,0:T(8,128)(2,1)S(1)}, bf16[128,2048]{1,0:T(8,128)(2,1)S(1)}, u32[]{:S(2)}, u32[]{:S(2)}) collective-permute-start(bf16[128,2048]{1,0:T(8,128)(2,1)S(1)} %get-tuple-element.45.refs_6_), channel_id=1, source_target_pairs={{8,16},{9,17},{10,18},{11,19},{12,20},{13,21},{14,22},{15,23}} | collective-permute-start | bytes 1572872 | tf_op jit(solution)/shard_map/ppermute | solution.py:549
  115.4 2.0 collective-permute-start.17
  116.0 1.4 collective-permute-start.18
  116.7 0.7 collective-permute-start.19
  119.2 2.8 %collective-permute-start.20 = (bf16[64,128]{1,0:T(8,128)(2,1)S(1)}, bf16[64,128]{1,0:T(8,128)(2,1)S(1)}, u32[]{:S(2)}, u32[]{:S(2)}) collective-permute-start(bf16[64,128]{1,0:T(8,128)(2,1)S(1)} %get-tuple-element.44), channel_id=1, source_target_pairs={{8,16},{9,17},{10,18},{11,19},{12,20},{13,21},{14,22},{15,23}} | collective-permute-start | bytes 49160 | tf_op jit(solution)/shard_map/ppermute | solution.py:486
  120.0 2.0 collective-permute-start.21
  120.7 1.4 collective-permute-start.22
  121.4 0.7 collective-permute-start.23
  127.6 63.8 %collective-permute-start.32 = (bf16[128,2048]{1,0:T(8,128)(2,1)}, bf16[128,2048]{1,0:T(8,128)(2,1)}, u32[]{:S(2)}, u32[]{:S(2)}) collective-permute-start(bf16[128,2048]{1,0:T(8,128)(2,1)} %get-tuple-element.53.refs_7_), channel_id=1, source_target_pairs={{16,24},{17,25},{18,26},{19,27},{20,28},{21,29},{22,30},{23,31}} | collective-permute-start | bytes 1572872 | tf_op jit(solution)/shard_map/ppermute | solution.py:549
  129.6 14.6 %collective-permute-start.25 = (bf16[144,256]{1,0:T(8,128)(2,1)}, bf16[144,256]{1,0:T(8,128)(2,1)}, u32[]{:S(2)}, u32[]{:S(2)}) collective-permute-start(bf16[144,256]{1,0:T(8,128)(2,1)} %get-tuple-element.47), channel_id=1, source_target_pairs={{16,19},{17,16},{18,17},{19,18},{20,23},{21,20},{22,21},{23,22}} | collective-permute-start | bytes 221192 | tf_op jit(solution)/shard_map/ppermute | solution.py:482
  130.9 13.4 %collective-permute-start.26 = (bf16[144,256]{1,0:T(8,128)(2,1)}, bf16[144,256]{1,0:T(8,128)(2,1)}, u32[]{:S(2)}, u32[]{:S(2)}) collective-permute-start(bf16[144,256]{1,0:T(8,128)(2,1)} %get-tuple-element.48), channel_id=1, source_target_pairs={{16,18},{17,19},{18,16},{19,17},{20,22},{21,23},{22,20},{23,21}} | collective-permute-start | bytes 221192 | tf_op jit(solution)/shard_map/ppermute | solution.py:482
  132.2 12.1 %collective-permute-start.27 = (bf16[144,256]{1,0:T(8,128)(2,1)}, bf16[144,256]{1,0:T(8,128)(2,1)}, u32[]{:S(2)}, u32[]{:S(2)}) collective-permute-start(bf16[144,256]{1,0:T(8,128)(2,1)} %get-tuple-element.49), channel_id=1, source_target_pairs={{16,17},{17,18},{18,19},{19,16},{20,21},{21,22},{22,23},{23,20}} | collective-permute-start | bytes 221192 | tf_op jit(solution)/shard_map/ppermute | solution.py:482
  149.5 37.7 %collective-permute-start.28 = (bf16[64,128]{1,0:T(8,128)(2,1)S(1)}, bf16[64,128]{1,0:T(8,128)(2,1)S(1)}, u32[]{:S(2)}, u32[]{:S(2)}) collective-permute-start(bf16[64,128]{1,0:T(8,128)(2,1)S(1)} %get-tuple-element.52), channel_id=1, source_target_pairs={{16,24},{17,25},{18,26},{19,27},{20,28},{21,29},{22,30},{23,31}} | collective-permute-start | bytes 49160 | tf_op jit(solution)/shard_map/ppermute | solution.py:486
  150.8 37.1 %collective-permute-start.29 = (bf16[64,128]{1,0:T(8,128)(2,1)S(1)}, bf16[64,128]{1,0:T(8,128)(2,1)S(1)}, u32[]{:S(2)}, u32[]{:S(2)}) collective-permute-start(bf16[64,128]{1,0:T(8,128)(2,1)S(1)} %get-tuple-element.52), channel_id=1, source_target_pairs={{16,25},{17,26},{18,27},{19,24},{20,29},{21,30},{22,31},{23,28}} | collective-permute-start | bytes 49160 | tf_op jit(solution)/shard_map/ppermute | solution.py:486
  152.1 38.9 %collective-permute-start.30 = (bf16[64,128]{1,0:T(8,128)(2,1)S(1)}, bf16[64,128]{1,0:T(8,128)(2,1)S(1)}, u32[]{:S(2)}, u32[]{:S(2)}) collective-permute-start(bf16[64,128]{1,0:T(8,128)(2,1)S(1)} %get-tuple-element.52), channel_id=1, source_target_pairs={{16,26},{17,27},{18,24},{19,25},{20,30},{21,31},{22,28},{23,29}} | collective-permute-start | bytes 49160 | tf_op jit(solution)/shard_map/ppermute | solution.py:486
  153.4 38.0 %collective-permute-start.31 = (bf16[64,128]{1,0:T(8,128)(2,1)S(1)}, bf16[64,128]{1,0:T(8,128)(2,1)S(1)}, u32[]{:S(2)}, u32[]{:S(2)}) collective-permute-start(bf16[64,128]{1,0:T(8,128)(2,1)S(1)} %get-tuple-element.52), channel_id=1, source_target_pairs={{16,27},{17,24},{18,25},{19,26},{20,31},{21,28},{22,29},{23,30}} | collective-permute-start | bytes 49160 | tf_op jit(solution)/shard_map/ppermute | solution.py:486
  155.3 50.7 %copy-start.52 = (s32[16]{0:T(128)S(1)}, s32[16]{0:T(128)}, u32[]{:S(2)}) copy-start(s32[16]{0:T(128)} %get-tuple-element.81) | copy-start | bytes 196
  155.3 50.7 %copy-start.53 = (s32[16]{0:T(128)S(1)}, s32[16]{0:T(128)}, u32[]{:S(2)}) copy-start(s32[16]{0:T(128)} %get-tuple-element.82) | copy-start | bytes 196
  155.3 52.8 %copy-start.12 = (f32[128,128]{1,0:T(8,128)S(1)}, f32[128,128]{1,0:T(8,128)}, u32[]{:S(2)}) copy-start(f32[128,128]{1,0:T(8,128)} %copy-done.9) | copy-start | bytes 196612
  155.3 52.8 %copy-start.16 = (f32[128,128]{1,0:T(8,128)S(1)}, f32[128,128]{1,0:T(8,128)}, u32[]{:S(2)}) copy-start(f32[128,128]{1,0:T(8,128)} %copy-done.13) | copy-start | bytes 196612
  155.4 56.7 %copy-start.4 = (bf16[1,128,2,64,128]{4,3,2,1,0:T(8,128)(2,1)S(1)}, bf16[1,128,2,64,128]{4,3,2,1,0:T(8,128)(2,1)}, u32[]{:S(2)}) copy-start(bf16[1,128,2,64,128]{4,3,2,1,0:T(8,128)(2,1)} %param.18) | copy-start | bytes 12582916
  196.4 9.7 %collective-permute-start.34 = (bf16[144,256]{1,0:T(8,128)(2,1)S(1)}, bf16[144,256]{1,0:T(8,128)(2,1)S(1)}, u32[]{:S(2)}, u32[]{:S(2)}) collective-permute-start(bf16[144,256]{1,0:T(8,128)(2,1)S(1)} %get-tuple-element.58), channel_id=1, source_target_pairs={{24,27},{25,24},{26,25},{27,26},{28,31},{29,28},{30,29},{31,30}} | collective-permute-start | bytes 221192 | tf_op jit(solution)/shard_map/ppermute | solution.py:482
  200.2 6.1 %collective-permute-start.35 = (bf16[144,256]{1,0:T(8,128)(2,1)S(1)}, bf16[144,256]{1,0:T(8,128)(2,1)S(1)}, u32[]{:S(2)}, u32[]{:S(2)}) collective-permute-start(bf16[144,256]{1,0:T(8,128)(2,1)S(1)} %get-tuple-element.59), channel_id=1, source_target_pairs={{24,26},{25,27},{26,24},{27,25},{28,30},{29,31},{30,28},{31,29}} | collective-permute-start | bytes 221192 | tf_op jit(solution)/shard_map/ppermute | solution.py:482
  202.7 5.4 %collective-permute-start.36 = (bf16[144,256]{1,0:T(8,128)(2,1)S(1)}, bf16[144,256]{1,0:T(8,128)(2,1)S(1)}, u32[]{:S(2)}, u32[]{:S(2)}) collective-permute-start(bf16[144,256]{1,0:T(8,128)(2,1)S(1)} %get-tuple-element.60), channel_id=1, source_target_pairs={{24,25},{25,26},{26,27},{27,24},{28,29},{29,30},{30,31},{31,28}} | collective-permute-start | bytes 221192 | tf_op jit(solution)/shard_map/ppermute | solution.py:482
  215.7 20.4 %collective-permute-start.40 = (bf16[16,2,64,128]{3,2,1,0:T(8,128)(2,1)S(1)}, bf16[16,2,64,128]{3,2,1,0:T(8,128)(2,1)S(1)}, u32[]{:S(2)}, u32[]{:S(2)}) collective-permute-start(bf16[16,2,64,128]{3,2,1,0:T(8,128)(2,1)S(1)} %leaving_pages.1), channel_id=1, source_target_pairs={{0,4},{4,0},{1,5},{5,1},{2,6},{6,2},{3,7},{7,3},{8,12},{12,8},{9,1... | collective-permute-start | bytes 1572872 | tf_op jit(solution)/shard_map/ppermute | solution.py:489
  217.8 11.6 %collective-permute-start.33 = (bf16[64,128]{1,0:T(8,128)(2,1)S(1)}, bf16[64,128]{1,0:T(8,128)(2,1)S(1)}, u32[]{:S(2)}, u32[]{:S(2)}) collective-permute-start(bf16[64,128]{1,0:T(8,128)(2,1)S(1)} %select_select_fusion), channel_id=1, source_target_pairs={{8,0},{16,8},{24,16},{9,1},{17,9},{25,17},{10,2},{18,10},{26,18},{... | collective-permute-start | bytes 49160 | tf_op jit(solution)/shard_map/ppermute | solution.py:561
  219.0 10.4 %collective-permute-start.37 = (bf16[64,128]{1,0:T(8,128)(2,1)S(1)}, bf16[64,128]{1,0:T(8,128)(2,1)S(1)}, u32[]{:S(2)}, u32[]{:S(2)}) collective-permute-start(bf16[64,128]{1,0:T(8,128)(2,1)S(1)} %get-tuple-element.63.refs_0_), channel_id=1, source_target_pairs={{24,25},{25,26},{26,27},{27,24},{28,29},{29,30},{30,31},{31,28}} | collective-permute-start | bytes 49160 | tf_op jit(solution)/shard_map/ppermute | solution.py:482
  222.3 7.1 %collective-permute-start.38 = (bf16[64,128]{1,0:T(8,128)(2,1)S(1)}, bf16[64,128]{1,0:T(8,128)(2,1)S(1)}, u32[]{:S(2)}, u32[]{:S(2)}) collective-permute-start(bf16[64,128]{1,0:T(8,128)(2,1)S(1)} %get-tuple-element.63.refs_0_), channel_id=1, source_target_pairs={{24,26},{25,27},{26,24},{27,25},{28,30},{29,31},{30,28},{31,29}} | collective-permute-start | bytes 49160 | tf_op jit(solution)/shard_map/ppermute | solution.py:482
  226.8 4.5 %collective-permute-start.39 = (bf16[64,128]{1,0:T(8,128)(2,1)S(1)}, bf16[64,128]{1,0:T(8,128)(2,1)S(1)}, u32[]{:S(2)}, u32[]{:S(2)}) collective-permute-start(bf16[64,128]{1,0:T(8,128)(2,1)S(1)} %get-tuple-element.63.refs_0_), channel_id=1, source_target_pairs={{24,27},{25,24},{26,25},{27,26},{28,31},{29,28},{30,29},{31,30}} | collective-permute-start | bytes 49160 | tf_op jit(solution)/shard_map/ppermute | solution.py:482
  (49 other events, 476.9 us)

commit v2 on v1

v2 whole, which is shorter than its diff:
```python
import functools
import math

import jax
import jax.numpy as jnp
from jax import lax
from jax.experimental import pallas as pl
from jax.experimental.pallas import tpu as pltpu
from jax.sharding import PartitionSpec as P

HD = 128
R = 64
S = 4
PAGE = 64
MAXP = 4
EPS = 1e-05
BIG = -1e30
VMEM_MIB = 32
SCALE = HD ** (-0.5)
VM = pl.BlockSpec(memory_space=pltpu.VMEM)
SM = pl.BlockSpec(memory_space=pltpu.SMEM)
ANY = pl.BlockSpec(memory_space=pltpu.HBM)
NT = (((1,), (1,)), ((), ()))


def vmem(mib=VMEM_MIB):
    return pltpu.CompilerParams(vmem_limit_bytes=mib << 20)


def kept(shape, dtype):
    return pltpu.VMEM(shape, dtype)


def in_hbm(x):
    return pltpu.with_memory_space_constraint(x, pltpu.HBM)


def cost(micros):
    return pl.CostEstimate(flops=0, bytes_accessed=int(micros * 3_000_000), transcendentals=0)


def sds(shape, dtype):
    return jax.ShapeDtypeStruct(shape, dtype)


def halves_of(rows):
    return rows // 2


def split_kernel(chunks, section_of, sec_ref, *refs):
    raw_refs, (out_ref, buf, wide, sems) = refs[:-4], refs[-4:]
    rows = buf.shape[1] // 2

    @pl.when(section_of(sec_ref[0]))
    def _():
        loads = []
        for index, (source, start, _) in enumerate(chunks):
            first = pl.multiple_of(start(sec_ref) * 2 * rows, 2 * rows)
            loads.append(
                pltpu.make_async_copy(
                    raw_refs[source].at[pl.ds(first, 2 * rows)], buf.at[index], sems.at[index]
                )
            )
            loads[-1].start()
        for index, (_, _, to) in enumerate(chunks):
            loads[index].wait()
            wide[...] = buf[index].astype(jnp.float32)
            out = pl.ds(pl.multiple_of(to(sec_ref) * rows, rows), rows)
            out_ref[out, :HD] = wide[pl.ds(0, rows, stride=2), :].astype(jnp.bfloat16)
            out_ref[out, HD:] = wide[pl.ds(1, rows, stride=2), :].astype(jnp.bfloat16)


def split_parts(sec, raws, chunks, section_of, rows, name):
    return pl.pallas_call(
        functools.partial(split_kernel, chunks, section_of),
        in_specs=[SM] + [ANY] * len(raws),
        out_specs=VM,
        out_shape=kept((rows * len(chunks), 2 * HD), jnp.bfloat16),
        scratch_shapes=[
            pltpu.VMEM((len(chunks), 2 * rows, HD), jnp.bfloat16),
            pltpu.VMEM((2 * rows, HD), jnp.float32),
            pltpu.SemaphoreType.DMA((len(chunks),)),
        ],
        compiler_params=vmem(),
        cost_estimate=cost(5),
        name=name,
    )(sec, *[in_hbm(x) for x in raws])


def parcel_kernel(n_tp, sec_ref, h_ref, raw_ref, *refs):
    out_refs, sems = refs[:-1], refs[-1]
    rows = out_refs[0].shape[0]
    width = h_ref.shape[1]

    @pl.when(sec_ref[0] == 0)
    def _():
        for out in out_refs:
            for c in range(width // HD):
                out[c * HD : (c + 1) * HD, :] = h_ref[:, c * HD : (c + 1) * HD]

    @pl.when(sec_ref[0] != 0)
    def _():
        loads = []
        for s in range(1, n_tp):
            place = lax.rem(sec_ref[1] + s, n_tp) * 2 + sec_ref[2]
            first = pl.multiple_of(place * rows, rows)
            loads.append(
                pltpu.make_async_copy(
                    raw_ref.at[pl.ds(first, rows)], out_refs[s - 1], sems.at[s - 1]
                )
            )
            loads[-1].start()
        for load in loads:
            load.wait()


def parcels(sec, hidden, raw, n_tp):
    tokens, width = hidden.shape
    rows = raw.shape[0] // (2 * n_tp)
    assert tokens == HD and rows * HD == tokens * width
    return pl.pallas_call(
        functools.partial(parcel_kernel, n_tp),
        in_specs=[SM, VM, ANY],
        out_specs=(VM,) * (n_tp - 1),
        out_shape=(sds((rows, HD), jnp.bfloat16),) * (n_tp - 1),
        scratch_shapes=[pltpu.SemaphoreType.DMA((n_tp - 1,))],
        compiler_params=vmem(),
        cost_estimate=cost(2),
        name="parcels",
    )(sec, hidden, in_hbm(raw))


def local_kernel(
    paired,
    adapters,
    sec_ref,
    table_ref,
    len_ref,
    ids_ref,
    rows_ref,
    move_ref,
    q_ref,
    pages_ref,
    acc_ref,
    lse_ref,
    slot_ref,
    cos_ref,
    sin_ref,
    leave_ref,
    spot_ref,
    buf,
    place,
    sems,
    leave_sem,
):
    heads, tokens, _ = acc_ref.shape
    reqs = tokens // S
    moves = leave_ref.shape[0]
    per = 16 // S
    ctx = MAXP * PAGE
    pages = per * MAXP

    def start(i, _):
        page = table_ref[i]
        place[page] = i
        pltpu.make_async_copy(pages_ref.at[page], buf.at[i], sems.at[i // pages]).start()
        return 0

    lax.fori_loop(0, reqs * MAXP, start, 0, unroll=8)
    lanes = lax.broadcasted_iota(jnp.int32, (1, tokens), 1)

    def leave(i, _):
        page = move_ref[3 * i + 1]
        to = move_ref[3 * i + 2] if paired else i
        pltpu.make_async_copy(pages_ref.at[page], leave_ref.at[to], leave_sem).start()
        index = place[page]
        req = index // MAXP
        position = len_ref[req] + lanes % S
        hit = (lanes // S == req) & (position // PAGE == index % MAXP)
        spot_ref[pl.ds(to, 1), :] = jnp.where(hit, position % PAGE, -1)
        return 0

    lax.fori_loop(0, moves, leave, 0)

    eight = lax.broadcasted_iota(jnp.int32, (8, HD), 0)
    freq = jnp.exp(
        (-math.log(500000.0) * 2.0 / HD)
        * (lax.broadcasted_iota(jnp.int32, (8, HD), 1) % (HD // 2)).astype(jnp.float32)
    )
    sign = jnp.where(lax.broadcasted_iota(jnp.int32, (8, HD), 1) < HD // 2, -1.0, 1.0)
    for i in range(tokens // 8):
        slot, length = [], []
        for r in (2 * i, 2 * i + 1):
            row = rows_ref[ids_ref[r]]
            if paired:
                away = jnp.where(row // adapters == sec_ref[3], 0, adapters)
                row = row % adapters + away
            slot.append(row)
            length.append(len_ref[r])
        span = slice(8 * i, 8 * i + 8)
        first = eight < S
        slot_ref[span, :] = jnp.where(first, slot[0], slot[1])
        position = jnp.where(first, length[0], length[1]) + eight % S
        angle = position.astype(jnp.float32) * freq
        cos_ref[span, :] = jnp.cos(angle)
        sin_ref[span, :] = jnp.sin(angle) * sign

    lane = lax.broadcasted_iota(jnp.int32, (ctx, HD), 1)
    mine = (lane % 16) // S
    lane16 = lax.broadcasted_iota(jnp.int32, (16, HD), 1)
    key_at = lax.broadcasted_iota(jnp.int32, (ctx, HD), 0)
    row_of = (lax.broadcasted_iota(jnp.int32, (HD, HD), 0) % 16) // S

    def group(g, _):
        first = pl.multiple_of(g * pages, pages)
        block = buf.at[pl.ds(first, pages)]
        pltpu.make_async_copy(block, block, sems.at[g]).wait()
        row = pl.multiple_of(g * 16, 16)
        q = jnp.concatenate(
            [q_ref[pl.ds(row, 16), h * HD : (h + 1) * HD] for h in range(heads)], axis=0
        )
        scores = None
        limit = None
        for r in range(per):
            keys = buf[pl.ds(first + r * MAXP, MAXP), 0].reshape(ctx, HD)
            part = lax.dot_general(keys, q, NT, preferred_element_type=jnp.float32)
            length = len_ref[g * per + r]
            scores = part if r == 0 else jnp.where(mine == r, part, scores)
            limit = length if r == 0 else jnp.where(mine[:1] == r, length, limit)
        scores = jnp.where(key_at < limit, scores * SCALE, BIG)
        top = jnp.max(scores, axis=0, keepdims=True)
        weights = jnp.exp(scores - top)
        total = jnp.sum(weights, axis=0, keepdims=True)
        column = jnp.transpose(jnp.broadcast_to(top + jnp.log(total), (HD, HD)))
        packed = column[:16]
        for h in range(1, heads):
            packed = jnp.where(lane16 == h, column[h * 16 : (h + 1) * 16], packed)
        lse_ref[pl.ds(row, 16), :] = packed
        weights = jnp.transpose(weights * (1.0 / total)).astype(jnp.bfloat16)
        mixed = None
        for r in range(per):
            values = buf[pl.ds(first + r * MAXP, MAXP), 1].reshape(ctx, HD)
            part = jnp.dot(weights, values, preferred_element_type=jnp.float32)
            mixed = part if r == 0 else jnp.where(row_of == r, part, mixed)
        for h in range(heads):
            acc_ref[h, pl.ds(row, 16), :] = mixed[h * 16 : (h + 1) * 16]
        return 0

    lax.fori_loop(0, reqs // per, group, 0, unroll=2)
    pltpu.make_async_copy(leave_ref, leave_ref, leave_sem).wait()


def local_work(paired, adapters, sec, table, lengths, ids, rows, moves, queries, pages):
    tokens, width = queries.shape
    heads = width // HD
    count = moves.shape[0] // 3
    groups = tokens // 16
    square = (tokens, HD)
    return pl.pallas_call(
        functools.partial(local_kernel, paired, adapters),
        in_specs=[SM] * 6 + [VM, ANY],
        out_specs=(VM,) * 7,
        out_shape=(
            kept((heads, tokens, HD), jnp.float32),
            kept(square, jnp.float32),
            kept(square, jnp.int32),
            kept(square, jnp.float32),
            kept(square, jnp.float32),
            sds((count, *pages.shape[1:]), jnp.bfloat16),
            sds((count, tokens), jnp.int32),
        ),
        scratch_shapes=[
            pltpu.VMEM(pages.shape, pages.dtype),
            pltpu.SMEM((pages.shape[0],), jnp.int32),
            pltpu.SemaphoreType.DMA((groups,)),
            pltpu.SemaphoreType.DMA,
        ],
        compiler_params=vmem(),
        cost_estimate=cost(10),
        name="local_work",
    )(sec, table, lengths, ids, rows, moves, queries, in_hbm(pages))


def attend_new(proj_k, proj_v, refs, fresh_ref, low_ref, mixed_all, loads):
    q_ref, cos_ref, sin_ref, acc_ref, lse_ref, slot_ref, a_refs = refs
    tokens = proj_k.shape[0]
    heads = q_ref.shape[1] // HD
    keys = (proj_k * cos_ref[...] + pltpu.roll(proj_k, HD // 2, 1) * sin_ref[...]).astype(
        jnp.bfloat16
    )
    values = proj_v.astype(jnp.bfloat16)
    fresh_ref[:, :HD] = keys
    fresh_ref[:, HD:] = values
    rows = lax.broadcasted_iota(jnp.int32, (tokens, tokens), 0)
    cols = lax.broadcasted_iota(jnp.int32, (tokens, tokens), 1)
    allowed = (rows // S == cols // S) & (cols <= rows)
    for h in range(heads):
        span = slice(h * HD, (h + 1) * HD)
        scores = lax.dot_general(q_ref[:, span], keys, NT, preferred_element_type=jnp.float32)
        scores = jnp.where(allowed, scores * SCALE, BIG)
        lse = lse_ref[:, h : h + 1]
        top = jnp.maximum(jnp.max(scores, axis=1, keepdims=True), lse)
        weights = jnp.exp(scores - top)
        old = jnp.exp(lse - top)
        total = jnp.sum(weights, axis=1, keepdims=True) + old
        mixed = jnp.dot(weights.astype(jnp.bfloat16), values, preferred_element_type=jnp.float32)
        mixed_all[:, span] = ((mixed + old * acc_ref[h]) / total).astype(jnp.bfloat16)
    slots = slot_ref[...]
    half = lax.broadcasted_iota(jnp.int32, (tokens, HD), 1) // R
    folded = jnp.zeros((tokens, HD), jnp.float32)
    base = 0
    for a_ref, load in zip(a_refs, loads):
        load.wait()
        low = lax.dot_general(
            mixed_all[...], a_ref[...], NT, preferred_element_type=jnp.float32
        )
        for j in range(a_ref.shape[0] // HD):
            folded = folded + jnp.where(
                slots == base + 2 * j + half, low[:, j * HD : (j + 1) * HD], 0.0
            )
        base += a_ref.shape[0] // R
    folded = folded + pltpu.roll(folded, R, 1)
    low_ref[...] = jnp.where(
        half[: tokens // 2] == 0, folded[: tokens // 2], folded[tokens // 2 :]
    ).astype(jnp.bfloat16)


def start_loads(sources, targets, sems):
    loads = [
        pltpu.make_async_copy(source, target, sems.at[i])
        for i, (source, target) in enumerate(zip(sources, targets))
    ]
    for load in loads:
        load.start()
    return loads


def first_kernel(n_tp, n_a, sec_ref, *refs):
    h_refs, (w_ref, gain_ref) = refs[:n_tp], refs[n_tp : n_tp + 2]
    shared = refs[n_tp + 2 : n_tp + 8]
    a_refs = refs[n_tp + 8 : n_tp + 8 + n_a]
    fresh_ref, low_ref, mixed_all, *a_bufs, sems = refs[n_tp + 8 + n_a :]
    width = h_refs[0].shape[1]

    @pl.when(sec_ref[0] == 0)
    def _():
        loads = start_loads(a_refs, a_bufs, sems)
        tokens = h_refs[0].shape[0]
        proj = jnp.zeros((tokens, 2 * HD), jnp.float32)
        square = jnp.zeros((tokens, 1), jnp.float32)
        for s in range(n_tp):
            place = lax.rem(sec_ref[1] + n_tp - s, n_tp)
            lane = pl.multiple_of(place * width, width)
            row = pl.multiple_of(place * width, width)
            if s == 0:
                h = h_refs[s][...]
            else:
                h = jnp.concatenate(
                    [h_refs[s][c * HD : (c + 1) * HD, :] for c in range(width // HD)], axis=1
                )
            h = h.astype(jnp.float32)
            square = square + jnp.sum(h * h, axis=1, keepdims=True)
            x = (h * gain_ref[:, pl.ds(lane, width)].astype(jnp.float32)).astype(jnp.bfloat16)
            proj = proj + jnp.dot(
                x, w_ref[pl.ds(row, width), :], preferred_element_type=jnp.float32
            )
        proj = proj * lax.rsqrt(square / (n_tp * width) + EPS)
        attend_new(
            proj[:, :HD], proj[:, HD:], (*shared, a_bufs), fresh_ref, low_ref, mixed_all, loads
        )


def later_kernel(section, n_tp, n_a, total_width, sec_ref, *refs):
    m_refs = refs[:n_tp]
    shared = refs[n_tp : n_tp + 6]
    a_refs = refs[n_tp + 6 : n_tp + 6 + n_a]
    fresh_ref, low_ref, mixed_all, *a_bufs, sems = refs[n_tp + 6 + n_a :]

    @pl.when(sec_ref[0] == section)
    def _():
        loads = start_loads(a_refs, a_bufs, sems)
        tokens = fresh_ref.shape[0]
        proj = jnp.zeros((tokens, 2 * HD), jnp.float32)
        square = jnp.zeros((1, HD), jnp.float32)
        for m_ref in m_refs:
            proj = proj + m_ref[:tokens, :].astype(jnp.float32)
            tail = m_ref[tokens : tokens + 16, :HD].astype(jnp.float32)
            square = square + jnp.sum(tail, axis=0, keepdims=True) * 0.125
        inv = lax.rsqrt(square / total_width + EPS)
        inv = jnp.transpose(jnp.broadcast_to(inv, (tokens, HD)))
        attend_new(
            proj[:, :HD] * inv,
            proj[:, HD:] * inv,
            (*shared, a_bufs),
            fresh_ref,
            low_ref,
            mixed_all,
            loads,
        )


def attend_call(kernel, operands, a_blocks, tokens, q_width, name):
    return pl.pallas_call(
        kernel,
        in_specs=[SM] + [VM] * (len(operands) - 1) + [ANY] * len(a_blocks),
        out_specs=(VM, VM),
        out_shape=(
            sds((tokens, 2 * HD), jnp.bfloat16),
            sds((tokens // 2, HD), jnp.bfloat16),
        ),
        scratch_shapes=[
            pltpu.VMEM((tokens, q_width), jnp.bfloat16),
            *[pltpu.VMEM(a.shape, jnp.bfloat16) for a in a_blocks],
            pltpu.SemaphoreType.DMA((len(a_blocks),)),
        ],
        compiler_params=vmem(),
        cost_estimate=cost(5),
        name=name,
    )(*operands, *[in_hbm(a) for a in a_blocks])


def unfold_low(packed, slots, base, rows):
    count = packed.shape[0]
    half = lax.broadcasted_iota(jnp.int32, (count, HD), 1) // R
    turned = pltpu.roll(packed, R, 1)
    low = jnp.concatenate(
        [jnp.where(half == 0, packed, turned), jnp.where(half == 1, packed, turned)], axis=0
    )
    half = lax.broadcasted_iota(jnp.int32, (2 * count, HD), 1) // R
    return jnp.concatenate(
        [
            jnp.where(slots == base + 2 * j + half, low, 0.0).astype(jnp.bfloat16)
            for j in range(rows // HD)
        ],
        axis=1,
    )


def add_delta(low, b_refs, h, span):
    delta = None
    for b_ref, spread in zip(b_refs, low):
        part = jnp.dot(spread, b_ref[:, span], preferred_element_type=jnp.float32)
        delta = part if delta is None else delta + part
    delta = delta.astype(jnp.bfloat16).astype(jnp.float32)
    return (h.astype(jnp.float32) + delta).astype(jnp.bfloat16)


def spreads(packed, slots, b_refs):
    out = []
    base = 0
    for b_ref in b_refs:
        out.append(unfold_low(packed, slots, base, b_ref.shape[0]))
        base += b_ref.shape[0] // R
    return out


def slice_kernel(section, n_tp, n_b, sec_ref, *refs):
    low_refs = refs[:n_tp]
    slot_ref, gain_ref, w_ref, h_ref = refs[n_tp : n_tp + 4]
    b_refs = refs[n_tp + 4 : n_tp + 4 + n_b]
    rest = refs[n_tp + 4 + n_b :]
    h_out, m_refs = rest[0], rest[1 : 1 + n_tp]
    x_all, h_buf = rest[1 + n_tp : 3 + n_tp]
    b_bufs = rest[3 + n_tp : 3 + n_tp + n_b]
    sems = rest[3 + n_tp + n_b]
    tokens, width = h_buf.shape
    part = width // 4

    @pl.when(sec_ref[0] == section)
    def _():
        loads = [pltpu.make_async_copy(h_ref, h_buf, sems.at[0])]
        for i in range(n_b):
            loads.append(pltpu.make_async_copy(b_refs[i], b_bufs[i], sems.at[1 + i]))
        for load in loads:
            load.start()
        packed = low_refs[0][...].astype(jnp.float32)
        for low_ref in low_refs[1:]:
            packed = packed + low_ref[...].astype(jnp.float32)
        rounded = packed.astype(jnp.bfloat16)
        low = spreads(rounded.astype(jnp.float32), slot_ref[...], b_refs)
        for load in loads:
            load.wait()
        square = jnp.zeros((tokens, 1), jnp.float32)
        for c in range(4):
            span = slice(c * part, (c + 1) * part)
            h = add_delta(low, b_bufs, h_buf[:, span], span)
            h_buf[:, span] = h
            h = h.astype(jnp.float32)
            square = square + jnp.sum(h * h, axis=1, keepdims=True)
            lane = pl.multiple_of(sec_ref[1] * width + c * part, part)
            gain = gain_ref[:, pl.ds(lane, part)].astype(jnp.float32)
            x_all[:, span] = (h * gain).astype(jnp.bfloat16)
        store = pltpu.make_async_copy(h_buf, h_out, sems.at[0])
        store.start()
        square = jnp.transpose(jnp.broadcast_to(square, (tokens, HD)))[:16]
        high = square.astype(jnp.bfloat16).astype(jnp.float32)
        upper = lax.broadcasted_iota(jnp.int32, (16, HD), 0) < 8
        tail = jnp.where(upper, high, square - high).astype(jnp.bfloat16)
        for s in range(n_tp):
            rows = pl.ds(s * width, width)
            proj = jnp.dot(x_all[...], w_ref[rows, :], preferred_element_type=jnp.float32)
            m_refs[s][:tokens, :] = proj.astype(jnp.bfloat16)
            m_refs[s][tokens:, :HD] = tail
            m_refs[s][tokens:, HD:] = jnp.zeros_like(tail)
        store.wait()


def section_slice(section, n_tp, sec, lows, slots, gain, h_prev, weights, b_blocks):
    tokens, width = h_prev.shape
    operands = [sec, *lows, slots, gain, weights, *[in_hbm(x) for x in (h_prev, *b_blocks)]]
    return pl.pallas_call(
        functools.partial(slice_kernel, section, n_tp, len(b_blocks)),
        in_specs=[SM] + [VM] * (n_tp + 3) + [ANY] * (1 + len(b_blocks)),
        out_specs=(ANY,) + (VM,) * n_tp,
        out_shape=(
            sds((tokens, width), jnp.bfloat16),
            *[sds((tokens + 16, 2 * HD), jnp.bfloat16)] * n_tp,
        ),
        scratch_shapes=[
            pltpu.VMEM((tokens, width), jnp.bfloat16),
            pltpu.VMEM((tokens, width), jnp.bfloat16),
            *[pltpu.VMEM(b.shape, jnp.bfloat16) for b in b_blocks],
            pltpu.SemaphoreType.DMA((1 + len(b_blocks),)),
        ],
        compiler_params=vmem(),
        cost_estimate=cost(5),
        name="section_slice_%d" % section,
    )(*operands)


def result_kernel(last, n_tp, n_b, sec_ref, back_ref, *refs):
    low_refs = refs[:n_tp]
    slot_ref, h_ref = refs[n_tp : n_tp + 2]
    b_refs = refs[n_tp + 2 : n_tp + 2 + n_b]
    out_ref = refs[n_tp + 2 + n_b]

    @pl.when(sec_ref[0] != last)
    def _():
        out_ref[0] = back_ref[...]

    @pl.when(sec_ref[0] == last)
    def _():
        packed = low_refs[0][...].astype(jnp.float32)
        for low_ref in low_refs[1:]:
            packed = packed + low_ref[...].astype(jnp.float32)
        rounded = packed.astype(jnp.bfloat16).astype(jnp.float32)
        slots = slot_ref[...]
        low = spreads(rounded, slots, b_refs)
        part = h_ref.shape[1] // 4
        for c in range(4):
            span = slice(c * part, (c + 1) * part)
            out_ref[0, :, span] = add_delta(low, b_refs, h_ref[:, span], span)


def section_result(last, n_tp, sec, back, lows, slots, held, b_blocks):
    operands = [sec, back, *lows, slots, held, *b_blocks]
    return pl.pallas_call(
        functools.partial(result_kernel, last, n_tp, len(b_blocks)),
        in_specs=[SM] + [VM] * (len(operands) - 1),
        out_specs=VM,
        out_shape=sds((1, *held.shape), jnp.bfloat16),
        compiler_params=vmem(),
        cost_estimate=cost(3),
        name="section_result",
    )(*operands)


def insert_kernel(spot_ref, new_ref, old_ref, out_ref):
    count = old_ref.shape[0]
    tokens = new_ref.shape[0]
    rows = lax.broadcasted_iota(jnp.int32, (PAGE, tokens), 0)

    def insert(i, _):
        spot = spot_ref[pl.ds(i, 1), :]
        hit = jnp.where(spot == rows, 1.0, 0.0)
        fresh = jnp.sum(hit, axis=1, keepdims=True) > 0.0
        hit = hit.astype(jnp.bfloat16)
        values = jnp.dot(hit, new_ref[...], preferred_element_type=jnp.float32)
        for part in range(2):
            value = values[:, part * HD : (part + 1) * HD]
            old = old_ref[i, part].astype(jnp.float32)
            out_ref[0, i, part] = jnp.where(fresh, value, old).astype(jnp.bfloat16)
        return 0

    lax.fori_loop(0, count, insert, 0, unroll=4)


def insert_new(spots, fresh, old):
    return pl.pallas_call(
        insert_kernel,
        in_specs=[VM] * 3,
        out_specs=VM,
        out_shape=sds((1, *old.shape), jnp.bfloat16),
        compiler_params=vmem(),
        cost_estimate=cost(3),
        name="insert_new",
    )(spots, fresh, old)


def body(
    hidden,
    queries,
    norm_gain,
    kv_weight,
    adapter_in,
    adapter_out,
    kv_pages,
    adapter_ids,
    owner_rows,
    page_table,
    lengths,
    moves,
):
    n_sec, n_req, n_tp = (lax.axis_size(a) for a in ("pipe", "req", "tp"))
    section, my_req, my_tp = (lax.axis_index(a) for a in ("pipe", "req", "tp"))
    tokens, width = hidden.shape
    depth = width * n_tp
    adapters = adapter_in.shape[1]
    q_width = queries.shape[2]

    def around(x, shift):
        return lax.ppermute(x, "tp", [(t, (t + shift) % n_tp) for t in range(n_tp)])

    def onward(x, shift, step=1, sections=range(n_sec)):
        pairs = [
            (l * n_tp + t, (l + step) % n_sec * n_tp + (t + shift) % n_tp)
            for l in sections
            for t in range(n_tp)
        ]
        return lax.ppermute(x, ("pipe", "tp"), pairs)

    def partner(x, sections=range(n_sec), step=0):
        pairs = [
            (l * n_req + i, (l + step) % n_sec * n_req + (i ^ 1))
            for l in sections
            for i in range(n_req)
        ]
        return lax.ppermute(x, ("pipe", "req"), pairs)

    def gather(x):
        return [x, partner(x)] if paired else [lax.all_gather(x, "req", axis=0, tiled=True)]

    def after(x, *others):
        return lax.optimization_barrier((x, *others))[0]

    paired = n_req == 2
    later = list(range(1, n_sec))
    sec = jnp.stack([section, my_tp, my_req % 2, my_req]).astype(jnp.int32)

    a_own = adapter_in[0].reshape(adapters * R, q_width)
    b_own = adapter_out[0].reshape(adapters * R, width)
    raw = kv_weight[0].reshape(2 * depth, HD)
    half = width // 2
    final = n_sec - 1
    sent = parcels(sec, hidden, raw, n_tp)
    mine = [around(sent[s - 1], s) for s in range(1, n_tp)]
    a_blocks = gather(a_own)
    acc, lse, slots, cos, sin, leaving, spots = local_work(
        paired,
        adapters,
        sec,
        page_table.reshape(-1),
        lengths,
        adapter_ids,
        owner_rows,
        moves.reshape(-1),
        queries[0],
        kv_pages[0],
    )
    if paired:
        spots = partner(spots)
        ready = after(b_own, lse)
        own_before = onward(ready, 0)
        early = partner(ready, [0], 1)
    else:
        b_blocks = [lax.all_gather(b_own, "req", axis=0, tiled=True)]
        before = [onward(b_blocks[0], 0)]
    chunks = [(0, lambda sec, i=i: i, lambda sec, i=i: i) for i in range(2 * n_tp)]
    weights = split_parts(
        sec,
        [after(raw, lse, *a_blocks)],
        chunks,
        lambda section: section == 0,
        half,
        "split_first",
    )
    other = [partner(after(m, lse), later) for m in mine]

    shared = [queries[0], cos, sin, acc, lse, slots]
    n_a = len(a_blocks)
    fresh, low = attend_call(
        functools.partial(first_kernel, n_tp, n_a),
        [sec, hidden, *mine, weights, norm_gain, *shared],
        a_blocks,
        tokens,
        q_width,
        "first_section",
    )
    chunks = [(0, lambda sec, i=i: 2 * sec[1] + i, lambda sec, i=i: i) for i in range(2)]
    for s in range(1, n_tp):
        chunks.append((s, lambda sec: 0, lambda sec, s=s: 2 * s + sec[2]))
    for s in range(1, n_tp):
        chunks.append((n_tp - 1 + s, lambda sec: 0, lambda sec, s=s: 2 * s + 1 - sec[2]))
    own_rows = split_parts(
        sec,
        [after(raw, low), *mine, *other],
        chunks,
        lambda section: section > 0,
        half,
        "split_later",
    )
    h_prev = h_new = hidden
    hs, news = [hidden], [fresh]
    for l in later:
        lows = [onward(low, s, 1, [0] if l == 1 else range(n_sec)) for s in range(n_tp)]
        if l == 1 and paired:
            late = partner(after(b_own, lows[0]), later[:-1], 1)
        if l == 2 and paired:
            b_blocks = [b_own, partner(after(b_own, low), [final])]
            leaving = partner(after(leaving, low))
        if paired:
            before = [own_before, early if l == 1 else late]
        h_new, *parts = section_slice(
            l, n_tp, sec, lows, slots, norm_gain, h_prev, own_rows, before
        )
        hs.append(h_new)
        parts = [parts[0]] + [around(parts[s], -s) for s in range(1, n_tp)]
        if l < final:
            h_prev = onward(after(h_new, *parts[1:]), 0)
        else:
            back = h_new
            for m in later[:-1]:
                back = jnp.where(section == m, hs[m], back)
            back = onward(after(back, *parts[1:]), 0, -1)
        fresh, low = attend_call(
            functools.partial(later_kernel, l, n_tp, n_a, depth),
            [sec, *parts, *shared],
            a_blocks,
            tokens,
            q_width,
            "section_%d" % l,
        )
        news.append(fresh)
    lows = [low] + [around(low, s) for s in range(1, n_tp)]
    fresh = news[0]
    for l in later:
        fresh = jnp.where(section == l, news[l], fresh)
    if paired:
        arrived = insert_new(spots, partner(fresh), leaving)
    else:
        leaving = insert_new(spots, fresh, leaving)[0]
        count = moves.shape[0]
        free_slots = (n_req - 1) * ((count + n_req - 2) // (n_req - 1))
        received, dest_in, spots_in = (
            lax.all_gather(x, "req", axis=0, tiled=True)
            for x in (leaving, moves[:, 0], moves[:, 2])
        )
        target = jnp.where(dest_in == my_req, spots_in, free_slots)
        empty = jnp.zeros((free_slots, *leaving.shape[1:]), jnp.bfloat16)
        arrived = empty.at[target].set(received, mode="drop")[None]
    section_out = section_result(final, n_tp, sec, back, lows, slots, h_new, b_blocks)
    return (section_out, fresh.reshape(1, tokens, 2, HD), arrived)


def solution(mesh):
    in_specs = (
        P("req", "tp"),
        P("pipe", "req", "tp"),
        P("pipe", None),
        P("pipe", None, None, "tp"),
        P("pipe", "req", None, "tp"),
        P("pipe", "req", None, "tp"),
        P("pipe", "req", None, None, "tp"),
        P("req"),
        P(),
        P("req", None),
        P("req"),
        P("req", None),
    )
    out_specs = (
        P("pipe", "req", "tp"),
        P("pipe", "req", None, "tp"),
        P("pipe", "req", None, None, "tp"),
    )
    return jax.shard_map(body, mesh=mesh, in_specs=in_specs, out_specs=out_specs, check_vma=False)
```

time: 239 us -> 184 us (0.77)
  the two profiles are of different devices: /device:TPU:13 before, /device:TPU:0 now
where the time goes in v2:
time: 184 us; the launch traced here: 182 us
  starting transfers between devices  79.5 us (43%)
  waiting for transfers between devices  50.4 us (27%)
  Pallas kernels  27.6 us (15%)
  local copies, waits for them, and re-layouts  21.6 us (12%)
  other arithmetic  1.89 us (1%)
    ppermute x16, starting transfers between devices, onward(): return lax.ppermute(x, ('pipe', 'tp'), pairs)  47.5 us
    ppermute x15, waiting for transfers between devices, around(): return lax.ppermute(x, 'tp', [(t, (t + shift) % n_tp) for t in range(n_tp)])  39.4 us
    unnamed x94, local copies, waits for them, and re-layouts  20.7 us
    ppermute x15, starting transfers between devices, around(): return lax.ppermute(x, 'tp', [(t, (t + shift) % n_tp) for t in range(n_tp)])  20 us
    ppermute x10, starting transfers between devices, partner(): return lax.ppermute(x, ('pipe', 'req'), pairs)  12 us
    ppermute x16, waiting for transfers between devices, onward(): return lax.ppermute(x, ('pipe', 'tp'), pairs)  8.65 us
    pallas_call x4, Pallas kernels, attend_call(): pl.pallas_call(kernel, in_specs=[SM] + [VM] * (len(operands) - 1) + [ANY]...  8.63 us
    pallas_call x1, Pallas kernels, local_work(): pl.pallas_call(functools.partial(local_kernel, paired, adapters), in_spec...  6.98 us
  transfers between devices with their start and end apart: 41, of which 17 were waited for; matrix products, arithmetic and copies ran while one was open for 2% of the time, Pallas kernels for 13%

profile of v2, /device:TPU:0, one launch (start us, length us, event | category | flops | bytes accessed | tf_op | source)
XLA Modules:
  0.0 182.1 jit_solution(8108998589253320820)
XLA Ops:
  0.7 1.0 copy-done.3
  1.8 2.0 %parcels.1 = (bf16[2048,128]{1,0:T(8,128)(2,1)}, bf16[2048,128]{1,0:T(8,128)(2,1)}, bf16[2048,128]{1,0:T(8,128)(2,1)}) custom-call(s32[4]{0:T(128)S(1)} %pad_add_fusion.sec_ref, bf16[128,2048]{1,0:T(8,128)(2,1)S(1)} %copy-done.3, bf16[16384,128]{1,0:T(8,128)(2,1)} %bitcast.19), custom_call_target="tpu_custom_call" | custom-call | bytes 6000000 | tf_op jit(solution)/shard_map/parcels/pallas_call | solution.py:121
  3.8 5.1 %collective-permute-start.2 = (bf16[2048,128]{1,0:T(8,128)(2,1)}, bf16[2048,128]{1,0:T(8,128)(2,1)S(1)}, u32[]{:S(2)}, u32[]{:S(2)}) collective-permute-start(bf16[2048,128]{1,0:T(8,128)(2,1)} %get-tuple-element.50), channel_id=1, source_target_pairs={{0,3},{1,0},{2,1},{3,2},{4,7},{5,4},{6,5},{7,6},{8,11},{9,8},{10,9... | collective-permute-start | bytes 1572872 | tf_op jit(solution)/shard_map/ppermute | solution.py:622
  8.9 1.5 collective-permute-start.3
  10.4 1.0 collective-permute-start.1
  13.1 7.0 %local_work.1 = (f32[8,128,128]{2,1,0:T(8,128)S(1)}, f32[128,128]{1,0:T(8,128)S(1)}, s32[128,128]{1,0:T(8,128)S(1)}, f32[128,128]{1,0:T(8,128)S(1)}, f32[128,128...) custom-call(s32[4]{0:T(128)S(1)} %pad_add_fusion.sec_ref, s32[128]{0:T(128)S(1)} %reshape.15.table_ref, ...), custom_call_target="tpu_custom_call" | custom-call | bytes 30000000 | tf_op jit(solution)/shard_map/local_work/pallas_call | solution.py:259
  21.6 4.8 %collective-permute-start.12 = (bf16[256,2048]{1,0:T(8,128)(2,1)S(1)}, bf16[256,2048]{1,0:T(8,128)(2,1)S(1)}, u32[]{:S(2)}, u32[]{:S(2)}) collective-permute-start(bf16[256,2048]{1,0:T(8,128)(2,1)S(1)} %bitcast.15), channel_id=1, source_target_pairs={{0,12},{4,8},{1,13},{5,9},{2,14},{6,10},{3,15},{7,11}} | collective-permute-start | bytes 3145736 | tf_op jit(solution)/shard_map/ppermute | solution.py:638
  27.2 2.9 %split_first.1.refs_4_ = bf16[8192,256]{1,0:T(8,128)(2,1)S(1)} custom-call(s32[4]{0:T(128)S(1)} %pad_add_fusion.sec_ref, bf16[16384,128]{1,0:T(8,128)(2,1)} %bitcast.20), custom_call_target="tpu_custom_call" | custom-call | bytes 15000000 | tf_op jit(solution)/shard_map/split_first/pallas_call | solution.py:74
  30.1 3.6 %collective-permute-done.refs_1_ = bf16[2048,128]{1,0:T(8,128)(2,1)S(1)} collective-permute-done((bf16[2048,128]{1,0:T(8,128)(2,1)}, bf16[2048,128]{1,0:T(8,128)(2,1)S(1)}, u32[]{:S(2)}, u32[]{:S(2)}) %collective-permute-start) | collective-permute-done | bytes 524320 | tf_op jit(solution)/shard_map/ppermute | solution.py:622
  33.6 21.3 %collective-permute-done.1.refs_2_ = bf16[2048,128]{1,0:T(8,128)(2,1)S(1)} collective-permute-done((bf16[2048,128]{1,0:T(8,128)(2,1)}, bf16[2048,128]{1,0:T(8,128)(2,1)S(1)}, u32[]{:S(2)}, u32[]{:S(2)}) %collective-permute-start.1) | collective-permute-done | bytes 524320 | tf_op jit(solution)/shard_map/ppermute | solution.py:622
  55.0 5.6 %first_section.1 = (bf16[128,256]{1,0:T(8,128)(2,1)S(1)}, bf16[64,128]{1,0:T(8,128)(2,1)S(1)}) custom-call(s32[4]{0:T(128)S(1)} %pad_add_fusion.sec_ref, bf16[128,2048]{1,0:T(8,128)(2,1)S(1)} %copy-done.4, bf16[2048,128]{1,0:T(8,128)(2,1)S(1)} %collective-permute-done.refs_1_, bf16[2048,128]{1,0:T(8,128)(2,1)S(1)} %collective-permute-done.1.refs_2_, ...), custom_call_target="tpu_custom_call" | custom-call | bytes 15000000 | tf_op jit(solution)/shard_map/first_section/pallas_call | solution.py:403
  60.6 1.3 collective-permute-start.4
  61.9 1.3 collective-permute-start.5
  66.1 8.0 %collective-permute-start.6 = (bf16[64,128]{1,0:T(8,128)(2,1)S(1)}, bf16[64,128]{1,0:T(8,128)(2,1)S(1)}, u32[]{:S(2)}, u32[]{:S(2)}) collective-permute-start(bf16[64,128]{1,0:T(8,128)(2,1)S(1)} %get-tuple-element.57), channel_id=1, source_target_pairs={{0,10},{1,11},{2,8},{3,9},{4,14},{5,15},{6,12},{7,13}} | collective-permute-start | bytes 49160 | tf_op jit(solution)/shard_map/ppermute | solution.py:630
  74.1 9.8 %collective-permute-start.7 = (bf16[64,128]{1,0:T(8,128)(2,1)S(1)}, bf16[64,128]{1,0:T(8,128)(2,1)S(1)}, u32[]{:S(2)}, u32[]{:S(2)}) collective-permute-start(bf16[64,128]{1,0:T(8,128)(2,1)S(1)} %get-tuple-element.57), channel_id=1, source_target_pairs={{0,11},{1,8},{2,9},{3,10},{4,15},{5,12},{6,13},{7,14}} | collective-permute-start | bytes 49160 | tf_op jit(solution)/shard_map/ppermute | solution.py:630
  85.4 1.4 copy-done.37
  86.8 1.0 copy-done.39
  88.5 1.9 %collective-permute-start.15 = (bf16[144,256]{1,0:T(8,128)(2,1)S(1)}, bf16[144,256]{1,0:T(8,128)(2,1)S(1)}, u32[]{:S(2)}, u32[]{:S(2)}) collective-permute-start(bf16[144,256]{1,0:T(8,128)(2,1)S(1)} %get-tuple-element.66), channel_id=1, source_target_pairs={{0,1},{1,2},{2,3},{3,0},{4,5},{5,6},{6,7},{7,4},{8,9},{9,10},{10,1... | collective-permute-start | bytes 221192 | tf_op jit(solution)/shard_map/ppermute | solution.py:622
  90.5 3.2 %collective-permute-done.13.refs_1_ = bf16[144,256]{1,0:T(8,128)(2,1)S(1)} collective-permute-done((bf16[144,256]{1,0:T(8,128)(2,1)S(1)}, bf16[144,256]{1,0:T(8,128)(2,1)S(1)}, u32[]{:S(2)}, u32[]{:S(2)}) %collective-permute-start.13) | collective-permute-done | bytes 73760 | tf_op jit(solution)/shard_map/ppermute | solution.py:622
  93.7 2.5 %collective-permute-done.14.refs_2_ = bf16[144,256]{1,0:T(8,128)(2,1)S(1)} collective-permute-done((bf16[144,256]{1,0:T(8,128)(2,1)S(1)}, bf16[144,256]{1,0:T(8,128)(2,1)S(1)}, u32[]{:S(2)}, u32[]{:S(2)}) %collective-permute-start.14) | collective-permute-done | bytes 73760 | tf_op jit(solution)/shard_map/ppermute | solution.py:622
  96.1 3.6 %collective-permute-start.20 = (bf16[128,2048]{1,0:T(8,128)(2,1)S(1)}, bf16[128,2048]{1,0:T(8,128)(2,1)S(1)}, u32[]{:S(2)}, u32[]{:S(2)}) collective-permute-start(bf16[128,2048]{1,0:T(8,128)(2,1)S(1)} %get-tuple-element.69), channel_id=1, source_target_pairs={{0,8},{1,9},{2,10},{3,11},{8,16},{9,17},{10,18},{11,19},{16,24},{1... | collective-permute-start | bytes 1572872 | tf_op jit(solution)/shard_map/ppermute | solution.py:630
  101.1 6.1 %collective-permute-start.16 = (bf16[64,128]{1,0:T(8,128)(2,1)S(1)}, bf16[64,128]{1,0:T(8,128)(2,1)S(1)}, u32[]{:S(2)}, u32[]{:S(2)}) collective-permute-start(bf16[64,128]{1,0:T(8,128)(2,1)S(1)} %get-tuple-element.67), channel_id=1, source_target_pairs={{0,8},{1,9},{2,10},{3,11},{8,16},{9,17},{10,18},{11,19},{16,24},{1... | collective-permute-start | bytes 49160 | tf_op jit(solution)/shard_map/ppermute | solution.py:630
  107.2 1.0 collective-permute-start.18
  108.2 1.3 collective-permute-start.19
  109.5 3.6 %collective-permute-done.17.refs_1_ = bf16[64,128]{1,0:T(8,128)(2,1)S(1)} collective-permute-done((bf16[64,128]{1,0:T(8,128)(2,1)S(1)}, bf16[64,128]{1,0:T(8,128)(2,1)S(1)}, u32[]{:S(2)}, u32[]{:S(2)}) %collective-permute-start.17) | collective-permute-done | bytes 16416 | tf_op jit(solution)/shard_map/ppermute | solution.py:630
  113.3 0.9 copy-done.38
  115.6 3.3 %collective-permute-start.22 = (bf16[144,256]{1,0:T(8,128)(2,1)S(1)}, bf16[144,256]{1,0:T(8,128)(2,1)S(1)}, u32[]{:S(2)}, u32[]{:S(2)}) collective-permute-start(bf16[144,256]{1,0:T(8,128)(2,1)S(1)} %get-tuple-element.73), channel_id=1, source_target_pairs={{0,3},{1,0},{2,1},{3,2},{4,7},{5,4},{6,5},{7,6},{8,11},{9,8},{10,9... | collective-permute-start | bytes 221192 | tf_op jit(solution)/shard_map/ppermute | solution.py:622
  119.6 1.3 collective-permute-done.22.refs_1_
  120.9 3.3 %collective-permute-done.23.refs_2_ = bf16[144,256]{1,0:T(8,128)(2,1)S(1)} collective-permute-done((bf16[144,256]{1,0:T(8,128)(2,1)S(1)}, bf16[144,256]{1,0:T(8,128)(2,1)S(1)}, u32[]{:S(2)}, u32[]{:S(2)}) %collective-permute-start.23) | collective-permute-done | bytes 73760 | tf_op jit(solution)/shard_map/ppermute | solution.py:622
  125.1 1.2 section_2.1
  126.9 5.2 %collective-permute-start.25 = (bf16[64,128]{1,0:T(8,128)(2,1)}, bf16[64,128]{1,0:T(8,128)(2,1)S(1)}, u32[]{:S(2)}, u32[]{:S(2)}) collective-permute-start(bf16[64,128]{1,0:T(8,128)(2,1)} %get-tuple-element.76), channel_id=1, source_target_pairs={{0,8},{1,9},{2,10},{3,11},{8,16},{9,17},{10,18},{11,19},{16,24},{1... | collective-permute-start | bytes 49160 | tf_op jit(solution)/shard_map/ppermute | solution.py:630
  132.9 3.4 %collective-permute-start.26 = (bf16[64,128]{1,0:T(8,128)(2,1)}, bf16[64,128]{1,0:T(8,128)(2,1)}, u32[]{:S(2)}, u32[]{:S(2)}) collective-permute-start(bf16[64,128]{1,0:T(8,128)(2,1)} %get-tuple-element.76), channel_id=1, source_target_pairs={{0,9},{1,10},{2,11},{3,8},{8,17},{9,18},{10,19},{11,16},{16,25},{1... | collective-permute-start | bytes 49160 | tf_op jit(solution)/shard_map/ppermute | solution.py:630
  136.2 1.4 collective-permute-start.27
  138.2 2.1 %collective-permute-start.28 = (bf16[64,128]{1,0:T(8,128)(2,1)}, bf16[64,128]{1,0:T(8,128)(2,1)}, u32[]{:S(2)}, u32[]{:S(2)}) collective-permute-start(bf16[64,128]{1,0:T(8,128)(2,1)} %get-tuple-element.76), channel_id=1, source_target_pairs={{0,11},{1,8},{2,9},{3,10},{8,19},{9,16},{10,17},{11,18},{16,27},{1... | collective-permute-start | bytes 49160 | tf_op jit(solution)/shard_map/ppermute | solution.py:630
  140.4 1.1 collective-permute-done.27.refs_2_
  141.5 2.3 %collective-permute-done.28.refs_3_ = bf16[64,128]{1,0:T(8,128)(2,1)} collective-permute-done((bf16[64,128]{1,0:T(8,128)(2,1)}, bf16[64,128]{1,0:T(8,128)(2,1)}, u32[]{:S(2)}, u32[]{:S(2)}) %collective-permute-start.28) | collective-permute-done | bytes 16416 | tf_op jit(solution)/shard_map/ppermute | solution.py:630
  143.8 2.2 %copy-done.1 = bf16[8192,256]{1,0:T(8,128)(2,1)S(1)} copy-done((bf16[8192,256]{1,0:T(8,128)(2,1)S(1)}, bf16[8192,256]{1,0:T(8,128)(2,1)}, u32[]{:S(2)}) %copy-start.1) | copy-done | bytes 4194328
  148.3 3.3 %collective-permute-start.30 = (bf16[144,256]{1,0:T(8,128)(2,1)S(1)}, bf16[144,256]{1,0:T(8,128)(2,1)S(1)}, u32[]{:S(2)}, u32[]{:S(2)}) collective-permute-start(bf16[144,256]{1,0:T(8,128)(2,1)S(1)} %get-tuple-element.79), channel_id=1, source_target_pairs={{0,3},{1,0},{2,1},{3,2},{4,7},{5,4},{6,5},{7,6},{8,11},{9,8},{10,9... | collective-permute-start | bytes 221192 | tf_op jit(solution)/shard_map/ppermute | solution.py:622
  152.3 0.9 select_select_fusion
  154.5 2.5 %collective-permute-done.31.refs_2_ = bf16[144,256]{1,0:T(8,128)(2,1)S(1)} collective-permute-done((bf16[144,256]{1,0:T(8,128)(2,1)S(1)}, bf16[144,256]{1,0:T(8,128)(2,1)S(1)}, u32[]{:S(2)}, u32[]{:S(2)}) %collective-permute-start.31) | collective-permute-done | bytes 73760 | tf_op jit(solution)/shard_map/ppermute | solution.py:622
  158.4 2.9 %collective-permute-start.33 = (bf16[128,2048]{1,0:T(8,128)(2,1)}, bf16[128,2048]{1,0:T(8,128)(2,1)}, u32[]{:S(2)}, u32[]{:S(2)}) collective-permute-start(bf16[128,2048]{1,0:T(8,128)(2,1)} %select_select_fusion), channel_id=1, source_target_pairs={{0,24},{1,25},{2,26},{3,27},{8,0},{9,1},{10,2},{11,3},{16,8},{17,9... | collective-permute-start | bytes 1572872 | tf_op jit(solution)/shard_map/ppermute | solution.py:630
  166.6 1.2 section_3.1
  169.0 1.7 collective-permute-start.38
  170.7 2.3 %collective-permute-done.38.spot_ref = s32[16,128]{1,0:T(8,128)S(1)} collective-permute-done((s32[16,128]{1,0:T(8,128)S(1)}, s32[16,128]{1,0:T(8,128)S(1)}, u32[]{:S(2)}, u32[]{:S(2)}) %collective-permute-start.38) | collective-permute-done | bytes 8224 | tf_op jit(solution)/shard_map/ppermute | solution.py:638
  173.1 1.9 %collective-permute-start.35 = (bf16[64,128]{1,0:T(8,128)(2,1)}, bf16[64,128]{1,0:T(8,128)(2,1)S(1)}, u32[]{:S(2)}, u32[]{:S(2)}) collective-permute-start(bf16[64,128]{1,0:T(8,128)(2,1)} %get-tuple-element.84.refs_0_), channel_id=1, source_target_pairs={{0,2},{1,3},{2,0},{3,1},{4,6},{5,7},{6,4},{7,5},{8,10},{9,11},{10,... | collective-permute-start | bytes 49160 | tf_op jit(solution)/shard_map/ppermute | solution.py:622
  175.0 2.0 %collective-permute-start.36 = (bf16[64,128]{1,0:T(8,128)(2,1)}, bf16[64,128]{1,0:T(8,128)(2,1)S(1)}, u32[]{:S(2)}, u32[]{:S(2)}) collective-permute-start(bf16[64,128]{1,0:T(8,128)(2,1)} %get-tuple-element.84.refs_0_), channel_id=1, source_target_pairs={{0,3},{1,0},{2,1},{3,2},{4,7},{5,4},{6,5},{7,6},{8,11},{9,8},{10,9... | collective-permute-start | bytes 49160 | tf_op jit(solution)/shard_map/ppermute | solution.py:622
  177.6 2.5 %insert_new.1 = bf16[1,16,2,64,128]{4,3,2,1,0:T(8,128)(2,1)} custom-call(s32[16,128]{1,0:T(8,128)S(1)} %collective-permute-done.38.spot_ref, bf16[128,256]{1,0:T(8,128)(2,1)S(1)} %collective-permute-done.39.new_ref, bf16[16,2,64,128]{3,2,1,0:T(8,128)(2,1)} %collective-permute-done.40.old_ref), custom_call_target="tpu_custom_call" | custom-call | bytes 9000000 | tf_op jit(solution)/shard_map/insert_new/pallas_call | solution.py:589
  180.2 1.9 %section_result.1 = bf16[1,128,2048]{2,1,0:T(8,128)(2,1)} custom-call(s32[4]{0:T(128)S(1)} %pad_add_fusion.sec_ref, bf16[128,2048]{1,0:T(8,128)(2,1)} %collective-permute-done.33.back_ref, bf16[64,128]{1,0:T(8,128)(2,1)} %get-tuple-element.84.refs_0_, bf16[64,128]{1,0:T(8,128)(2,1)S(1)} %collective-permute-done.34.refs_1_, ...), custom_call_target="tpu_custom_call" | custom-call | bytes 9000000 | tf_op jit(solution)/shard_map/section_result/pallas_call | solution.py:557
  (147 shorter events, 28.2 us)
Async XLA Ops:
  3.8 17.8 %collective-permute-start.2 = (bf16[2048,128]{1,0:T(8,128)(2,1)}, bf16[2048,128]{1,0:T(8,128)(2,1)S(1)}, u32[]{:S(2)}, u32[]{:S(2)}) collective-permute-start(bf16[2048,128]{1,0:T(8,128)(2,1)} %get-tuple-element.50), channel_id=1, source_target_pairs={{0,3},{1,0},{2,1},{3,2},{4,7},{5,4},{6,5},{7,6},{8,11},{9,8},{10,9... | collective-permute-start | bytes 1572872 | tf_op jit(solution)/shard_map/ppermute | solution.py:622
  8.9 17.6 %collective-permute-start.3 = (bf16[256,1024]{1,0:T(8,128)(2,1)}, bf16[256,1024]{1,0:T(8,128)(2,1)}, u32[]{:S(2)}, u32[]{:S(2)}) collective-permute-start(bf16[256,1024]{1,0:T(8,128)(2,1)} %bitcast.7.refs_12_.refs_10_), channel_id=1, source_target_pairs={{0,4},{4,0},{8,12},{12,8},{16,20},{20,16},{24,28},{28,24},{1,5},{5... | collective-permute-start | bytes 1572872 | tf_op jit(solution)/shard_map/ppermute | solution.py:638
  10.4 23.3 %collective-permute-start = (bf16[2048,128]{1,0:T(8,128)(2,1)}, bf16[2048,128]{1,0:T(8,128)(2,1)S(1)}, u32[]{:S(2)}, u32[]{:S(2)}) collective-permute-start(bf16[2048,128]{1,0:T(8,128)(2,1)} %get-tuple-element.48), channel_id=1, source_target_pairs={{0,1},{1,2},{2,3},{3,0},{4,5},{5,6},{6,7},{7,4},{8,9},{9,10},{10,1... | collective-permute-start | bytes 1572872 | tf_op jit(solution)/shard_map/ppermute | solution.py:622
  10.4 44.6 %collective-permute-start.1 = (bf16[2048,128]{1,0:T(8,128)(2,1)}, bf16[2048,128]{1,0:T(8,128)(2,1)S(1)}, u32[]{:S(2)}, u32[]{:S(2)}) collective-permute-start(bf16[2048,128]{1,0:T(8,128)(2,1)} %get-tuple-element.49), channel_id=1, source_target_pairs={{0,2},{1,3},{2,0},{3,1},{4,6},{5,7},{6,4},{7,5},{8,10},{9,11},{10,... | collective-permute-start | bytes 1572872 | tf_op jit(solution)/shard_map/ppermute | solution.py:622
  21.5 103.6 %copy-start.9 = (f32[128,128]{1,0:T(8,128)}, f32[128,128]{1,0:T(8,128)S(1)}, u32[]{:S(2)}) copy-start(f32[128,128]{1,0:T(8,128)S(1)} %get-tuple-element.53.refs_7_.refs_5_) | copy-start | bytes 196612
  21.5 103.6 %copy-start.11 = (f32[128,128]{1,0:T(8,128)}, f32[128,128]{1,0:T(8,128)S(1)}, u32[]{:S(2)}) copy-start(f32[128,128]{1,0:T(8,128)S(1)} %get-tuple-element.54.refs_8_.refs_6_) | copy-start | bytes 196612
  21.5 33.5 %copy-start.4 = (bf16[128,2048]{1,0:T(8,128)(2,1)S(1)}, bf16[128,2048]{1,0:T(8,128)(2,1)}, u32[]{:S(2)}) copy-start(bf16[128,2048]{1,0:T(8,128)(2,1)} %refs_7_.1) | copy-start | bytes 1572868
  21.5 33.5 %copy-start.13 = (bf16[1,8192]{1,0:T(2,128)(2,1)S(1)}, bf16[1,8192]{1,0:T(2,128)(2,1)}, u32[]{:S(2)}) copy-start(bf16[1,8192]{1,0:T(2,128)(2,1)} %refs_5_.7) | copy-start | bytes 49156
  21.5 63.9 %collective-permute-start.11 = (bf16[256,2048]{1,0:T(8,128)(2,1)S(1)}, bf16[256,2048]{1,0:T(8,128)(2,1)S(1)}, u32[]{:S(2)}, u32[]{:S(2)}) collective-permute-start(bf16[256,2048]{1,0:T(8,128)(2,1)S(1)} %bitcast.14), channel_id=1, source_target_pairs={{0,8},{1,9},{2,10},{3,11},{8,16},{9,17},{10,18},{11,19},{16,24},{1... | collective-permute-start | bytes 3145736 | tf_op jit(solution)/shard_map/ppermute | solution.py:630
  21.6 33.4 %copy-start.5 = (bf16[2048,128]{1,0:T(8,128)(2,1)}, bf16[2048,128]{1,0:T(8,128)(2,1)S(1)}, u32[]{:S(2)}) copy-start(bf16[2048,128]{1,0:T(8,128)(2,1)S(1)} %collective-permute-done.2.refs_3_) | copy-start | bytes 1572868
  21.6 63.8 %collective-permute-start.12 = (bf16[256,2048]{1,0:T(8,128)(2,1)S(1)}, bf16[256,2048]{1,0:T(8,128)(2,1)S(1)}, u32[]{:S(2)}, u32[]{:S(2)}) collective-permute-start(bf16[256,2048]{1,0:T(8,128)(2,1)S(1)} %bitcast.15), channel_id=1, source_target_pairs={{0,12},{4,8},{1,13},{5,9},{2,14},{6,10},{3,15},{7,11}} | collective-permute-start | bytes 3145736 | tf_op jit(solution)/shard_map/ppermute | solution.py:638
  26.5 38.8 %collective-permute-start.10 = (bf16[2048,128]{1,0:T(8,128)(2,1)S(1)}, bf16[2048,128]{1,0:T(8,128)(2,1)S(1)}, u32[]{:S(2)}, u32[]{:S(2)}) collective-permute-start(bf16[2048,128]{1,0:T(8,128)(2,1)S(1)} %collective-permute-done.2.refs_3_), channel_id=1, source_target_pairs={{8,12},{12,8},{16,20},{20,16},{24,28},{28,24},{9,13},{13,9},{17,21... | collective-permute-start | bytes 1572872 | tf_op jit(solution)/shard_map/ppermute | solution.py:638
  33.6 29.5 %copy-start.6 = (bf16[2048,128]{1,0:T(8,128)(2,1)}, bf16[2048,128]{1,0:T(8,128)(2,1)S(1)}, u32[]{:S(2)}) copy-start(bf16[2048,128]{1,0:T(8,128)(2,1)S(1)} %collective-permute-done.refs_1_) | copy-start | bytes 1572868
  60.6 2.6 %collective-permute-start.4 = (bf16[64,128]{1,0:T(8,128)(2,1)S(1)}, bf16[64,128]{1,0:T(8,128)(2,1)S(1)}, u32[]{:S(2)}, u32[]{:S(2)}) collective-permute-start(bf16[64,128]{1,0:T(8,128)(2,1)S(1)} %get-tuple-element.57), channel_id=1, source_target_pairs={{0,8},{1,9},{2,10},{3,11},{4,12},{5,13},{6,14},{7,15}} | collective-permute-start | bytes 49160 | tf_op jit(solution)/shard_map/ppermute | solution.py:630
  61.9 2.7 %collective-permute-start.5 = (bf16[64,128]{1,0:T(8,128)(2,1)S(1)}, bf16[64,128]{1,0:T(8,128)(2,1)S(1)}, u32[]{:S(2)}, u32[]{:S(2)}) collective-permute-start(bf16[64,128]{1,0:T(8,128)(2,1)S(1)} %get-tuple-element.57), channel_id=1, source_target_pairs={{0,9},{1,10},{2,11},{3,8},{4,13},{5,14},{6,15},{7,12}} | collective-permute-start | bytes 49160 | tf_op jit(solution)/shard_map/ppermute | solution.py:630
  63.2 2.9 %collective-permute-start.8 = (bf16[2048,128]{1,0:T(8,128)(2,1)S(1)}, bf16[2048,128]{1,0:T(8,128)(2,1)S(1)}, u32[]{:S(2)}, u32[]{:S(2)}) collective-permute-start(bf16[2048,128]{1,0:T(8,128)(2,1)S(1)} %collective-permute-done.refs_1_), channel_id=1, source_target_pairs={{8,12},{12,8},{16,20},{20,16},{24,28},{28,24},{9,13},{13,9},{17,21... | collective-permute-start | bytes 1572872 | tf_op jit(solution)/shard_map/ppermute | solution.py:638
  64.6 9.5 %collective-permute-start.9 = (bf16[2048,128]{1,0:T(8,128)(2,1)S(1)}, bf16[2048,128]{1,0:T(8,128)(2,1)S(1)}, u32[]{:S(2)}, u32[]{:S(2)}) collective-permute-start(bf16[2048,128]{1,0:T(8,128)(2,1)S(1)} %collective-permute-done.1.refs_2_), channel_id=1, source_target_pairs={{8,12},{12,8},{16,20},{20,16},{24,28},{28,24},{9,13},{13,9},{17,21... | collective-permute-start | bytes 1572872 | tf_op jit(solution)/shard_map/ppermute | solution.py:638
  65.3 47.9 %collective-permute-start.21 = (bf16[256,2048]{1,0:T(8,128)(2,1)S(1)}, bf16[256,2048]{1,0:T(8,128)(2,1)S(1)}, u32[]{:S(2)}, u32[]{:S(2)}) collective-permute-start(bf16[256,2048]{1,0:T(8,128)(2,1)S(1)} %bitcast.16), channel_id=1, source_target_pairs={{8,20},{12,16},{16,28},{20,24},{9,21},{13,17},{17,29},{21,25},{10,... | collective-permute-start | bytes 3145736 | tf_op jit(solution)/shard_map/ppermute | solution.py:638
  66.1 18.6 %collective-permute-start.6 = (bf16[64,128]{1,0:T(8,128)(2,1)S(1)}, bf16[64,128]{1,0:T(8,128)(2,1)S(1)}, u32[]{:S(2)}, u32[]{:S(2)}) collective-permute-start(bf16[64,128]{1,0:T(8,128)(2,1)S(1)} %get-tuple-element.57), channel_id=1, source_target_pairs={{0,10},{1,11},{2,8},{3,9},{4,14},{5,15},{6,12},{7,13}} | collective-permute-start | bytes 49160 | tf_op jit(solution)/shard_map/ppermute | solution.py:630
  74.1 11.3 %collective-permute-start.7 = (bf16[64,128]{1,0:T(8,128)(2,1)S(1)}, bf16[64,128]{1,0:T(8,128)(2,1)S(1)}, u32[]{:S(2)}, u32[]{:S(2)}) collective-permute-start(bf16[64,128]{1,0:T(8,128)(2,1)S(1)} %get-tuple-element.57), channel_id=1, source_target_pairs={{0,11},{1,8},{2,9},{3,10},{4,15},{5,12},{6,13},{7,14}} | collective-permute-start | bytes 49160 | tf_op jit(solution)/shard_map/ppermute | solution.py:630
  84.6 28.6 %copy-start = (bf16[8192,256]{1,0:T(8,128)(2,1)}, bf16[8192,256]{1,0:T(8,128)(2,1)S(1)}, u32[]{:S(2)}) copy-start(bf16[8192,256]{1,0:T(8,128)(2,1)S(1)} %split_later.1.refs_6_) | copy-start | bytes 12582916
  88.4 5.3 %collective-permute-start.13 = (bf16[144,256]{1,0:T(8,128)(2,1)S(1)}, bf16[144,256]{1,0:T(8,128)(2,1)S(1)}, u32[]{:S(2)}, u32[]{:S(2)}) collective-permute-start(bf16[144,256]{1,0:T(8,128)(2,1)S(1)} %get-tuple-element.64), channel_id=1, source_target_pairs={{0,3},{1,0},{2,1},{3,2},{4,7},{5,4},{6,5},{7,6},{8,11},{9,8},{10,9... | collective-permute-start | bytes 221192 | tf_op jit(solution)/shard_map/ppermute | solution.py:622
  88.5 7.7 %collective-permute-start.14 = (bf16[144,256]{1,0:T(8,128)(2,1)S(1)}, bf16[144,256]{1,0:T(8,128)(2,1)S(1)}, u32[]{:S(2)}, u32[]{:S(2)}) collective-permute-start(bf16[144,256]{1,0:T(8,128)(2,1)S(1)} %get-tuple-element.65), channel_id=1, source_target_pairs={{0,2},{1,3},{2,0},{3,1},{4,6},{5,7},{6,4},{7,5},{8,10},{9,11},{10,... | collective-permute-start | bytes 221192 | tf_op jit(solution)/shard_map/ppermute | solution.py:622
  88.5 7.6 %collective-permute-start.15 = (bf16[144,256]{1,0:T(8,128)(2,1)S(1)}, bf16[144,256]{1,0:T(8,128)(2,1)S(1)}, u32[]{:S(2)}, u32[]{:S(2)}) collective-permute-start(bf16[144,256]{1,0:T(8,128)(2,1)S(1)} %get-tuple-element.66), channel_id=1, source_target_pairs={{0,1},{1,2},{2,3},{3,0},{4,5},{5,6},{6,7},{7,4},{8,9},{9,10},{10,1... | collective-permute-start | bytes 221192 | tf_op jit(solution)/shard_map/ppermute | solution.py:622
  96.1 17.1 %collective-permute-start.20 = (bf16[128,2048]{1,0:T(8,128)(2,1)S(1)}, bf16[128,2048]{1,0:T(8,128)(2,1)S(1)}, u32[]{:S(2)}, u32[]{:S(2)}) collective-permute-start(bf16[128,2048]{1,0:T(8,128)(2,1)S(1)} %get-tuple-element.69), channel_id=1, source_target_pairs={{0,8},{1,9},{2,10},{3,11},{8,16},{9,17},{10,18},{11,19},{16,24},{1... | collective-permute-start | bytes 1572872 | tf_op jit(solution)/shard_map/ppermute | solution.py:630
  101.1 7.1 %collective-permute-start.16 = (bf16[64,128]{1,0:T(8,128)(2,1)S(1)}, bf16[64,128]{1,0:T(8,128)(2,1)S(1)}, u32[]{:S(2)}, u32[]{:S(2)}) collective-permute-start(bf16[64,128]{1,0:T(8,128)(2,1)S(1)} %get-tuple-element.67), channel_id=1, source_target_pairs={{0,8},{1,9},{2,10},{3,11},{8,16},{9,17},{10,18},{11,19},{16,24},{1... | collective-permute-start | bytes 49160 | tf_op jit(solution)/shard_map/ppermute | solution.py:630
  107.2 5.9 %collective-permute-start.17 = (bf16[64,128]{1,0:T(8,128)(2,1)S(1)}, bf16[64,128]{1,0:T(8,128)(2,1)S(1)}, u32[]{:S(2)}, u32[]{:S(2)}) collective-permute-start(bf16[64,128]{1,0:T(8,128)(2,1)S(1)} %get-tuple-element.67), channel_id=1, source_target_pairs={{0,9},{1,10},{2,11},{3,8},{8,17},{9,18},{10,19},{11,16},{16,25},{1... | collective-permute-start | bytes 49160 | tf_op jit(solution)/shard_map/ppermute | solution.py:630
  107.2 5.9 %collective-permute-start.18 = (bf16[64,128]{1,0:T(8,128)(2,1)S(1)}, bf16[64,128]{1,0:T(8,128)(2,1)S(1)}, u32[]{:S(2)}, u32[]{:S(2)}) collective-permute-start(bf16[64,128]{1,0:T(8,128)(2,1)S(1)} %get-tuple-element.67), channel_id=1, source_target_pairs={{0,10},{1,11},{2,8},{3,9},{8,18},{9,19},{10,16},{11,17},{16,26},{1... | collective-permute-start | bytes 49160 | tf_op jit(solution)/shard_map/ppermute | solution.py:630
  108.2 5.1 %collective-permute-start.19 = (bf16[64,128]{1,0:T(8,128)(2,1)S(1)}, bf16[64,128]{1,0:T(8,128)(2,1)S(1)}, u32[]{:S(2)}, u32[]{:S(2)}) collective-permute-start(bf16[64,128]{1,0:T(8,128)(2,1)S(1)} %get-tuple-element.67), channel_id=1, source_target_pairs={{0,11},{1,8},{2,9},{3,10},{8,19},{9,16},{10,17},{11,18},{16,27},{1... | collective-permute-start | bytes 49160 | tf_op jit(solution)/shard_map/ppermute | solution.py:630
  115.6 5.3 %collective-permute-start.22 = (bf16[144,256]{1,0:T(8,128)(2,1)S(1)}, bf16[144,256]{1,0:T(8,128)(2,1)S(1)}, u32[]{:S(2)}, u32[]{:S(2)}) collective-permute-start(bf16[144,256]{1,0:T(8,128)(2,1)S(1)} %get-tuple-element.73), channel_id=1, source_target_pairs={{0,3},{1,0},{2,1},{3,2},{4,7},{5,4},{6,5},{7,6},{8,11},{9,8},{10,9... | collective-permute-start | bytes 221192 | tf_op jit(solution)/shard_map/ppermute | solution.py:622
  118.9 5.3 %collective-permute-start.23 = (bf16[144,256]{1,0:T(8,128)(2,1)S(1)}, bf16[144,256]{1,0:T(8,128)(2,1)S(1)}, u32[]{:S(2)}, u32[]{:S(2)}) collective-permute-start(bf16[144,256]{1,0:T(8,128)(2,1)S(1)} %get-tuple-element.74), channel_id=1, source_target_pairs={{0,2},{1,3},{2,0},{3,1},{4,6},{5,7},{6,4},{7,5},{8,10},{9,11},{10,... | collective-permute-start | bytes 221192 | tf_op jit(solution)/shard_map/ppermute | solution.py:622
  118.9 6.2 %collective-permute-start.24 = (bf16[144,256]{1,0:T(8,128)(2,1)S(1)}, bf16[144,256]{1,0:T(8,128)(2,1)S(1)}, u32[]{:S(2)}, u32[]{:S(2)}) collective-permute-start(bf16[144,256]{1,0:T(8,128)(2,1)S(1)} %get-tuple-element.75), channel_id=1, source_target_pairs={{0,1},{1,2},{2,3},{3,0},{4,5},{5,6},{6,7},{7,4},{8,9},{9,10},{10,1... | collective-permute-start | bytes 221192 | tf_op jit(solution)/shard_map/ppermute | solution.py:622
  125.1 18.7 %collective-permute-start.29 = (bf16[128,2048]{1,0:T(8,128)(2,1)S(1)}, bf16[128,2048]{1,0:T(8,128)(2,1)}, u32[]{:S(2)}, u32[]{:S(2)}) collective-permute-start(bf16[128,2048]{1,0:T(8,128)(2,1)S(1)} %get-tuple-element.77), channel_id=1, source_target_pairs={{0,8},{1,9},{2,10},{3,11},{8,16},{9,17},{10,18},{11,19},{16,24},{1... | collective-permute-start | bytes 1572872 | tf_op jit(solution)/shard_map/ppermute | solution.py:630
  126.9 10.8 %collective-permute-start.25 = (bf16[64,128]{1,0:T(8,128)(2,1)}, bf16[64,128]{1,0:T(8,128)(2,1)S(1)}, u32[]{:S(2)}, u32[]{:S(2)}) collective-permute-start(bf16[64,128]{1,0:T(8,128)(2,1)} %get-tuple-element.76), channel_id=1, source_target_pairs={{0,8},{1,9},{2,10},{3,11},{8,16},{9,17},{10,18},{11,19},{16,24},{1... | collective-permute-start | bytes 49160 | tf_op jit(solution)/shard_map/ppermute | solution.py:630
  132.1 48.0 %collective-permute-start.37 = (bf16[256,2048]{1,0:T(8,128)(2,1)S(1)}, bf16[256,2048]{1,0:T(8,128)(2,1)S(1)}, u32[]{:S(2)}, u32[]{:S(2)}) collective-permute-start(bf16[256,2048]{1,0:T(8,128)(2,1)S(1)} %bitcast.17), channel_id=1, source_target_pairs={{24,28},{28,24},{25,29},{29,25},{26,30},{30,26},{27,31},{31,27}} | collective-permute-start | bytes 3145736 | tf_op jit(solution)/shard_map/ppermute | solution.py:638
  132.9 7.5 %collective-permute-start.26 = (bf16[64,128]{1,0:T(8,128)(2,1)}, bf16[64,128]{1,0:T(8,128)(2,1)}, u32[]{:S(2)}, u32[]{:S(2)}) collective-permute-start(bf16[64,128]{1,0:T(8,128)(2,1)} %get-tuple-element.76), channel_id=1, source_target_pairs={{0,9},{1,10},{2,11},{3,8},{8,17},{9,18},{10,19},{11,16},{16,25},{1... | collective-permute-start | bytes 49160 | tf_op jit(solution)/shard_map/ppermute | solution.py:630
  136.2 5.3 %collective-permute-start.27 = (bf16[64,128]{1,0:T(8,128)(2,1)}, bf16[64,128]{1,0:T(8,128)(2,1)}, u32[]{:S(2)}, u32[]{:S(2)}) collective-permute-start(bf16[64,128]{1,0:T(8,128)(2,1)} %get-tuple-element.76), channel_id=1, source_target_pairs={{0,10},{1,11},{2,8},{3,9},{8,18},{9,19},{10,16},{11,17},{16,26},{1... | collective-permute-start | bytes 49160 | tf_op jit(solution)/shard_map/ppermute | solution.py:630
  138.2 5.6 %collective-permute-start.28 = (bf16[64,128]{1,0:T(8,128)(2,1)}, bf16[64,128]{1,0:T(8,128)(2,1)}, u32[]{:S(2)}, u32[]{:S(2)}) collective-permute-start(bf16[64,128]{1,0:T(8,128)(2,1)} %get-tuple-element.76), channel_id=1, source_target_pairs={{0,11},{1,8},{2,9},{3,10},{8,19},{9,16},{10,17},{11,18},{16,27},{1... | collective-permute-start | bytes 49160 | tf_op jit(solution)/shard_map/ppermute | solution.py:630
  140.3 32.7 %collective-permute-start.40 = (bf16[16,2,64,128]{3,2,1,0:T(8,128)(2,1)}, bf16[16,2,64,128]{3,2,1,0:T(8,128)(2,1)}, u32[]{:S(2)}, u32[]{:S(2)}) collective-permute-start(bf16[16,2,64,128]{3,2,1,0:T(8,128)(2,1)} %copy-done.34), channel_id=1, source_target_pairs={{0,4},{4,0},{8,12},{12,8},{16,20},{20,16},{24,28},{28,24},{1,5},{5... | collective-permute-start | bytes 1572872 | tf_op jit(solution)/shard_map/ppermute | solution.py:638
  148.3 5.5 %collective-permute-start.30 = (bf16[144,256]{1,0:T(8,128)(2,1)S(1)}, bf16[144,256]{1,0:T(8,128)(2,1)S(1)}, u32[]{:S(2)}, u32[]{:S(2)}) collective-permute-start(bf16[144,256]{1,0:T(8,128)(2,1)S(1)} %get-tuple-element.79), channel_id=1, source_target_pairs={{0,3},{1,0},{2,1},{3,2},{4,7},{5,4},{6,5},{7,6},{8,11},{9,8},{10,9... | collective-permute-start | bytes 221192 | tf_op jit(solution)/shard_map/ppermute | solution.py:622
  151.7 5.3 %collective-permute-start.31 = (bf16[144,256]{1,0:T(8,128)(2,1)S(1)}, bf16[144,256]{1,0:T(8,128)(2,1)S(1)}, u32[]{:S(2)}, u32[]{:S(2)}) collective-permute-start(bf16[144,256]{1,0:T(8,128)(2,1)S(1)} %get-tuple-element.80), channel_id=1, source_target_pairs={{0,2},{1,3},{2,0},{3,1},{4,6},{5,7},{6,4},{7,5},{8,10},{9,11},{10,... | collective-permute-start | bytes 221192 | tf_op jit(solution)/shard_map/ppermute | solution.py:622
  151.7 6.2 %collective-permute-start.32 = (bf16[144,256]{1,0:T(8,128)(2,1)S(1)}, bf16[144,256]{1,0:T(8,128)(2,1)S(1)}, u32[]{:S(2)}, u32[]{:S(2)}) collective-permute-start(bf16[144,256]{1,0:T(8,128)(2,1)S(1)} %get-tuple-element.81), channel_id=1, source_target_pairs={{0,1},{1,2},{2,3},{3,0},{4,5},{5,6},{6,7},{7,4},{8,9},{9,10},{10,1... | collective-permute-start | bytes 221192 | tf_op jit(solution)/shard_map/ppermute | solution.py:622
  158.4 21.7 %collective-permute-start.33 = (bf16[128,2048]{1,0:T(8,128)(2,1)}, bf16[128,2048]{1,0:T(8,128)(2,1)}, u32[]{:S(2)}, u32[]{:S(2)}) collective-permute-start(bf16[128,2048]{1,0:T(8,128)(2,1)} %select_select_fusion), channel_id=1, source_target_pairs={{0,24},{1,25},{2,26},{3,27},{8,0},{9,1},{10,2},{11,3},{16,8},{17,9... | collective-permute-start | bytes 1572872 | tf_op jit(solution)/shard_map/ppermute | solution.py:630
  168.6 6.3 %collective-permute-start.39 = (bf16[128,256]{1,0:T(8,128)(2,1)S(1)}, bf16[128,256]{1,0:T(8,128)(2,1)S(1)}, u32[]{:S(2)}, u32[]{:S(2)}) collective-permute-start(bf16[128,256]{1,0:T(8,128)(2,1)S(1)} %select_select_fusion.1), channel_id=1, source_target_pairs={{0,4},{4,0},{8,12},{12,8},{16,20},{20,16},{24,28},{28,24},{1,5},{5... | collective-permute-start | bytes 196616 | tf_op jit(solution)/shard_map/ppermute | solution.py:638
  169.0 4.0 %collective-permute-start.38 = (s32[16,128]{1,0:T(8,128)S(1)}, s32[16,128]{1,0:T(8,128)S(1)}, u32[]{:S(2)}, u32[]{:S(2)}) collective-permute-start(s32[16,128]{1,0:T(8,128)S(1)} %copy-done.36), channel_id=1, source_target_pairs={{0,4},{4,0},{8,12},{12,8},{16,20},{20,16},{24,28},{28,24},{1,5},{5... | collective-permute-start | bytes 24584 | tf_op jit(solution)/shard_map/ppermute | solution.py:638
  173.1 7.1 %collective-permute-start.34 = (bf16[64,128]{1,0:T(8,128)(2,1)}, bf16[64,128]{1,0:T(8,128)(2,1)S(1)}, u32[]{:S(2)}, u32[]{:S(2)}) collective-permute-start(bf16[64,128]{1,0:T(8,128)(2,1)} %get-tuple-element.84.refs_0_), channel_id=1, source_target_pairs={{0,1},{1,2},{2,3},{3,0},{4,5},{5,6},{6,7},{7,4},{8,9},{9,10},{10,1... | collective-permute-start | bytes 49160 | tf_op jit(solution)/shard_map/ppermute | solution.py:622
  173.1 7.1 %collective-permute-start.35 = (bf16[64,128]{1,0:T(8,128)(2,1)}, bf16[64,128]{1,0:T(8,128)(2,1)S(1)}, u32[]{:S(2)}, u32[]{:S(2)}) collective-permute-start(bf16[64,128]{1,0:T(8,128)(2,1)} %get-tuple-element.84.refs_0_), channel_id=1, source_target_pairs={{0,2},{1,3},{2,0},{3,1},{4,6},{5,7},{6,4},{7,5},{8,10},{9,11},{10,... | collective-permute-start | bytes 49160 | tf_op jit(solution)/shard_map/ppermute | solution.py:622
  175.0 5.2 %collective-permute-start.36 = (bf16[64,128]{1,0:T(8,128)(2,1)}, bf16[64,128]{1,0:T(8,128)(2,1)S(1)}, u32[]{:S(2)}, u32[]{:S(2)}) collective-permute-start(bf16[64,128]{1,0:T(8,128)(2,1)} %get-tuple-element.84.refs_0_), channel_id=1, source_target_pairs={{0,3},{1,0},{2,1},{3,2},{4,7},{5,4},{6,5},{7,6},{8,11},{9,8},{10,9... | collective-permute-start | bytes 49160 | tf_op jit(solution)/shard_map/ppermute | solution.py:622
  (39 other events, 247.6 us)

commit v3 on v2

--- a/solution.py
+++ b/solution.py
@@ -15,7 +15,7 @@
 MAXP = 4
 EPS = 1e-05
 BIG = -1e30
-VMEM_MIB = 32
+VMEM_MIB = 20
 SCALE = HD ** (-0.5)
 VM = pl.BlockSpec(memory_space=pltpu.VMEM)
 SM = pl.BlockSpec(memory_space=pltpu.SMEM)
@@ -23,8 +23,9 @@
 NT = (((1,), (1,)), ((), ()))
 
 
-def vmem(mib=VMEM_MIB):
-    return pltpu.CompilerParams(vmem_limit_bytes=mib << 20)
+def vmem(*large):
+    size = sum(x.size * x.dtype.itemsize for x in large)
+    return pltpu.CompilerParams(vmem_limit_bytes=(VMEM_MIB << 20) + size)
 
 
 def kept(shape, dtype):
@@ -82,7 +83,7 @@
             pltpu.SemaphoreType.DMA((len(chunks),)),
         ],
         compiler_params=vmem(),
-        cost_estimate=cost(5),
+        cost_estimate=cost(0.3),
         name=name,
     )(sec, *[in_hbm(x) for x in raws])
 
@@ -276,7 +277,7 @@
             pltpu.SemaphoreType.DMA,
         ],
         compiler_params=vmem(),
-        cost_estimate=cost(10),
+        cost_estimate=cost(0.3),
         name="local_work",
     )(sec, table, lengths, ids, rows, moves, queries, in_hbm(pages))
 
@@ -370,11 +371,15 @@
         )
 
 
-def later_kernel(section, n_tp, n_a, total_width, sec_ref, *refs):
+def later_kernel(section, n_tp, n_a, total_width, sec_ref, held_ref, *refs):
     m_refs = refs[:n_tp]
     shared = refs[n_tp : n_tp + 6]
     a_refs = refs[n_tp + 6 : n_tp + 6 + n_a]
     fresh_ref, low_ref, mixed_all, *a_bufs, sems = refs[n_tp + 6 + n_a :]
+
+    @pl.when(sec_ref[0] != section)
+    def _():
+        fresh_ref[...] = held_ref[...]
 
     @pl.when(sec_ref[0] == section)
     def _():
@@ -413,7 +418,7 @@
             *[pltpu.VMEM(a.shape, jnp.bfloat16) for a in a_blocks],
             pltpu.SemaphoreType.DMA((len(a_blocks),)),
         ],
-        compiler_params=vmem(),
+        compiler_params=vmem(*a_blocks),
         cost_estimate=cost(5),
         name=name,
     )(*operands, *[in_hbm(a) for a in a_blocks])
@@ -445,6 +450,10 @@
     return (h.astype(jnp.float32) + delta).astype(jnp.bfloat16)
 
 
+def far_shift(n_tp):
+    return n_tp // 2
+
+
 def spreads(packed, slots, b_refs):
     out = []
     base = 0
@@ -456,73 +465,63 @@
 
 def slice_kernel(section, n_tp, n_b, sec_ref, *refs):
     low_refs = refs[:n_tp]
-    slot_ref, gain_ref, w_ref, h_ref = refs[n_tp : n_tp + 4]
-    b_refs = refs[n_tp + 4 : n_tp + 4 + n_b]
-    rest = refs[n_tp + 4 + n_b :]
-    h_out, m_refs = rest[0], rest[1 : 1 + n_tp]
-    x_all, h_buf = rest[1 + n_tp : 3 + n_tp]
-    b_bufs = rest[3 + n_tp : 3 + n_tp + n_b]
-    sems = rest[3 + n_tp + n_b]
-    tokens, width = h_buf.shape
+    slot_ref, gain_ref, near_ref, far_ref, h_ref, held_ref = refs[n_tp : n_tp + 6]
+    b_refs = refs[n_tp + 6 : n_tp + 6 + n_b]
+    h_out, *m_refs, x_all = refs[n_tp + 6 + n_b :]
+    tokens, width = h_ref.shape
+    far = far_shift(n_tp)
     part = width // 4
 
+    @pl.when(sec_ref[0] != section)
+    def _():
+        h_out[...] = held_ref[...]
+
     @pl.when(sec_ref[0] == section)
     def _():
-        loads = [pltpu.make_async_copy(h_ref, h_buf, sems.at[0])]
-        for i in range(n_b):
-            loads.append(pltpu.make_async_copy(b_refs[i], b_bufs[i], sems.at[1 + i]))
-        for load in loads:
-            load.start()
         packed = low_refs[0][...].astype(jnp.float32)
         for low_ref in low_refs[1:]:
             packed = packed + low_ref[...].astype(jnp.float32)
         rounded = packed.astype(jnp.bfloat16)
         low = spreads(rounded.astype(jnp.float32), slot_ref[...], b_refs)
-        for load in loads:
-            load.wait()
         square = jnp.zeros((tokens, 1), jnp.float32)
         for c in range(4):
             span = slice(c * part, (c + 1) * part)
-            h = add_delta(low, b_bufs, h_buf[:, span], span)
-            h_buf[:, span] = h
+            h = add_delta(low, b_refs, h_ref[:, span], span)
+            h_out[:, span] = h
             h = h.astype(jnp.float32)
             square = square + jnp.sum(h * h, axis=1, keepdims=True)
             lane = pl.multiple_of(sec_ref[1] * width + c * part, part)
             gain = gain_ref[:, pl.ds(lane, part)].astype(jnp.float32)
             x_all[:, span] = (h * gain).astype(jnp.bfloat16)
-        store = pltpu.make_async_copy(h_buf, h_out, sems.at[0])
-        store.start()
         square = jnp.transpose(jnp.broadcast_to(square, (tokens, HD)))[:16]
         high = square.astype(jnp.bfloat16).astype(jnp.float32)
         upper = lax.broadcasted_iota(jnp.int32, (16, HD), 0) < 8
         tail = jnp.where(upper, high, square - high).astype(jnp.bfloat16)
         for s in range(n_tp):
-            rows = pl.ds(s * width, width)
-            proj = jnp.dot(x_all[...], w_ref[rows, :], preferred_element_type=jnp.float32)
+            if s == far:
+                rows = far_ref[...]
+            else:
+                place = s - (s > far)
+                rows = near_ref[place * width : (place + 1) * width, :]
+            proj = jnp.dot(x_all[...], rows, preferred_element_type=jnp.float32)
             m_refs[s][:tokens, :] = proj.astype(jnp.bfloat16)
             m_refs[s][tokens:, :HD] = tail
             m_refs[s][tokens:, HD:] = jnp.zeros_like(tail)
-        store.wait()
-
-
-def section_slice(section, n_tp, sec, lows, slots, gain, h_prev, weights, b_blocks):
+
+
+def section_slice(section, n_tp, sec, lows, slots, gain, near, far, h_prev, held, b_blocks):
     tokens, width = h_prev.shape
-    operands = [sec, *lows, slots, gain, weights, *[in_hbm(x) for x in (h_prev, *b_blocks)]]
+    operands = [sec, *lows, slots, gain, near, far, h_prev, held, *b_blocks]
     return pl.pallas_call(
         functools.partial(slice_kernel, section, n_tp, len(b_blocks)),
-        in_specs=[SM] + [VM] * (n_tp + 3) + [ANY] * (1 + len(b_blocks)),
-        out_specs=(ANY,) + (VM,) * n_tp,
+        in_specs=[SM] + [VM] * (len(operands) - 1),
+        out_specs=(VM,) * (1 + n_tp),
         out_shape=(
             sds((tokens, width), jnp.bfloat16),
             *[sds((tokens + 16, 2 * HD), jnp.bfloat16)] * n_tp,
         ),
-        scratch_shapes=[
-            pltpu.VMEM((tokens, width), jnp.bfloat16),
-            pltpu.VMEM((tokens, width), jnp.bfloat16),
-            *[pltpu.VMEM(b.shape, jnp.bfloat16) for b in b_blocks],
-            pltpu.SemaphoreType.DMA((1 + len(b_blocks),)),
-        ],
-        compiler_params=vmem(),
+        scratch_shapes=[pltpu.VMEM((tokens, width), jnp.bfloat16)],
+        compiler_params=vmem(*b_blocks),
         cost_estimate=cost(5),
         name="section_slice_%d" % section,
     )(*operands)
@@ -559,7 +558,7 @@
         in_specs=[SM] + [VM] * (len(operands) - 1),
         out_specs=VM,
         out_shape=sds((1, *held.shape), jnp.bfloat16),
-        compiler_params=vmem(),
+        compiler_params=vmem(*b_blocks),
         cost_estimate=cost(3),
         name="section_result",
     )(*operands)
@@ -684,7 +683,10 @@
         half,
         "split_first",
     )
-    other = [partner(after(m, lse), later) for m in mine]
+    far = far_shift(n_tp)
+    turns = [s for s in range(1, n_tp) if s != far]
+    other = {s: partner(after(mine[s - 1], lse), later) for s in turns}
+    weights = after(weights, *other.values())
 
     shared = [queries[0], cos, sin, acc, lse, slots]
     n_a = len(a_blocks)
@@ -696,55 +698,44 @@
         q_width,
         "first_section",
     )
+    other[far] = partner(after(mine[far - 1], low), later)
     chunks = [(0, lambda sec, i=i: 2 * sec[1] + i, lambda sec, i=i: i) for i in range(2)]
-    for s in range(1, n_tp):
-        chunks.append((s, lambda sec: 0, lambda sec, s=s: 2 * s + sec[2]))
-    for s in range(1, n_tp):
-        chunks.append((n_tp - 1 + s, lambda sec: 0, lambda sec, s=s: 2 * s + 1 - sec[2]))
-    own_rows = split_parts(
-        sec,
-        [after(raw, low), *mine, *other],
-        chunks,
-        lambda section: section > 0,
-        half,
-        "split_later",
-    )
+    raws = [after(raw, low)]
+    for place, s in enumerate(turns, 1):
+        chunks.append((len(raws), lambda sec: 0, lambda sec, p=place: 2 * p + sec[2]))
+        chunks.append((len(raws) + 1, lambda sec: 0, lambda sec, p=place: 2 * p + 1 - sec[2]))
+        raws += [mine[s - 1], other[s]]
+    inner = lambda section: section > 0
+    near_rows = split_parts(sec, raws, chunks, inner, half, "split_near")
+    chunks = [(0, lambda sec: 0, lambda sec: sec[2]), (1, lambda sec: 0, lambda sec: 1 - sec[2])]
+    far_rows = split_parts(sec, [mine[far - 1], other[far]], chunks, inner, half, "split_far")
+    if paired:
+        late = partner(after(b_own, near_rows), later[:-1], 1)
     h_prev = h_new = hidden
-    hs, news = [hidden], [fresh]
     for l in later:
         lows = [onward(low, s, 1, [0] if l == 1 else range(n_sec)) for s in range(n_tp)]
-        if l == 1 and paired:
-            late = partner(after(b_own, lows[0]), later[:-1], 1)
         if l == 2 and paired:
             b_blocks = [b_own, partner(after(b_own, low), [final])]
             leaving = partner(after(leaving, low))
         if paired:
             before = [own_before, early if l == 1 else late]
         h_new, *parts = section_slice(
-            l, n_tp, sec, lows, slots, norm_gain, h_prev, own_rows, before
+            l, n_tp, sec, lows, slots, norm_gain, near_rows, far_rows, h_prev, h_new, before
         )
-        hs.append(h_new)
         parts = [parts[0]] + [around(parts[s], -s) for s in range(1, n_tp)]
         if l < final:
             h_prev = onward(after(h_new, *parts[1:]), 0)
         else:
-            back = h_new
-            for m in later[:-1]:
-                back = jnp.where(section == m, hs[m], back)
-            back = onward(after(back, *parts[1:]), 0, -1)
+            back = onward(after(h_new, *parts[1:]), 0, -1)
         fresh, low = attend_call(
             functools.partial(later_kernel, l, n_tp, n_a, depth),
-            [sec, *parts, *shared],
+            [sec, fresh, *parts, *shared],
             a_blocks,
             tokens,
             q_width,
             "section_%d" % l,
         )
-        news.append(fresh)
     lows = [low] + [around(low, s) for s in range(1, n_tp)]
-    fresh = news[0]
-    for l in later:
-        fresh = jnp.where(section == l, news[l], fresh)
     if paired:
         arrived = insert_new(spots, partner(fresh), leaving)
     else:

time: 184 us -> 156 us (0.85)
  local copies, waits for them, and re-layouts: 21.6 us -> 2.12 us
  starting transfers between devices: 79.5 us -> 68.4 us
  waiting for transfers between devices: 50.4 us -> 57.7 us
    unnamed x94 -> x34, local copies, waits for them, and re-layouts: 20.7 us -> 1.28 us
    ppermute x16, starting transfers between devices: 47.5 us -> 29.4 us  [onward(): return lax.ppermute(x, ('pipe', 'tp'), pairs)]
    ppermute x15, waiting for transfers between devices: 39.4 us -> 44.3 us  [around(): return lax.ppermute(x, 'tp', [(t, (t + shift) % n_tp) for t in range(n_tp)])]
    ppermute x10, starting transfers between devices: 12 us -> 15.6 us  [partner(): return lax.ppermute(x, ('pipe', 'req'), pairs)]
    ppermute x15, starting transfers between devices: 20 us -> 23.5 us  [around(): return lax.ppermute(x, 'tp', [(t, (t + shift) % n_tp) for t in range(n_tp)])]
    ppermute x16, waiting for transfers between devices: 8.65 us -> 10.7 us  [onward(): return lax.ppermute(x, ('pipe', 'tp'), pairs)]
    pallas_call x2 -> x3, Pallas kernels: 3.54 us -> 4.09 us  [split_parts(): pl.pallas_call(functools.partial(split_kernel, chunks, section_of), in_sp...]
  transfers between devices with their start and end apart: 41 -> 41, of which waited for: 17 -> 18; matrix products, arithmetic and copies ran while one was open for 2% -> 1% of each run, Pallas kernels for 13% -> 14%
where the time goes in v3:
time: 156 us; the launch traced here: 155 us
  starting transfers between devices  68.4 us (44%)
  waiting for transfers between devices  57.7 us (37%)
  Pallas kernels  25.9 us (17%)
  local copies, waits for them, and re-layouts  2.12 us (1%)
    ppermute x15, waiting for transfers between devices, around(): return lax.ppermute(x, 'tp', [(t, (t + shift) % n_tp) for t in range(n_tp)])  44.3 us
    ppermute x16, starting transfers between devices, onward(): return lax.ppermute(x, ('pipe', 'tp'), pairs)  29.4 us
    ppermute x15, starting transfers between devices, around(): return lax.ppermute(x, 'tp', [(t, (t + shift) % n_tp) for t in range(n_tp)])  23.5 us
    ppermute x10, starting transfers between devices, partner(): return lax.ppermute(x, ('pipe', 'req'), pairs)  15.6 us
    ppermute x16, waiting for transfers between devices, onward(): return lax.ppermute(x, ('pipe', 'tp'), pairs)  10.7 us
    pallas_call x4, Pallas kernels, attend_call(): pl.pallas_call(kernel, in_specs=[SM] + [VM] * (len(operands) - 1) + [ANY]...  7.91 us
    pallas_call x1, Pallas kernels, local_work(): pl.pallas_call(functools.partial(local_kernel, paired, adapters), in_spec...  6.96 us
    pallas_call x3, Pallas kernels, split_parts(): pl.pallas_call(functools.partial(split_kernel, chunks, section_of), in_sp...  4.09 us
  transfers between devices with their start and end apart: 41, of which 18 were waited for; matrix products, arithmetic and copies ran while one was open for 1% of the time, Pallas kernels for 14%

profile of v3, /device:TPU:0, one launch (start us, length us, event | category | flops | bytes accessed | tf_op | source)
XLA Modules:
  0.0 155.3 jit_solution(14604359934036525863)
XLA Ops:
  0.8 1.0 copy-done
  1.8 1.8 %parcels.1 = (bf16[2048,128]{1,0:T(8,128)(2,1)}, bf16[2048,128]{1,0:T(8,128)(2,1)S(1)}, bf16[2048,128]{1,0:T(8,128)(2,1)}) custom-call(s32[4]{0:T(128)S(1)} %pad_add_fusion.sec_ref, bf16[128,2048]{1,0:T(8,128)(2,1)S(1)} %copy-done, bf16[16384,128]{1,0:T(8,128)(2,1)} %bitcast.19), custom_call_target="tpu_custom_call" | custom-call | bytes 6000000 | tf_op jit(solution)/shard_map/parcels/pallas_call | solution.py:122
  3.6 3.1 %collective-permute-start = (bf16[2048,128]{1,0:T(8,128)(2,1)}, bf16[2048,128]{1,0:T(8,128)(2,1)S(1)}, u32[]{:S(2)}, u32[]{:S(2)}) collective-permute-start(bf16[2048,128]{1,0:T(8,128)(2,1)} %get-tuple-element.49), channel_id=1, source_target_pairs={{0,1},{1,2},{2,3},{3,0},{4,5},{5,6},{6,7},{7,4},{8,9},{9,10},{10,1... | collective-permute-start | bytes 1572872 | tf_op jit(solution)/shard_map/ppermute | solution.py:621
  6.7 2.1 %collective-permute-start.2 = (bf16[2048,128]{1,0:T(8,128)(2,1)}, bf16[2048,128]{1,0:T(8,128)(2,1)S(1)}, u32[]{:S(2)}, u32[]{:S(2)}) collective-permute-start(bf16[2048,128]{1,0:T(8,128)(2,1)} %get-tuple-element.51), channel_id=1, source_target_pairs={{0,3},{1,0},{2,1},{3,2},{4,7},{5,4},{6,5},{7,6},{8,11},{9,8},{10,9... | collective-permute-start | bytes 1572872 | tf_op jit(solution)/shard_map/ppermute | solution.py:621
  8.8 1.6 %collective-permute-start.3 = (bf16[256,1024]{1,0:T(8,128)(2,1)}, bf16[256,1024]{1,0:T(8,128)(2,1)}, u32[]{:S(2)}, u32[]{:S(2)}) collective-permute-start(bf16[256,1024]{1,0:T(8,128)(2,1)} %bitcast.7.refs_12_.refs_10_), channel_id=1, source_target_pairs={{0,4},{4,0},{8,12},{12,8},{16,20},{20,16},{24,28},{28,24},{1,5},{5... | collective-permute-start | bytes 1572872 | tf_op jit(solution)/shard_map/ppermute | solution.py:637
  10.8 7.0 %local_work.1 = (f32[8,128,128]{2,1,0:T(8,128)S(1)}, f32[128,128]{1,0:T(8,128)S(1)}, s32[128,128]{1,0:T(8,128)S(1)}, f32[128,128]{1,0:T(8,128)S(1)}, f32[128,128...) custom-call(s32[4]{0:T(128)S(1)} %pad_add_fusion.sec_ref, s32[128]{0:T(128)S(1)} %reshape.15.table_ref, ...), custom_call_target="tpu_custom_call" | custom-call | bytes 900000 | tf_op jit(solution)/shard_map/local_work/pallas_call | solution.py:260
  17.8 3.8 %collective-permute-done.refs_1_ = bf16[2048,128]{1,0:T(8,128)(2,1)S(1)} collective-permute-done((bf16[2048,128]{1,0:T(8,128)(2,1)}, bf16[2048,128]{1,0:T(8,128)(2,1)S(1)}, u32[]{:S(2)}, u32[]{:S(2)}) %collective-permute-start) | collective-permute-done | bytes 524320 | tf_op jit(solution)/shard_map/ppermute | solution.py:621
  22.3 10.4 %collective-permute-done.2.refs_3_ = bf16[2048,128]{1,0:T(8,128)(2,1)S(1)} collective-permute-done((bf16[2048,128]{1,0:T(8,128)(2,1)}, bf16[2048,128]{1,0:T(8,128)(2,1)S(1)}, u32[]{:S(2)}, u32[]{:S(2)}) %collective-permute-start.2) | collective-permute-done | bytes 524320 | tf_op jit(solution)/shard_map/ppermute | solution.py:621
  33.3 2.1 %collective-permute-start.1 = (bf16[2048,128]{1,0:T(8,128)(2,1)S(1)}, bf16[2048,128]{1,0:T(8,128)(2,1)S(1)}, u32[]{:S(2)}, u32[]{:S(2)}) collective-permute-start(bf16[2048,128]{1,0:T(8,128)(2,1)S(1)} %get-tuple-element.50), channel_id=1, source_target_pairs={{0,2},{1,3},{2,0},{3,1},{4,6},{5,7},{6,4},{7,5},{8,10},{9,11},{10,... | collective-permute-start | bytes 1572872 | tf_op jit(solution)/shard_map/ppermute | solution.py:621
  35.4 1.4 collective-permute-start.11
  36.8 7.8 %collective-permute-start.12 = (bf16[256,2048]{1,0:T(8,128)(2,1)S(1)}, bf16[256,2048]{1,0:T(8,128)(2,1)S(1)}, u32[]{:S(2)}, u32[]{:S(2)}) collective-permute-start(bf16[256,2048]{1,0:T(8,128)(2,1)S(1)} %bitcast.15), channel_id=1, source_target_pairs={{0,12},{4,8},{1,13},{5,9},{2,14},{6,10},{3,15},{7,11}} | collective-permute-start | bytes 3145736 | tf_op jit(solution)/shard_map/ppermute | solution.py:637
  44.6 2.9 %split_first.1.refs_4_ = bf16[8192,256]{1,0:T(8,128)(2,1)S(1)} custom-call(s32[4]{0:T(128)S(1)} %pad_add_fusion.sec_ref, bf16[16384,128]{1,0:T(8,128)(2,1)} %bitcast.20), custom_call_target="tpu_custom_call" | custom-call | bytes 900000 | tf_op jit(solution)/shard_map/split_first/pallas_call | solution.py:75
  47.5 12.4 %collective-permute-done.1.refs_2_.refs_0_ = bf16[2048,128]{1,0:T(8,128)(2,1)S(1)} collective-permute-done((bf16[2048,128]{1,0:T(8,128)(2,1)S(1)}, bf16[2048,128]{1,0:T(8,128)(2,1)S(1)}, u32[]{:S(2)}, u32[]{:S(2)}) %collective-permute-start.1) | collective-permute-done | bytes 524320 | tf_op jit(solution)/shard_map/ppermute | solution.py:621
  59.9 5.6 %first_section.1 = (bf16[128,256]{1,0:T(8,128)(2,1)S(1)}, bf16[64,128]{1,0:T(8,128)(2,1)S(1)}) custom-call(s32[4]{0:T(128)S(1)} %pad_add_fusion.sec_ref, bf16[128,2048]{1,0:T(8,128)(2,1)S(1)} %copy-done.1, bf16[2048,128]{1,0:T(8,128)(2,1)S(1)} %collective-permute-done.refs_1_, bf16[2048,128]{1,0:T(8,128)(2,1)S(1)} %collective-permute-done.1.refs_2_.refs_0_, ...), custom_call_target="tpu_custom_call" | custom-call | bytes 15000000 | tf_op jit(solution)/shard_map/first_section/pallas_call | solution.py:408
  67.6 5.9 %collective-permute-start.6 = (bf16[64,128]{1,0:T(8,128)(2,1)S(1)}, bf16[64,128]{1,0:T(8,128)(2,1)S(1)}, u32[]{:S(2)}, u32[]{:S(2)}) collective-permute-start(bf16[64,128]{1,0:T(8,128)(2,1)S(1)} %get-tuple-element.62), channel_id=1, source_target_pairs={{0,8},{1,9},{2,10},{3,11},{4,12},{5,13},{6,14},{7,15}} | collective-permute-start | bytes 49160 | tf_op jit(solution)/shard_map/ppermute | solution.py:629
  73.5 1.3 collective-permute-start.7
  74.8 1.3 collective-permute-start.8
  76.1 2.6 %collective-permute-start.9 = (bf16[64,128]{1,0:T(8,128)(2,1)S(1)}, bf16[64,128]{1,0:T(8,128)(2,1)S(1)}, u32[]{:S(2)}, u32[]{:S(2)}) collective-permute-start(bf16[64,128]{1,0:T(8,128)(2,1)S(1)} %get-tuple-element.62), channel_id=1, source_target_pairs={{0,11},{1,8},{2,9},{3,10},{4,15},{5,12},{6,13},{7,14}} | collective-permute-start | bytes 49160 | tf_op jit(solution)/shard_map/ppermute | solution.py:629
  80.7 2.2 %collective-permute-start.13 = (bf16[144,256]{1,0:T(8,128)(2,1)S(1)}, bf16[144,256]{1,0:T(8,128)(2,1)S(1)}, u32[]{:S(2)}, u32[]{:S(2)}) collective-permute-start(bf16[144,256]{1,0:T(8,128)(2,1)S(1)} %get-tuple-element.67), channel_id=1, source_target_pairs={{0,3},{1,0},{2,1},{3,2},{4,7},{5,4},{6,5},{7,6},{8,11},{9,8},{10,9... | collective-permute-start | bytes 221192 | tf_op jit(solution)/shard_map/ppermute | solution.py:621
  82.9 1.1 collective-permute-start.15
  84.0 1.1 collective-permute-done.13.refs_1_
  85.2 6.0 %collective-permute-done.14.refs_2_ = bf16[144,256]{1,0:T(8,128)(2,1)S(1)} collective-permute-done((bf16[144,256]{1,0:T(8,128)(2,1)S(1)}, bf16[144,256]{1,0:T(8,128)(2,1)S(1)}, u32[]{:S(2)}, u32[]{:S(2)}) %collective-permute-start.14) | collective-permute-done | bytes 73760 | tf_op jit(solution)/shard_map/ppermute | solution.py:621
  92.2 4.0 %collective-permute-start.16 = (bf16[64,128]{1,0:T(8,128)(2,1)S(1)}, bf16[64,128]{1,0:T(8,128)(2,1)S(1)}, u32[]{:S(2)}, u32[]{:S(2)}) collective-permute-start(bf16[64,128]{1,0:T(8,128)(2,1)S(1)} %get-tuple-element.71), channel_id=1, source_target_pairs={{0,8},{1,9},{2,10},{3,11},{8,16},{9,17},{10,18},{11,19},{16,24},{1... | collective-permute-start | bytes 49160 | tf_op jit(solution)/shard_map/ppermute | solution.py:629
  96.2 1.5 collective-permute-start.18
  97.7 2.3 %collective-permute-done.16.refs_0_ = bf16[64,128]{1,0:T(8,128)(2,1)S(1)} collective-permute-done((bf16[64,128]{1,0:T(8,128)(2,1)S(1)}, bf16[64,128]{1,0:T(8,128)(2,1)S(1)}, u32[]{:S(2)}, u32[]{:S(2)}) %collective-permute-start.16) | collective-permute-done | bytes 16416 | tf_op jit(solution)/shard_map/ppermute | solution.py:629
  100.0 2.1 %collective-permute-done.17.refs_1_ = bf16[64,128]{1,0:T(8,128)(2,1)S(1)} collective-permute-done((bf16[64,128]{1,0:T(8,128)(2,1)S(1)}, bf16[64,128]{1,0:T(8,128)(2,1)S(1)}, u32[]{:S(2)}, u32[]{:S(2)}) %collective-permute-start.17) | collective-permute-done | bytes 16416 | tf_op jit(solution)/shard_map/ppermute | solution.py:629
  102.0 2.0 %collective-permute-done.19.refs_3_ = bf16[64,128]{1,0:T(8,128)(2,1)S(1)} collective-permute-done((bf16[64,128]{1,0:T(8,128)(2,1)S(1)}, bf16[64,128]{1,0:T(8,128)(2,1)S(1)}, u32[]{:S(2)}, u32[]{:S(2)}) %collective-permute-start.19) | collective-permute-done | bytes 16416 | tf_op jit(solution)/shard_map/ppermute | solution.py:629
  104.6 1.7 %collective-permute-start.22 = (bf16[144,256]{1,0:T(8,128)(2,1)S(1)}, bf16[144,256]{1,0:T(8,128)(2,1)S(1)}, u32[]{:S(2)}, u32[]{:S(2)}) collective-permute-start(bf16[144,256]{1,0:T(8,128)(2,1)S(1)} %get-tuple-element.76), channel_id=1, source_target_pairs={{0,3},{1,0},{2,1},{3,2},{4,7},{5,4},{6,5},{7,6},{8,11},{9,8},{10,9... | collective-permute-start | bytes 221192 | tf_op jit(solution)/shard_map/ppermute | solution.py:621
  106.5 1.9 %collective-permute-start.24 = (bf16[144,256]{1,0:T(8,128)(2,1)S(1)}, bf16[144,256]{1,0:T(8,128)(2,1)S(1)}, u32[]{:S(2)}, u32[]{:S(2)}) collective-permute-start(bf16[144,256]{1,0:T(8,128)(2,1)S(1)} %get-tuple-element.78), channel_id=1, source_target_pairs={{0,1},{1,2},{2,3},{3,0},{4,5},{5,6},{6,7},{7,4},{8,9},{9,10},{10,1... | collective-permute-start | bytes 221192 | tf_op jit(solution)/shard_map/ppermute | solution.py:621
  109.0 4.5 %collective-permute-done.23.refs_2_ = bf16[144,256]{1,0:T(8,128)(2,1)S(1)} collective-permute-done((bf16[144,256]{1,0:T(8,128)(2,1)S(1)}, bf16[144,256]{1,0:T(8,128)(2,1)S(1)}, u32[]{:S(2)}, u32[]{:S(2)}) %collective-permute-start.23) | collective-permute-done | bytes 73760 | tf_op jit(solution)/shard_map/ppermute | solution.py:621
  114.9 2.2 %collective-permute-start.25 = (bf16[64,128]{1,0:T(8,128)(2,1)S(1)}, bf16[64,128]{1,0:T(8,128)(2,1)S(1)}, u32[]{:S(2)}, u32[]{:S(2)}) collective-permute-start(bf16[64,128]{1,0:T(8,128)(2,1)S(1)} %get-tuple-element.79), channel_id=1, source_target_pairs={{0,8},{1,9},{2,10},{3,11},{8,16},{9,17},{10,18},{11,19},{16,24},{1... | collective-permute-start | bytes 49160 | tf_op jit(solution)/shard_map/ppermute | solution.py:629
  117.1 3.4 %collective-permute-start.26 = (bf16[64,128]{1,0:T(8,128)(2,1)S(1)}, bf16[64,128]{1,0:T(8,128)(2,1)S(1)}, u32[]{:S(2)}, u32[]{:S(2)}) collective-permute-start(bf16[64,128]{1,0:T(8,128)(2,1)S(1)} %get-tuple-element.79), channel_id=1, source_target_pairs={{0,9},{1,10},{2,11},{3,8},{8,17},{9,18},{10,19},{11,16},{16,25},{1... | collective-permute-start | bytes 49160 | tf_op jit(solution)/shard_map/ppermute | solution.py:629
  120.5 1.5 collective-permute-start.27
  122.3 1.6 %collective-permute-start.28 = (bf16[64,128]{1,0:T(8,128)(2,1)S(1)}, bf16[64,128]{1,0:T(8,128)(2,1)S(1)}, u32[]{:S(2)}, u32[]{:S(2)}) collective-permute-start(bf16[64,128]{1,0:T(8,128)(2,1)S(1)} %get-tuple-element.79), channel_id=1, source_target_pairs={{0,11},{1,8},{2,9},{3,10},{8,19},{9,16},{10,17},{11,18},{16,27},{1... | collective-permute-start | bytes 49160 | tf_op jit(solution)/shard_map/ppermute | solution.py:629
  124.0 1.5 collective-permute-done.27.refs_2_
  125.4 1.6 %collective-permute-done.28.refs_3_ = bf16[64,128]{1,0:T(8,128)(2,1)S(1)} collective-permute-done((bf16[64,128]{1,0:T(8,128)(2,1)S(1)}, bf16[64,128]{1,0:T(8,128)(2,1)S(1)}, u32[]{:S(2)}, u32[]{:S(2)}) %collective-permute-start.28) | collective-permute-done | bytes 16416 | tf_op jit(solution)/shard_map/ppermute | solution.py:629
  127.7 3.3 %collective-permute-start.30 = (bf16[144,256]{1,0:T(8,128)(2,1)S(1)}, bf16[144,256]{1,0:T(8,128)(2,1)S(1)}, u32[]{:S(2)}, u32[]{:S(2)}) collective-permute-start(bf16[144,256]{1,0:T(8,128)(2,1)S(1)} %get-tuple-element.83), channel_id=1, source_target_pairs={{0,3},{1,0},{2,1},{3,2},{4,7},{5,4},{6,5},{7,6},{8,11},{9,8},{10,9... | collective-permute-start | bytes 221192 | tf_op jit(solution)/shard_map/ppermute | solution.py:621
  132.2 1.3 collective-permute-done.30.refs_1_
  133.5 3.9 %collective-permute-done.31.refs_2_ = bf16[144,256]{1,0:T(8,128)(2,1)S(1)} collective-permute-done((bf16[144,256]{1,0:T(8,128)(2,1)S(1)}, bf16[144,256]{1,0:T(8,128)(2,1)S(1)}, u32[]{:S(2)}, u32[]{:S(2)}) %collective-permute-start.31) | collective-permute-done | bytes 73760 | tf_op jit(solution)/shard_map/ppermute | solution.py:621
  137.4 2.4 %collective-permute-start.33 = (bf16[128,2048]{1,0:T(8,128)(2,1)S(1)}, bf16[128,2048]{1,0:T(8,128)(2,1)}, u32[]{:S(2)}, u32[]{:S(2)}) collective-permute-start(bf16[128,2048]{1,0:T(8,128)(2,1)S(1)} %get-tuple-element.86.refs_5_), channel_id=1, source_target_pairs={{0,24},{1,25},{2,26},{3,27},{8,0},{9,1},{10,2},{11,3},{16,8},{17,9... | collective-permute-start | bytes 1572872 | tf_op jit(solution)/shard_map/ppermute | solution.py:629
  139.7 1.2 section_3.1
  141.5 1.5 collective-permute-start.38
  143.0 2.7 %collective-permute-done.38.spot_ref = s32[16,128]{1,0:T(8,128)S(1)} collective-permute-done((s32[16,128]{1,0:T(8,128)S(1)}, s32[16,128]{1,0:T(8,128)S(1)}, u32[]{:S(2)}, u32[]{:S(2)}) %collective-permute-start.38) | collective-permute-done | bytes 8224 | tf_op jit(solution)/shard_map/ppermute | solution.py:637
  145.7 2.6 %collective-permute-start.34 = (bf16[64,128]{1,0:T(8,128)(2,1)}, bf16[64,128]{1,0:T(8,128)(2,1)S(1)}, u32[]{:S(2)}, u32[]{:S(2)}) collective-permute-start(bf16[64,128]{1,0:T(8,128)(2,1)} %get-tuple-element.89.refs_0_), channel_id=1, source_target_pairs={{0,1},{1,2},{2,3},{3,0},{4,5},{5,6},{6,7},{7,4},{8,9},{9,10},{10,1... | collective-permute-start | bytes 49160 | tf_op jit(solution)/shard_map/ppermute | solution.py:621
  148.3 1.2 collective-permute-start.35
  149.4 1.5 collective-permute-start.36
  151.6 1.5 insert_new.1
  153.4 1.9 %section_result.1 = bf16[1,128,2048]{2,1,0:T(8,128)(2,1)} custom-call(s32[4]{0:T(128)S(1)} %pad_add_fusion.sec_ref, bf16[128,2048]{1,0:T(8,128)(2,1)} %collective-permute-done.33.back_ref, bf16[64,128]{1,0:T(8,128)(2,1)} %get-tuple-element.89.refs_0_, bf16[64,128]{1,0:T(8,128)(2,1)S(1)} %collective-permute-done.34.refs_1_, ...), custom_call_target="tpu_custom_call" | custom-call | bytes 9000000 | tf_op jit(solution)/shard_map/section_result/pallas_call | solution.py:556
  (86 shorter events, 13.3 us)
Async XLA Ops:
  1.8 33.6 %copy-start.6 = (bf16[1,4,64,2048]{3,2,1,0:T(8,128)(2,1)S(1)}, bf16[1,4,64,2048]{3,2,1,0:T(8,128)(2,1)}, u32[]{:S(2)}) copy-start(bf16[1,4,64,2048]{3,2,1,0:T(8,128)(2,1)} %param.17) | copy-start | bytes 3145732
  3.6 18.0 %collective-permute-start = (bf16[2048,128]{1,0:T(8,128)(2,1)}, bf16[2048,128]{1,0:T(8,128)(2,1)S(1)}, u32[]{:S(2)}, u32[]{:S(2)}) collective-permute-start(bf16[2048,128]{1,0:T(8,128)(2,1)} %get-tuple-element.49), channel_id=1, source_target_pairs={{0,1},{1,2},{2,3},{3,0},{4,5},{5,6},{6,7},{7,4},{8,9},{9,10},{10,1... | collective-permute-start | bytes 1572872 | tf_op jit(solution)/shard_map/ppermute | solution.py:621
  6.7 26.0 %collective-permute-start.2 = (bf16[2048,128]{1,0:T(8,128)(2,1)}, bf16[2048,128]{1,0:T(8,128)(2,1)S(1)}, u32[]{:S(2)}, u32[]{:S(2)}) collective-permute-start(bf16[2048,128]{1,0:T(8,128)(2,1)} %get-tuple-element.51), channel_id=1, source_target_pairs={{0,3},{1,0},{2,1},{3,2},{4,7},{5,4},{6,5},{7,6},{8,11},{9,8},{10,9... | collective-permute-start | bytes 1572872 | tf_op jit(solution)/shard_map/ppermute | solution.py:621
  8.8 28.0 %collective-permute-start.3 = (bf16[256,1024]{1,0:T(8,128)(2,1)}, bf16[256,1024]{1,0:T(8,128)(2,1)}, u32[]{:S(2)}, u32[]{:S(2)}) collective-permute-start(bf16[256,1024]{1,0:T(8,128)(2,1)} %bitcast.7.refs_12_.refs_10_), channel_id=1, source_target_pairs={{0,4},{4,0},{8,12},{12,8},{16,20},{20,16},{24,28},{28,24},{1,5},{5... | collective-permute-start | bytes 1572872 | tf_op jit(solution)/shard_map/ppermute | solution.py:637
  21.6 38.3 %copy-start.3 = (bf16[2048,128]{1,0:T(8,128)(2,1)}, bf16[2048,128]{1,0:T(8,128)(2,1)S(1)}, u32[]{:S(2)}) copy-start(bf16[2048,128]{1,0:T(8,128)(2,1)S(1)} %collective-permute-done.refs_1_) | copy-start | bytes 1572868
  21.6 25.9 %collective-permute-start.4 = (bf16[2048,128]{1,0:T(8,128)(2,1)S(1)}, bf16[2048,128]{1,0:T(8,128)(2,1)S(1)}, u32[]{:S(2)}, u32[]{:S(2)}) collective-permute-start(bf16[2048,128]{1,0:T(8,128)(2,1)S(1)} %collective-permute-done.refs_1_), channel_id=1, source_target_pairs={{8,12},{12,8},{16,20},{20,16},{24,28},{28,24},{9,13},{13,9},{17,21... | collective-permute-start | bytes 1572872 | tf_op jit(solution)/shard_map/ppermute | solution.py:637
  32.6 27.3 %copy-start.4 = (bf16[2048,128]{1,0:T(8,128)(2,1)}, bf16[2048,128]{1,0:T(8,128)(2,1)S(1)}, u32[]{:S(2)}) copy-start(bf16[2048,128]{1,0:T(8,128)(2,1)S(1)} %collective-permute-done.2.refs_3_) | copy-start | bytes 1572868
  32.6 14.9 %collective-permute-start.5 = (bf16[2048,128]{1,0:T(8,128)(2,1)S(1)}, bf16[2048,128]{1,0:T(8,128)(2,1)S(1)}, u32[]{:S(2)}, u32[]{:S(2)}) collective-permute-start(bf16[2048,128]{1,0:T(8,128)(2,1)S(1)} %collective-permute-done.2.refs_3_), channel_id=1, source_target_pairs={{8,12},{12,8},{16,20},{20,16},{24,28},{28,24},{9,13},{13,9},{17,21... | collective-permute-start | bytes 1572872 | tf_op jit(solution)/shard_map/ppermute | solution.py:637
  33.3 26.6 %collective-permute-start.1 = (bf16[2048,128]{1,0:T(8,128)(2,1)S(1)}, bf16[2048,128]{1,0:T(8,128)(2,1)S(1)}, u32[]{:S(2)}, u32[]{:S(2)}) collective-permute-start(bf16[2048,128]{1,0:T(8,128)(2,1)S(1)} %get-tuple-element.50), channel_id=1, source_target_pairs={{0,2},{1,3},{2,0},{3,1},{4,6},{5,7},{6,4},{7,5},{8,10},{9,11},{10,... | collective-permute-start | bytes 1572872 | tf_op jit(solution)/shard_map/ppermute | solution.py:621
  35.4 24.5 %copy-start.1 = (bf16[128,2048]{1,0:T(8,128)(2,1)S(1)}, bf16[128,2048]{1,0:T(8,128)(2,1)}, u32[]{:S(2)}) copy-start(bf16[128,2048]{1,0:T(8,128)(2,1)} %refs_9_.1) | copy-start | bytes 1572868
  35.4 24.5 %copy-start.7 = (bf16[1,8192]{1,0:T(2,128)(2,1)S(1)}, bf16[1,8192]{1,0:T(2,128)(2,1)}, u32[]{:S(2)}) copy-start(bf16[1,8192]{1,0:T(2,128)(2,1)} %refs_5_.7) | copy-start | bytes 49156
  35.4 38.1 %collective-permute-start.11 = (bf16[256,2048]{1,0:T(8,128)(2,1)S(1)}, bf16[256,2048]{1,0:T(8,128)(2,1)S(1)}, u32[]{:S(2)}, u32[]{:S(2)}) collective-permute-start(bf16[256,2048]{1,0:T(8,128)(2,1)S(1)} %bitcast.14), channel_id=1, source_target_pairs={{0,8},{1,9},{2,10},{3,11},{8,16},{9,17},{10,18},{11,19},{16,24},{1... | collective-permute-start | bytes 3145736 | tf_op jit(solution)/shard_map/ppermute | solution.py:629
  36.8 38.0 %collective-permute-start.12 = (bf16[256,2048]{1,0:T(8,128)(2,1)S(1)}, bf16[256,2048]{1,0:T(8,128)(2,1)S(1)}, u32[]{:S(2)}, u32[]{:S(2)}) collective-permute-start(bf16[256,2048]{1,0:T(8,128)(2,1)S(1)} %bitcast.15), channel_id=1, source_target_pairs={{0,12},{4,8},{1,13},{5,9},{2,14},{6,10},{3,15},{7,11}} | collective-permute-start | bytes 3145736 | tf_op jit(solution)/shard_map/ppermute | solution.py:637
  47.5 18.0 %copy-start.11 = (bf16[2048,128]{1,0:T(8,128)(2,1)}, bf16[2048,128]{1,0:T(8,128)(2,1)S(1)}, u32[]{:S(2)}) copy-start(bf16[2048,128]{1,0:T(8,128)(2,1)S(1)} %collective-permute-done.4.refs_2_) | copy-start | bytes 1572868
  47.5 18.0 %copy-start.12 = (bf16[2048,128]{1,0:T(8,128)(2,1)}, bf16[2048,128]{1,0:T(8,128)(2,1)S(1)}, u32[]{:S(2)}) copy-start(bf16[2048,128]{1,0:T(8,128)(2,1)S(1)} %collective-permute-done.5.refs_4_) | copy-start | bytes 1572868
  65.5 10.6 %collective-permute-start.10 = (bf16[2048,128]{1,0:T(8,128)(2,1)S(1)}, bf16[2048,128]{1,0:T(8,128)(2,1)S(1)}, u32[]{:S(2)}, u32[]{:S(2)}) collective-permute-start(bf16[2048,128]{1,0:T(8,128)(2,1)S(1)} %collective-permute-done.1.refs_2_.refs_0_), channel_id=1, source_target_pairs={{8,12},{12,8},{16,20},{20,16},{24,28},{28,24},{9,13},{13,9},{17,21... | collective-permute-start | bytes 1572872 | tf_op jit(solution)/shard_map/ppermute | solution.py:637
  66.9 37.2 %collective-permute-start.21 = (bf16[256,2048]{1,0:T(8,128)(2,1)S(1)}, bf16[256,2048]{1,0:T(8,128)(2,1)S(1)}, u32[]{:S(2)}, u32[]{:S(2)}) collective-permute-start(bf16[256,2048]{1,0:T(8,128)(2,1)S(1)} %bitcast.16), channel_id=1, source_target_pairs={{8,20},{12,16},{16,28},{20,24},{9,21},{13,17},{17,29},{21,25},{10,... | collective-permute-start | bytes 3145736 | tf_op jit(solution)/shard_map/ppermute | solution.py:637
  67.6 11.7 %collective-permute-start.6 = (bf16[64,128]{1,0:T(8,128)(2,1)S(1)}, bf16[64,128]{1,0:T(8,128)(2,1)S(1)}, u32[]{:S(2)}, u32[]{:S(2)}) collective-permute-start(bf16[64,128]{1,0:T(8,128)(2,1)S(1)} %get-tuple-element.62), channel_id=1, source_target_pairs={{0,8},{1,9},{2,10},{3,11},{4,12},{5,13},{6,14},{7,15}} | collective-permute-start | bytes 49160 | tf_op jit(solution)/shard_map/ppermute | solution.py:629
  73.5 5.8 %collective-permute-start.7 = (bf16[64,128]{1,0:T(8,128)(2,1)S(1)}, bf16[64,128]{1,0:T(8,128)(2,1)S(1)}, u32[]{:S(2)}, u32[]{:S(2)}) collective-permute-start(bf16[64,128]{1,0:T(8,128)(2,1)S(1)} %get-tuple-element.62), channel_id=1, source_target_pairs={{0,9},{1,10},{2,11},{3,8},{4,13},{5,14},{6,15},{7,12}} | collective-permute-start | bytes 49160 | tf_op jit(solution)/shard_map/ppermute | solution.py:629
  74.8 4.5 %collective-permute-start.8 = (bf16[64,128]{1,0:T(8,128)(2,1)S(1)}, bf16[64,128]{1,0:T(8,128)(2,1)S(1)}, u32[]{:S(2)}, u32[]{:S(2)}) collective-permute-start(bf16[64,128]{1,0:T(8,128)(2,1)S(1)} %get-tuple-element.62), channel_id=1, source_target_pairs={{0,10},{1,11},{2,8},{3,9},{4,14},{5,15},{6,12},{7,13}} | collective-permute-start | bytes 49160 | tf_op jit(solution)/shard_map/ppermute | solution.py:629
  76.1 4.0 %collective-permute-start.9 = (bf16[64,128]{1,0:T(8,128)(2,1)S(1)}, bf16[64,128]{1,0:T(8,128)(2,1)S(1)}, u32[]{:S(2)}, u32[]{:S(2)}) collective-permute-start(bf16[64,128]{1,0:T(8,128)(2,1)S(1)} %get-tuple-element.62), channel_id=1, source_target_pairs={{0,11},{1,8},{2,9},{3,10},{4,15},{5,12},{6,13},{7,14}} | collective-permute-start | bytes 49160 | tf_op jit(solution)/shard_map/ppermute | solution.py:629
  80.7 4.4 %collective-permute-start.13 = (bf16[144,256]{1,0:T(8,128)(2,1)S(1)}, bf16[144,256]{1,0:T(8,128)(2,1)S(1)}, u32[]{:S(2)}, u32[]{:S(2)}) collective-permute-start(bf16[144,256]{1,0:T(8,128)(2,1)S(1)} %get-tuple-element.67), channel_id=1, source_target_pairs={{0,3},{1,0},{2,1},{3,2},{4,7},{5,4},{6,5},{7,6},{8,11},{9,8},{10,9... | collective-permute-start | bytes 221192 | tf_op jit(solution)/shard_map/ppermute | solution.py:621
  82.9 8.3 %collective-permute-start.14 = (bf16[144,256]{1,0:T(8,128)(2,1)S(1)}, bf16[144,256]{1,0:T(8,128)(2,1)S(1)}, u32[]{:S(2)}, u32[]{:S(2)}) collective-permute-start(bf16[144,256]{1,0:T(8,128)(2,1)S(1)} %get-tuple-element.68), channel_id=1, source_target_pairs={{0,2},{1,3},{2,0},{3,1},{4,6},{5,7},{6,4},{7,5},{8,10},{9,11},{10,... | collective-permute-start | bytes 221192 | tf_op jit(solution)/shard_map/ppermute | solution.py:621
  82.9 8.3 %collective-permute-start.15 = (bf16[144,256]{1,0:T(8,128)(2,1)S(1)}, bf16[144,256]{1,0:T(8,128)(2,1)S(1)}, u32[]{:S(2)}, u32[]{:S(2)}) collective-permute-start(bf16[144,256]{1,0:T(8,128)(2,1)S(1)} %get-tuple-element.69), channel_id=1, source_target_pairs={{0,1},{1,2},{2,3},{3,0},{4,5},{5,6},{6,7},{7,4},{8,9},{9,10},{10,1... | collective-permute-start | bytes 221192 | tf_op jit(solution)/shard_map/ppermute | solution.py:621
  91.2 12.9 %collective-permute-start.20 = (bf16[128,2048]{1,0:T(8,128)(2,1)S(1)}, bf16[128,2048]{1,0:T(8,128)(2,1)S(1)}, u32[]{:S(2)}, u32[]{:S(2)}) collective-permute-start(bf16[128,2048]{1,0:T(8,128)(2,1)S(1)} %get-tuple-element.73.refs_9_), channel_id=1, source_target_pairs={{0,8},{1,9},{2,10},{3,11},{8,16},{9,17},{10,18},{11,19},{16,24},{1... | collective-permute-start | bytes 1572872 | tf_op jit(solution)/shard_map/ppermute | solution.py:629
  92.2 7.8 %collective-permute-start.16 = (bf16[64,128]{1,0:T(8,128)(2,1)S(1)}, bf16[64,128]{1,0:T(8,128)(2,1)S(1)}, u32[]{:S(2)}, u32[]{:S(2)}) collective-permute-start(bf16[64,128]{1,0:T(8,128)(2,1)S(1)} %get-tuple-element.71), channel_id=1, source_target_pairs={{0,8},{1,9},{2,10},{3,11},{8,16},{9,17},{10,18},{11,19},{16,24},{1... | collective-permute-start | bytes 49160 | tf_op jit(solution)/shard_map/ppermute | solution.py:629
  96.2 5.9 %collective-permute-start.17 = (bf16[64,128]{1,0:T(8,128)(2,1)S(1)}, bf16[64,128]{1,0:T(8,128)(2,1)S(1)}, u32[]{:S(2)}, u32[]{:S(2)}) collective-permute-start(bf16[64,128]{1,0:T(8,128)(2,1)S(1)} %get-tuple-element.71), channel_id=1, source_target_pairs={{0,9},{1,10},{2,11},{3,8},{8,17},{9,18},{10,19},{11,16},{16,25},{1... | collective-permute-start | bytes 49160 | tf_op jit(solution)/shard_map/ppermute | solution.py:629
  96.2 5.9 %collective-permute-start.18 = (bf16[64,128]{1,0:T(8,128)(2,1)S(1)}, bf16[64,128]{1,0:T(8,128)(2,1)S(1)}, u32[]{:S(2)}, u32[]{:S(2)}) collective-permute-start(bf16[64,128]{1,0:T(8,128)(2,1)S(1)} %get-tuple-element.71), channel_id=1, source_target_pairs={{0,10},{1,11},{2,8},{3,9},{8,18},{9,19},{10,16},{11,17},{16,26},{1... | collective-permute-start | bytes 49160 | tf_op jit(solution)/shard_map/ppermute | solution.py:629
  100.0 4.1 %collective-permute-start.19 = (bf16[64,128]{1,0:T(8,128)(2,1)S(1)}, bf16[64,128]{1,0:T(8,128)(2,1)S(1)}, u32[]{:S(2)}, u32[]{:S(2)}) collective-permute-start(bf16[64,128]{1,0:T(8,128)(2,1)S(1)} %get-tuple-element.71), channel_id=1, source_target_pairs={{0,11},{1,8},{2,9},{3,10},{8,19},{9,16},{10,17},{11,18},{16,27},{1... | collective-permute-start | bytes 49160 | tf_op jit(solution)/shard_map/ppermute | solution.py:629
  104.6 4.4 %collective-permute-start.22 = (bf16[144,256]{1,0:T(8,128)(2,1)S(1)}, bf16[144,256]{1,0:T(8,128)(2,1)S(1)}, u32[]{:S(2)}, u32[]{:S(2)}) collective-permute-start(bf16[144,256]{1,0:T(8,128)(2,1)S(1)} %get-tuple-element.76), channel_id=1, source_target_pairs={{0,3},{1,0},{2,1},{3,2},{4,7},{5,4},{6,5},{7,6},{8,11},{9,8},{10,9... | collective-permute-start | bytes 221192 | tf_op jit(solution)/shard_map/ppermute | solution.py:621
  106.4 7.2 %collective-permute-start.23 = (bf16[144,256]{1,0:T(8,128)(2,1)S(1)}, bf16[144,256]{1,0:T(8,128)(2,1)S(1)}, u32[]{:S(2)}, u32[]{:S(2)}) collective-permute-start(bf16[144,256]{1,0:T(8,128)(2,1)S(1)} %get-tuple-element.77), channel_id=1, source_target_pairs={{0,2},{1,3},{2,0},{3,1},{4,6},{5,7},{6,4},{7,5},{8,10},{9,11},{10,... | collective-permute-start | bytes 221192 | tf_op jit(solution)/shard_map/ppermute | solution.py:621
  106.5 7.1 %collective-permute-start.24 = (bf16[144,256]{1,0:T(8,128)(2,1)S(1)}, bf16[144,256]{1,0:T(8,128)(2,1)S(1)}, u32[]{:S(2)}, u32[]{:S(2)}) collective-permute-start(bf16[144,256]{1,0:T(8,128)(2,1)S(1)} %get-tuple-element.78), channel_id=1, source_target_pairs={{0,1},{1,2},{2,3},{3,0},{4,5},{5,6},{6,7},{7,4},{8,9},{9,10},{10,1... | collective-permute-start | bytes 221192 | tf_op jit(solution)/shard_map/ppermute | solution.py:621
  113.6 13.5 %collective-permute-start.29 = (bf16[128,2048]{1,0:T(8,128)(2,1)S(1)}, bf16[128,2048]{1,0:T(8,128)(2,1)S(1)}, u32[]{:S(2)}, u32[]{:S(2)}) collective-permute-start(bf16[128,2048]{1,0:T(8,128)(2,1)S(1)} %get-tuple-element.81.refs_9_), channel_id=1, source_target_pairs={{0,8},{1,9},{2,10},{3,11},{8,16},{9,17},{10,18},{11,19},{16,24},{1... | collective-permute-start | bytes 1572872 | tf_op jit(solution)/shard_map/ppermute | solution.py:629
  113.6 39.5 %collective-permute-start.37 = (bf16[256,2048]{1,0:T(8,128)(2,1)S(1)}, bf16[256,2048]{1,0:T(8,128)(2,1)S(1)}, u32[]{:S(2)}, u32[]{:S(2)}) collective-permute-start(bf16[256,2048]{1,0:T(8,128)(2,1)S(1)} %bitcast.17), channel_id=1, source_target_pairs={{24,28},{28,24},{25,29},{29,25},{26,30},{30,26},{27,31},{31,27}} | collective-permute-start | bytes 3145736 | tf_op jit(solution)/shard_map/ppermute | solution.py:637
  114.9 7.5 %collective-permute-start.25 = (bf16[64,128]{1,0:T(8,128)(2,1)S(1)}, bf16[64,128]{1,0:T(8,128)(2,1)S(1)}, u32[]{:S(2)}, u32[]{:S(2)}) collective-permute-start(bf16[64,128]{1,0:T(8,128)(2,1)S(1)} %get-tuple-element.79), channel_id=1, source_target_pairs={{0,8},{1,9},{2,10},{3,11},{8,16},{9,17},{10,18},{11,19},{16,24},{1... | collective-permute-start | bytes 49160 | tf_op jit(solution)/shard_map/ppermute | solution.py:629
  117.1 6.9 %collective-permute-start.26 = (bf16[64,128]{1,0:T(8,128)(2,1)S(1)}, bf16[64,128]{1,0:T(8,128)(2,1)S(1)}, u32[]{:S(2)}, u32[]{:S(2)}) collective-permute-start(bf16[64,128]{1,0:T(8,128)(2,1)S(1)} %get-tuple-element.79), channel_id=1, source_target_pairs={{0,9},{1,10},{2,11},{3,8},{8,17},{9,18},{10,19},{11,16},{16,25},{1... | collective-permute-start | bytes 49160 | tf_op jit(solution)/shard_map/ppermute | solution.py:629
  120.5 5.0 %collective-permute-start.27 = (bf16[64,128]{1,0:T(8,128)(2,1)S(1)}, bf16[64,128]{1,0:T(8,128)(2,1)S(1)}, u32[]{:S(2)}, u32[]{:S(2)}) collective-permute-start(bf16[64,128]{1,0:T(8,128)(2,1)S(1)} %get-tuple-element.79), channel_id=1, source_target_pairs={{0,10},{1,11},{2,8},{3,9},{8,18},{9,19},{10,16},{11,17},{16,26},{1... | collective-permute-start | bytes 49160 | tf_op jit(solution)/shard_map/ppermute | solution.py:629
  122.3 4.7 %collective-permute-start.28 = (bf16[64,128]{1,0:T(8,128)(2,1)S(1)}, bf16[64,128]{1,0:T(8,128)(2,1)S(1)}, u32[]{:S(2)}, u32[]{:S(2)}) collective-permute-start(bf16[64,128]{1,0:T(8,128)(2,1)S(1)} %get-tuple-element.79), channel_id=1, source_target_pairs={{0,11},{1,8},{2,9},{3,10},{8,19},{9,16},{10,17},{11,18},{16,27},{1... | collective-permute-start | bytes 49160 | tf_op jit(solution)/shard_map/ppermute | solution.py:629
  127.7 5.8 %collective-permute-start.30 = (bf16[144,256]{1,0:T(8,128)(2,1)S(1)}, bf16[144,256]{1,0:T(8,128)(2,1)S(1)}, u32[]{:S(2)}, u32[]{:S(2)}) collective-permute-start(bf16[144,256]{1,0:T(8,128)(2,1)S(1)} %get-tuple-element.83), channel_id=1, source_target_pairs={{0,3},{1,0},{2,1},{3,2},{4,7},{5,4},{6,5},{7,6},{8,11},{9,8},{10,9... | collective-permute-start | bytes 221192 | tf_op jit(solution)/shard_map/ppermute | solution.py:621
  131.0 6.4 %collective-permute-start.31 = (bf16[144,256]{1,0:T(8,128)(2,1)S(1)}, bf16[144,256]{1,0:T(8,128)(2,1)S(1)}, u32[]{:S(2)}, u32[]{:S(2)}) collective-permute-start(bf16[144,256]{1,0:T(8,128)(2,1)S(1)} %get-tuple-element.84), channel_id=1, source_target_pairs={{0,2},{1,3},{2,0},{3,1},{4,6},{5,7},{6,4},{7,5},{8,10},{9,11},{10,... | collective-permute-start | bytes 221192 | tf_op jit(solution)/shard_map/ppermute | solution.py:621
  131.0 6.4 %collective-permute-start.32 = (bf16[144,256]{1,0:T(8,128)(2,1)S(1)}, bf16[144,256]{1,0:T(8,128)(2,1)S(1)}, u32[]{:S(2)}, u32[]{:S(2)}) collective-permute-start(bf16[144,256]{1,0:T(8,128)(2,1)S(1)} %get-tuple-element.85), channel_id=1, source_target_pairs={{0,1},{1,2},{2,3},{3,0},{4,5},{5,6},{6,7},{7,4},{8,9},{9,10},{10,1... | collective-permute-start | bytes 221192 | tf_op jit(solution)/shard_map/ppermute | solution.py:621
  131.6 16.6 %collective-permute-start.40 = (bf16[16,2,64,128]{3,2,1,0:T(8,128)(2,1)S(1)}, bf16[16,2,64,128]{3,2,1,0:T(8,128)(2,1)S(1)}, u32[]{:S(2)}, u32[]{:S(2)}) collective-permute-start(bf16[16,2,64,128]{3,2,1,0:T(8,128)(2,1)S(1)} %get-tuple-element.94), channel_id=1, source_target_pairs={{0,4},{4,0},{8,12},{12,8},{16,20},{20,16},{24,28},{28,24},{1,5},{5... | collective-permute-start | bytes 1572872 | tf_op jit(solution)/shard_map/ppermute | solution.py:637
  137.4 16.0 %collective-permute-start.33 = (bf16[128,2048]{1,0:T(8,128)(2,1)S(1)}, bf16[128,2048]{1,0:T(8,128)(2,1)}, u32[]{:S(2)}, u32[]{:S(2)}) collective-permute-start(bf16[128,2048]{1,0:T(8,128)(2,1)S(1)} %get-tuple-element.86.refs_5_), channel_id=1, source_target_pairs={{0,24},{1,25},{2,26},{3,27},{8,0},{9,1},{10,2},{11,3},{16,8},{17,9... | collective-permute-start | bytes 1572872 | tf_op jit(solution)/shard_map/ppermute | solution.py:629
  140.9 8.5 %collective-permute-start.39 = (bf16[128,256]{1,0:T(8,128)(2,1)S(1)}, bf16[128,256]{1,0:T(8,128)(2,1)S(1)}, u32[]{:S(2)}, u32[]{:S(2)}) collective-permute-start(bf16[128,256]{1,0:T(8,128)(2,1)S(1)} %get-tuple-element.91), channel_id=1, source_target_pairs={{0,4},{4,0},{8,12},{12,8},{16,20},{20,16},{24,28},{28,24},{1,5},{5... | collective-permute-start | bytes 196616 | tf_op jit(solution)/shard_map/ppermute | solution.py:637
  141.5 4.2 %collective-permute-start.38 = (s32[16,128]{1,0:T(8,128)S(1)}, s32[16,128]{1,0:T(8,128)S(1)}, u32[]{:S(2)}, u32[]{:S(2)}) collective-permute-start(s32[16,128]{1,0:T(8,128)S(1)} %get-tuple-element.92), channel_id=1, source_target_pairs={{0,4},{4,0},{8,12},{12,8},{16,20},{20,16},{24,28},{28,24},{1,5},{5... | collective-permute-start | bytes 24584 | tf_op jit(solution)/shard_map/ppermute | solution.py:637
  145.7 7.4 %collective-permute-start.34 = (bf16[64,128]{1,0:T(8,128)(2,1)}, bf16[64,128]{1,0:T(8,128)(2,1)S(1)}, u32[]{:S(2)}, u32[]{:S(2)}) collective-permute-start(bf16[64,128]{1,0:T(8,128)(2,1)} %get-tuple-element.89.refs_0_), channel_id=1, source_target_pairs={{0,1},{1,2},{2,3},{3,0},{4,5},{5,6},{6,7},{7,4},{8,9},{9,10},{10,1... | collective-permute-start | bytes 49160 | tf_op jit(solution)/shard_map/ppermute | solution.py:621
  148.3 4.8 %collective-permute-start.35 = (bf16[64,128]{1,0:T(8,128)(2,1)}, bf16[64,128]{1,0:T(8,128)(2,1)S(1)}, u32[]{:S(2)}, u32[]{:S(2)}) collective-permute-start(bf16[64,128]{1,0:T(8,128)(2,1)} %get-tuple-element.89.refs_0_), channel_id=1, source_target_pairs={{0,2},{1,3},{2,0},{3,1},{4,6},{5,7},{6,4},{7,5},{8,10},{9,11},{10,... | collective-permute-start | bytes 49160 | tf_op jit(solution)/shard_map/ppermute | solution.py:621
  149.4 4.0 %collective-permute-start.36 = (bf16[64,128]{1,0:T(8,128)(2,1)}, bf16[64,128]{1,0:T(8,128)(2,1)S(1)}, u32[]{:S(2)}, u32[]{:S(2)}) collective-permute-start(bf16[64,128]{1,0:T(8,128)(2,1)} %get-tuple-element.89.refs_0_), channel_id=1, source_target_pairs={{0,3},{1,0},{2,1},{3,2},{4,7},{5,4},{6,5},{7,6},{8,11},{9,8},{10,9... | collective-permute-start | bytes 49160 | tf_op jit(solution)/shard_map/ppermute | solution.py:621
  (9 other events, 68.6 us)

commit v4 on v3

--- a/solution.py
+++ b/solution.py
@@ -142,8 +142,9 @@
     move_ref,
     q_ref,
     pages_ref,
-    acc_ref,
-    lse_ref,
+    acc_out,
+    lse_out,
+    line_ref,
     slot_ref,
     cos_ref,
     sin_ref,
@@ -151,6 +152,8 @@
     spot_ref,
     buf,
     place,
+    acc_ref,
+    lse_ref,
     sems,
     leave_sem,
 ):
@@ -248,6 +251,10 @@
         return 0
 
     lax.fori_loop(0, reqs // per, group, 0, unroll=2)
+    for h in range(heads):
+        acc_out[h] = jnp.transpose(acc_ref[h])
+    lse_out[...] = jnp.transpose(lse_ref[...])[:heads]
+    line_ref[...] = jnp.transpose(slot_ref[...].astype(jnp.float32))[:8]
     pltpu.make_async_copy(leave_ref, leave_ref, leave_sem).wait()
 
 
@@ -260,10 +267,11 @@
     return pl.pallas_call(
         functools.partial(local_kernel, paired, adapters),
         in_specs=[SM] * 6 + [VM, ANY],
-        out_specs=(VM,) * 7,
+        out_specs=(VM,) * 8,
         out_shape=(
-            kept((heads, tokens, HD), jnp.float32),
-            kept(square, jnp.float32),
+            kept((heads, HD, tokens), jnp.float32),
+            kept((heads, tokens), jnp.float32),
+            kept((8, tokens), jnp.float32),
             kept(square, jnp.int32),
             kept(square, jnp.float32),
             kept(square, jnp.float32),
@@ -273,6 +281,8 @@
         scratch_shapes=[
             pltpu.VMEM(pages.shape, pages.dtype),
             pltpu.SMEM((pages.shape[0],), jnp.int32),
+            pltpu.VMEM((heads, tokens, HD), jnp.float32),
+            pltpu.VMEM(square, jnp.float32),
             pltpu.SemaphoreType.DMA((groups,)),
             pltpu.SemaphoreType.DMA,
         ],
@@ -283,47 +293,44 @@
 
 
 def attend_new(proj_k, proj_v, refs, fresh_ref, low_ref, mixed_all, loads):
-    q_ref, cos_ref, sin_ref, acc_ref, lse_ref, slot_ref, a_refs = refs
+    q_ref, cos_ref, sin_ref, acc_ref, lse_ref, slot_ref, spot_ref, a_refs = refs
     tokens = proj_k.shape[0]
     heads = q_ref.shape[1] // HD
     keys = (proj_k * cos_ref[...] + pltpu.roll(proj_k, HD // 2, 1) * sin_ref[...]).astype(
         jnp.bfloat16
     )
     values = proj_v.astype(jnp.bfloat16)
-    fresh_ref[:, :HD] = keys
-    fresh_ref[:, HD:] = values
+    fresh_ref[:tokens, :HD] = keys
+    fresh_ref[:tokens, HD:] = values
+    spots = spot_ref[...].astype(jnp.float32).astype(jnp.bfloat16)
+    fresh_ref[tokens:, :HD] = spots
+    fresh_ref[tokens:, HD:] = jnp.zeros_like(spots)
+    values = jnp.transpose(values.astype(jnp.float32)).astype(jnp.bfloat16)
     rows = lax.broadcasted_iota(jnp.int32, (tokens, tokens), 0)
     cols = lax.broadcasted_iota(jnp.int32, (tokens, tokens), 1)
-    allowed = (rows // S == cols // S) & (cols <= rows)
+    allowed = (rows // S == cols // S) & (rows <= cols)
     for h in range(heads):
         span = slice(h * HD, (h + 1) * HD)
-        scores = lax.dot_general(q_ref[:, span], keys, NT, preferred_element_type=jnp.float32)
+        scores = lax.dot_general(keys, q_ref[:, span], NT, preferred_element_type=jnp.float32)
         scores = jnp.where(allowed, scores * SCALE, BIG)
-        lse = lse_ref[:, h : h + 1]
-        top = jnp.maximum(jnp.max(scores, axis=1, keepdims=True), lse)
+        lse = lse_ref[h : h + 1, :]
+        top = jnp.maximum(jnp.max(scores, axis=0, keepdims=True), lse)
         weights = jnp.exp(scores - top)
         old = jnp.exp(lse - top)
-        total = jnp.sum(weights, axis=1, keepdims=True) + old
-        mixed = jnp.dot(weights.astype(jnp.bfloat16), values, preferred_element_type=jnp.float32)
-        mixed_all[:, span] = ((mixed + old * acc_ref[h]) / total).astype(jnp.bfloat16)
-    slots = slot_ref[...]
-    half = lax.broadcasted_iota(jnp.int32, (tokens, HD), 1) // R
-    folded = jnp.zeros((tokens, HD), jnp.float32)
+        share = 1.0 / (jnp.sum(weights, axis=0, keepdims=True) + old)
+        weights = (weights * share).astype(jnp.bfloat16)
+        mixed = jnp.dot(values, weights, preferred_element_type=jnp.float32)
+        mixed_all[span, :] = (mixed + acc_ref[h] * (old * share)).astype(jnp.bfloat16)
+    slots = slot_ref[:1, :]
+    folded = jnp.zeros((R, tokens), jnp.float32)
     base = 0
     for a_ref, load in zip(a_refs, loads):
         load.wait()
-        low = lax.dot_general(
-            mixed_all[...], a_ref[...], NT, preferred_element_type=jnp.float32
-        )
-        for j in range(a_ref.shape[0] // HD):
-            folded = folded + jnp.where(
-                slots == base + 2 * j + half, low[:, j * HD : (j + 1) * HD], 0.0
-            )
+        low = jnp.dot(a_ref[...], mixed_all[...], preferred_element_type=jnp.float32)
+        for j in range(a_ref.shape[0] // R):
+            folded = folded + jnp.where(slots == float(base + j), low[j * R : (j + 1) * R], 0.0)
         base += a_ref.shape[0] // R
-    folded = folded + pltpu.roll(folded, R, 1)
-    low_ref[...] = jnp.where(
-        half[: tokens // 2] == 0, folded[: tokens // 2], folded[tokens // 2 :]
-    ).astype(jnp.bfloat16)
+    low_ref[...] = folded.astype(jnp.bfloat16)
 
 
 def start_loads(sources, targets, sems):
@@ -338,9 +345,9 @@
 
 def first_kernel(n_tp, n_a, sec_ref, *refs):
     h_refs, (w_ref, gain_ref) = refs[:n_tp], refs[n_tp : n_tp + 2]
-    shared = refs[n_tp + 2 : n_tp + 8]
-    a_refs = refs[n_tp + 8 : n_tp + 8 + n_a]
-    fresh_ref, low_ref, mixed_all, *a_bufs, sems = refs[n_tp + 8 + n_a :]
+    shared = refs[n_tp + 2 : n_tp + 9]
+    a_refs = refs[n_tp + 9 : n_tp + 9 + n_a]
+    fresh_ref, low_ref, mixed_all, *a_bufs, sems = refs[n_tp + 9 + n_a :]
     width = h_refs[0].shape[1]
 
     @pl.when(sec_ref[0] == 0)
@@ -353,7 +360,7 @@
             place = lax.rem(sec_ref[1] + n_tp - s, n_tp)
             lane = pl.multiple_of(place * width, width)
             row = pl.multiple_of(place * width, width)
-            if s == 0:
+            if h_refs[s].shape[1] == width:
                 h = h_refs[s][...]
             else:
                 h = jnp.concatenate(
@@ -373,9 +380,9 @@
 
 def later_kernel(section, n_tp, n_a, total_width, sec_ref, held_ref, *refs):
     m_refs = refs[:n_tp]
-    shared = refs[n_tp : n_tp + 6]
-    a_refs = refs[n_tp + 6 : n_tp + 6 + n_a]
-    fresh_ref, low_ref, mixed_all, *a_bufs, sems = refs[n_tp + 6 + n_a :]
+    shared = refs[n_tp : n_tp + 7]
+    a_refs = refs[n_tp + 7 : n_tp + 7 + n_a]
+    fresh_ref, low_ref, mixed_all, *a_bufs, sems = refs[n_tp + 7 + n_a :]
 
     @pl.when(sec_ref[0] != section)
     def _():
@@ -384,7 +391,7 @@
     @pl.when(sec_ref[0] == section)
     def _():
         loads = start_loads(a_refs, a_bufs, sems)
-        tokens = fresh_ref.shape[0]
+        tokens = low_ref.shape[1]
         proj = jnp.zeros((tokens, 2 * HD), jnp.float32)
         square = jnp.zeros((1, HD), jnp.float32)
         for m_ref in m_refs:
@@ -410,11 +417,11 @@
         in_specs=[SM] + [VM] * (len(operands) - 1) + [ANY] * len(a_blocks),
         out_specs=(VM, VM),
         out_shape=(
-            sds((tokens, 2 * HD), jnp.bfloat16),
-            sds((tokens // 2, HD), jnp.bfloat16),
+            sds((tokens + 16, 2 * HD), jnp.bfloat16),
+            sds((R, tokens), jnp.bfloat16),
         ),
         scratch_shapes=[
-            pltpu.VMEM((tokens, q_width), jnp.bfloat16),
+            pltpu.VMEM((q_width, tokens), jnp.bfloat16),
             *[pltpu.VMEM(a.shape, jnp.bfloat16) for a in a_blocks],
             pltpu.SemaphoreType.DMA((len(a_blocks),)),
         ],
@@ -425,13 +432,9 @@
 
 
 def unfold_low(packed, slots, base, rows):
-    count = packed.shape[0]
-    half = lax.broadcasted_iota(jnp.int32, (count, HD), 1) // R
-    turned = pltpu.roll(packed, R, 1)
-    low = jnp.concatenate(
-        [jnp.where(half == 0, packed, turned), jnp.where(half == 1, packed, turned)], axis=0
-    )
-    half = lax.broadcasted_iota(jnp.int32, (2 * count, HD), 1) // R
+    tokens = packed.shape[1]
+    low = jnp.transpose(jnp.concatenate([packed, packed], axis=0))
+    half = lax.broadcasted_iota(jnp.int32, (tokens, HD), 1) // R
     return jnp.concatenate(
         [
             jnp.where(slots == base + 2 * j + half, low, 0.0).astype(jnp.bfloat16)
@@ -564,17 +567,17 @@
     )(*operands)
 
 
-def insert_kernel(spot_ref, new_ref, old_ref, out_ref):
+def insert_kernel(new_ref, old_ref, out_ref, spot_ref):
     count = old_ref.shape[0]
-    tokens = new_ref.shape[0]
-    rows = lax.broadcasted_iota(jnp.int32, (PAGE, tokens), 0)
+    tokens = new_ref.shape[0] - count
+    rows = lax.broadcasted_iota(jnp.int32, (PAGE, tokens), 0).astype(jnp.float32)
+    spot_ref[...] = new_ref[tokens:, :HD].astype(jnp.float32)
 
     def insert(i, _):
-        spot = spot_ref[pl.ds(i, 1), :]
-        hit = jnp.where(spot == rows, 1.0, 0.0)
+        hit = jnp.where(spot_ref[pl.ds(i, 1), :] == rows, 1.0, 0.0)
         fresh = jnp.sum(hit, axis=1, keepdims=True) > 0.0
         hit = hit.astype(jnp.bfloat16)
-        values = jnp.dot(hit, new_ref[...], preferred_element_type=jnp.float32)
+        values = jnp.dot(hit, new_ref[:tokens, :], preferred_element_type=jnp.float32)
         for part in range(2):
             value = values[:, part * HD : (part + 1) * HD]
             old = old_ref[i, part].astype(jnp.float32)
@@ -584,16 +587,17 @@
     lax.fori_loop(0, count, insert, 0, unroll=4)
 
 
-def insert_new(spots, fresh, old):
+def insert_new(fresh, old):
     return pl.pallas_call(
         insert_kernel,
-        in_specs=[VM] * 3,
+        in_specs=[VM] * 2,
         out_specs=VM,
         out_shape=sds((1, *old.shape), jnp.bfloat16),
+        scratch_shapes=[pltpu.VMEM((old.shape[0], HD), jnp.float32)],
         compiler_params=vmem(),
         cost_estimate=cost(3),
         name="insert_new",
-    )(spots, fresh, old)
+    )(fresh, old)
 
 
 def body(
@@ -617,8 +621,11 @@
     adapters = adapter_in.shape[1]
     q_width = queries.shape[2]
 
-    def around(x, shift):
-        return lax.ppermute(x, "tp", [(t, (t + shift) % n_tp) for t in range(n_tp)])
+    def around(x, shift, sections=range(n_sec)):
+        pairs = [
+            (l * n_tp + t, l * n_tp + (t + shift) % n_tp) for l in sections for t in range(n_tp)
+        ]
+        return lax.ppermute(x, ("pipe", "tp"), pairs)
 
     def onward(x, shift, step=1, sections=range(n_sec)):
         pairs = [
@@ -643,6 +650,7 @@
         return lax.optimization_barrier((x, *others))[0]
 
     paired = n_req == 2
+    assert tokens == HD and moves.shape[0] == 16
     later = list(range(1, n_sec))
     sec = jnp.stack([section, my_tp, my_req % 2, my_req]).astype(jnp.int32)
 
@@ -652,9 +660,18 @@
     half = width // 2
     final = n_sec - 1
     sent = parcels(sec, hidden, raw, n_tp)
-    mine = [around(sent[s - 1], s) for s in range(1, n_tp)]
+    far = far_shift(n_tp)
+    turns = [s for s in range(1, n_tp) if s != far]
+    detour = n_sec // 2
+    passing = around(hidden, far, [detour])
+    mine = {s: around(sent[s - 1], s) for s in turns}
+    mine[far] = around(sent[far - 1], far, [1])
+    rows_in = [hidden] + [mine[s] for s in range(1, n_tp)]
+    rows_in[far] = onward(passing, 0, n_sec - detour, [detour])
+    mine_late = around(after(sent[far - 1], *[mine[s] for s in turns]), far, later[1:])
     a_blocks = gather(a_own)
-    acc, lse, slots, cos, sin, leaving, spots = local_work(
+    b_blocks = gather(b_own)
+    acc, lse, line, slots, cos, sin, leaving, spots = local_work(
         paired,
         adapters,
         sec,
@@ -667,60 +684,66 @@
         kv_pages[0],
     )
     if paired:
-        spots = partner(spots)
         ready = after(b_own, lse)
-        own_before = onward(ready, 0)
-        early = partner(ready, [0], 1)
+        before = [onward(x, 0, 1, range(final)) for x in (ready, b_blocks[1])]
     else:
-        b_blocks = [lax.all_gather(b_own, "req", axis=0, tiled=True)]
         before = [onward(b_blocks[0], 0)]
     chunks = [(0, lambda sec, i=i: i, lambda sec, i=i: i) for i in range(2 * n_tp)]
     weights = split_parts(
         sec,
-        [after(raw, lse, *a_blocks)],
+        [after(raw, lse, *a_blocks, *b_blocks)],
         chunks,
         lambda section: section == 0,
         half,
         "split_first",
     )
-    far = far_shift(n_tp)
-    turns = [s for s in range(1, n_tp) if s != far]
-    other = {s: partner(after(mine[s - 1], lse), later) for s in turns}
+    other = {s: partner(after(mine[s], lse), later) for s in turns}
     weights = after(weights, *other.values())
 
-    shared = [queries[0], cos, sin, acc, lse, slots]
+    shared = [queries[0], cos, sin, acc, lse, line, spots]
     n_a = len(a_blocks)
     fresh, low = attend_call(
         functools.partial(first_kernel, n_tp, n_a),
-        [sec, hidden, *mine, weights, norm_gain, *shared],
+        [sec, *rows_in, weights, norm_gain, *shared],
         a_blocks,
         tokens,
         q_width,
         "first_section",
     )
-    other[far] = partner(after(mine[far - 1], low), later)
+    other[far] = partner(mine[far], [1])
+    other_late = partner(mine_late, later[1:])
     chunks = [(0, lambda sec, i=i: 2 * sec[1] + i, lambda sec, i=i: i) for i in range(2)]
     raws = [after(raw, low)]
     for place, s in enumerate(turns, 1):
         chunks.append((len(raws), lambda sec: 0, lambda sec, p=place: 2 * p + sec[2]))
         chunks.append((len(raws) + 1, lambda sec: 0, lambda sec, p=place: 2 * p + 1 - sec[2]))
-        raws += [mine[s - 1], other[s]]
+        raws += [mine[s], other[s]]
     inner = lambda section: section > 0
     near_rows = split_parts(sec, raws, chunks, inner, half, "split_near")
     chunks = [(0, lambda sec: 0, lambda sec: sec[2]), (1, lambda sec: 0, lambda sec: 1 - sec[2])]
-    far_rows = split_parts(sec, [mine[far - 1], other[far]], chunks, inner, half, "split_far")
-    if paired:
-        late = partner(after(b_own, near_rows), later[:-1], 1)
+    far_rows = split_parts(
+        sec, [mine[far], other[far]], chunks, lambda section: section == 1, half, "split_far"
+    )
+    far_late = split_parts(
+        sec, [mine_late, other_late], chunks, lambda section: section > 1, half, "split_far_late"
+    )
     h_prev = h_new = hidden
     for l in later:
         lows = [onward(low, s, 1, [0] if l == 1 else range(n_sec)) for s in range(n_tp)]
         if l == 2 and paired:
-            b_blocks = [b_own, partner(after(b_own, low), [final])]
             leaving = partner(after(leaving, low))
-        if paired:
-            before = [own_before, early if l == 1 else late]
         h_new, *parts = section_slice(
-            l, n_tp, sec, lows, slots, norm_gain, near_rows, far_rows, h_prev, h_new, before
+            l,
+            n_tp,
+            sec,
+            lows,
+            slots,
+            norm_gain,
+            near_rows,
+            far_rows if l == 1 else far_late,
+            h_prev,
+            h_new,
+            before,
         )
         parts = [parts[0]] + [around(parts[s], -s) for s in range(1, n_tp)]
         if l < final:
@@ -737,9 +760,9 @@
         )
     lows = [low] + [around(low, s) for s in range(1, n_tp)]
     if paired:
-        arrived = insert_new(spots, partner(fresh), leaving)
+        arrived = insert_new(partner(fresh), leaving)
     else:
-        leaving = insert_new(spots, fresh, leaving)[0]
+        leaving = insert_new(fresh, leaving)[0]
         count = moves.shape[0]
         free_slots = (n_req - 1) * ((count + n_req - 2) // (n_req - 1))
         received, dest_in, spots_in = (
@@ -750,7 +773,7 @@
         empty = jnp.zeros((free_slots, *leaving.shape[1:]), jnp.bfloat16)
         arrived = empty.at[target].set(received, mode="drop")[None]
     section_out = section_result(final, n_tp, sec, back, lows, slots, h_new, b_blocks)
-    return (section_out, fresh.reshape(1, tokens, 2, HD), arrived)
+    return (section_out, fresh[:tokens].reshape(1, tokens, 2, HD), arrived)
 
 
 def solution(mesh):

time: 156 us -> 151 us (0.968)
  waiting for transfers between devices: 57.7 us -> 42.3 us
  starting transfers between devices: 68.4 us -> 77.7 us
  Pallas kernels: 25.9 us -> 28.4 us
    ppermute x15 -> x17, waiting for transfers between devices: 44.3 us -> 28.2 us  [around(): return lax.ppermute(x, ('pipe', 'tp'), pairs)]
    ppermute x16 -> x18, starting transfers between devices: 29.4 us -> 43 us  [onward(): return lax.ppermute(x, ('pipe', 'tp'), pairs)]
    ppermute x10 -> x8, starting transfers between devices: 15.6 us -> 9.13 us  [partner(): return lax.ppermute(x, ('pipe', 'req'), pairs)]
    ppermute x15 -> x17, starting transfers between devices: 23.5 us -> 25.6 us  [around(): return lax.ppermute(x, ('pipe', 'tp'), pairs)]
    ppermute x16 -> x18, waiting for transfers between devices: 10.7 us -> 12.6 us  [onward(): return lax.ppermute(x, ('pipe', 'tp'), pairs)]
    pallas_call x3 -> x4, Pallas kernels: 4.09 us -> 4.65 us  [split_parts(): pl.pallas_call(functools.partial(split_kernel, chunks, section_of), in_sp...]
  transfers between devices with their start and end apart: 41 -> 43, of which waited for: 18 -> 16; matrix products, arithmetic and copies ran while one was open for 1% -> 1% of each run, Pallas kernels for 14% -> 16%
where the time goes in v4:
time: 151 us
  starting transfers between devices  77.7 us (51%)
  waiting for transfers between devices  42.3 us (28%)
  Pallas kernels  28.4 us (19%)
    ppermute x18, starting transfers between devices, onward(): return lax.ppermute(x, ('pipe', 'tp'), pairs)  43 us
    ppermute x17, waiting for transfers between devices, around(): return lax.ppermute(x, ('pipe', 'tp'), pairs)  28.2 us
    ppermute x17, starting transfers between devices, around(): return lax.ppermute(x, ('pipe', 'tp'), pairs)  25.6 us
    ppermute x18, waiting for transfers between devices, onward(): return lax.ppermute(x, ('pipe', 'tp'), pairs)  12.6 us
    ppermute x8, starting transfers between devices, partner(): return lax.ppermute(x, ('pipe', 'req'), pairs)  9.13 us
    pallas_call x4, Pallas kernels, attend_call(): pl.pallas_call(kernel, in_specs=[SM] + [VM] * (len(operands) - 1) + [ANY]...  7.53 us
    pallas_call x1, Pallas kernels, local_work(): pl.pallas_call(functools.partial(local_kernel, paired, adapters), in_spec...  7.17 us
    pallas_call x4, Pallas kernels, split_parts(): pl.pallas_call(functools.partial(split_kernel, chunks, section_of), in_sp...  4.65 us
  transfers between devices with their start and end apart: 43, of which 16 were waited for; matrix products, arithmetic and copies ran while one was open for 1% of the time, Pallas kernels for 16%

profile of v4, /device:TPU:0, one launch (start us, length us, event | category | flops | bytes accessed | tf_op | source)
XLA Modules:
  0.0 150.7 jit_solution(18184170677214610341)
XLA Ops:
  0.7 3.0 %collective-permute-start.5 = (bf16[256,2048]{1,0:T(8,128)(2,1)}, bf16[256,2048]{1,0:T(8,128)(2,1)S(1)}, u32[]{:S(2)}, u32[]{:S(2)}) collective-permute-start(bf16[256,2048]{1,0:T(8,128)(2,1)} %bitcast.14), channel_id=1, source_target_pairs={{0,4},{4,0},{8,12},{12,8},{16,20},{20,16},{24,28},{28,24},{1,5},{5... | collective-permute-start | bytes 3145736 | tf_op jit(solution)/shard_map/ppermute | solution.py:644
  3.8 2.4 %parcels.1 = (bf16[2048,128]{1,0:T(8,128)(2,1)S(1)}, bf16[2048,128]{1,0:T(8,128)(2,1)}, bf16[2048,128]{1,0:T(8,128)(2,1)}) custom-call(s32[4]{0:T(128)S(1)} %pad_add_fusion.sec_ref, bf16[128,2048]{1,0:T(8,128)(2,1)} %refs_9_.1, bf16[16384,128]{1,0:T(8,128)(2,1)} %bitcast.17), custom_call_target="tpu_custom_call" | custom-call | bytes 6000000 | tf_op jit(solution)/shard_map/parcels/pallas_call | solution.py:122
  6.2 1.6 %collective-permute-start = (bf16[2048,128]{1,0:T(8,128)(2,1)S(1)}, bf16[2048,128]{1,0:T(8,128)(2,1)S(1)}, u32[]{:S(2)}, u32[]{:S(2)}) collective-permute-start(bf16[2048,128]{1,0:T(8,128)(2,1)S(1)} %get-tuple-element.48), channel_id=1, source_target_pairs={{0,1},{1,2},{2,3},{3,0},{8,9},{9,10},{10,11},{11,8},{16,17},{17,18... | collective-permute-start | bytes 1572872 | tf_op jit(solution)/shard_map/ppermute | solution.py:628
  7.8 1.4 collective-permute-start.1
  9.2 2.2 %collective-permute-start.3 = (bf16[2048,128]{1,0:T(8,128)(2,1)}, bf16[2048,128]{1,0:T(8,128)(2,1)S(1)}, u32[]{:S(2)}, u32[]{:S(2)}) collective-permute-start(bf16[2048,128]{1,0:T(8,128)(2,1)} %get-tuple-element.49), channel_id=1, source_target_pairs={{0,3},{1,0},{2,1},{3,2},{8,11},{9,8},{10,9},{11,10},{16,19},{17,16... | collective-permute-start | bytes 1572872 | tf_op jit(solution)/shard_map/ppermute | solution.py:628
  11.8 11.0 %collective-permute-done.refs_1_ = bf16[2048,128]{1,0:T(8,128)(2,1)S(1)} collective-permute-done((bf16[2048,128]{1,0:T(8,128)(2,1)S(1)}, bf16[2048,128]{1,0:T(8,128)(2,1)S(1)}, u32[]{:S(2)}, u32[]{:S(2)}) %collective-permute-start) | collective-permute-done | bytes 524320 | tf_op jit(solution)/shard_map/ppermute | solution.py:628
  22.9 1.5 collective-permute-start.12
  24.7 7.2 %local_work.1 = (f32[8,128,128]{2,1,0:T(8,128)S(1)}, f32[8,128]{1,0:T(8,128)S(1)}, f32[8,128]{1,0:T(8,128)S(1)}, s32[128,128]{1,0:T(8,128)S(1)}, f32[128,128]{1,...) custom-call(s32[4]{0:T(128)S(1)} %pad_add_fusion.sec_ref, ...), custom_call_target="tpu_custom_call" | custom-call | bytes 900000 | tf_op jit(solution)/shard_map/local_work/pallas_call | solution.py:267
  32.6 1.2 collective-permute-done.3.refs_3_
  33.8 2.9 %collective-permute-start.14 = (bf16[256,2048]{1,0:T(8,128)(2,1)S(1)}, bf16[256,2048]{1,0:T(8,128)(2,1)S(1)}, u32[]{:S(2)}, u32[]{:S(2)}) collective-permute-start(bf16[256,2048]{1,0:T(8,128)(2,1)S(1)} %bitcast.15), channel_id=1, source_target_pairs={{0,8},{1,9},{2,10},{3,11},{8,16},{9,17},{10,18},{11,19},{16,24},{1... | collective-permute-start | bytes 3145736 | tf_op jit(solution)/shard_map/ppermute | solution.py:636
  36.7 10.8 %collective-permute-start.15 = (bf16[256,2048]{1,0:T(8,128)(2,1)S(1)}, bf16[256,2048]{1,0:T(8,128)(2,1)S(1)}, u32[]{:S(2)}, u32[]{:S(2)}) collective-permute-start(bf16[256,2048]{1,0:T(8,128)(2,1)S(1)} %collective-permute-done.5.refs_7_), channel_id=1, source_target_pairs={{0,8},{1,9},{2,10},{3,11},{8,16},{9,17},{10,18},{11,19},{16,24},{1... | collective-permute-start | bytes 3145736 | tf_op jit(solution)/shard_map/ppermute | solution.py:636
  48.3 1.3 collective-permute-start.2
  51.0 2.9 %split_first.1.refs_4_ = bf16[8192,256]{1,0:T(8,128)(2,1)S(1)} custom-call(s32[4]{0:T(128)S(1)} %pad_add_fusion.sec_ref, bf16[16384,128]{1,0:T(8,128)(2,1)} %bitcast.18), custom_call_target="tpu_custom_call" | custom-call | bytes 900000 | tf_op jit(solution)/shard_map/split_first/pallas_call | solution.py:75
  54.0 5.6 %collective-permute-done.2.refs_2_ = bf16[128,2048]{1,0:T(8,128)(2,1)S(1)} collective-permute-done((bf16[128,2048]{1,0:T(8,128)(2,1)}, bf16[128,2048]{1,0:T(8,128)(2,1)S(1)}, u32[]{:S(2)}, u32[]{:S(2)}) %collective-permute-start.2) | collective-permute-done | bytes 524320 | tf_op jit(solution)/shard_map/ppermute | solution.py:636
  59.6 5.2 %first_section.1 = (bf16[144,256]{1,0:T(8,128)(2,1)S(1)}, bf16[64,128]{1,0:T(8,128)(2,1)S(1)}) custom-call(s32[4]{0:T(128)S(1)} %pad_add_fusion.sec_ref, bf16[128,2048]{1,0:T(8,128)(2,1)} %refs_9_.1, bf16[2048,128]{1,0:T(8,128)(2,1)S(1)} %collective-permute-done.refs_1_, bf16[128,2048]{1,0:T(8,128)(2,1)S(1)} %collective-permute-done.2.refs_2_, ...), custom_call_target="tpu_custom_call" | custom-call | bytes 15000000 | tf_op jit(solution)/shard_map/first_section/pallas_call | solution.py:415
  64.8 1.3 collective-permute-start.8
  66.1 2.9 %collective-permute-start.9 = (bf16[64,128]{1,0:T(8,128)(2,1)S(1)}, bf16[64,128]{1,0:T(8,128)(2,1)S(1)}, u32[]{:S(2)}, u32[]{:S(2)}) collective-permute-start(bf16[64,128]{1,0:T(8,128)(2,1)S(1)} %get-tuple-element.61), channel_id=1, source_target_pairs={{0,9},{1,10},{2,11},{3,8},{4,13},{5,14},{6,15},{7,12}} | collective-permute-start | bytes 49160 | tf_op jit(solution)/shard_map/ppermute | solution.py:636
  69.0 6.6 %collective-permute-start.10 = (bf16[64,128]{1,0:T(8,128)(2,1)S(1)}, bf16[64,128]{1,0:T(8,128)(2,1)S(1)}, u32[]{:S(2)}, u32[]{:S(2)}) collective-permute-start(bf16[64,128]{1,0:T(8,128)(2,1)S(1)} %get-tuple-element.61), channel_id=1, source_target_pairs={{0,10},{1,11},{2,8},{3,9},{4,14},{5,15},{6,12},{7,13}} | collective-permute-start | bytes 49160 | tf_op jit(solution)/shard_map/ppermute | solution.py:636
  75.6 1.3 collective-permute-start.11
  78.3 1.3 section_slice_1.1
  79.6 3.1 %collective-permute-start.16 = (bf16[144,256]{1,0:T(8,128)(2,1)S(1)}, bf16[144,256]{1,0:T(8,128)(2,1)S(1)}, u32[]{:S(2)}, u32[]{:S(2)}) collective-permute-start(bf16[144,256]{1,0:T(8,128)(2,1)S(1)} %get-tuple-element.67), channel_id=1, source_target_pairs={{0,3},{1,0},{2,1},{3,2},{8,11},{9,8},{10,9},{11,10},{16,19},{17,16... | collective-permute-start | bytes 221192 | tf_op jit(solution)/shard_map/ppermute | solution.py:628
  82.7 1.8 %collective-permute-start.18 = (bf16[144,256]{1,0:T(8,128)(2,1)S(1)}, bf16[144,256]{1,0:T(8,128)(2,1)S(1)}, u32[]{:S(2)}, u32[]{:S(2)}) collective-permute-start(bf16[144,256]{1,0:T(8,128)(2,1)S(1)} %get-tuple-element.69), channel_id=1, source_target_pairs={{0,1},{1,2},{2,3},{3,0},{8,9},{9,10},{10,11},{11,8},{16,17},{17,18... | collective-permute-start | bytes 221192 | tf_op jit(solution)/shard_map/ppermute | solution.py:628
  85.2 5.9 %collective-permute-done.17.refs_2_ = bf16[144,256]{1,0:T(8,128)(2,1)S(1)} collective-permute-done((bf16[144,256]{1,0:T(8,128)(2,1)S(1)}, bf16[144,256]{1,0:T(8,128)(2,1)S(1)}, u32[]{:S(2)}, u32[]{:S(2)}) %collective-permute-start.17) | collective-permute-done | bytes 73760 | tf_op jit(solution)/shard_map/ppermute | solution.py:628
  92.2 3.9 %collective-permute-start.19 = (bf16[64,128]{1,0:T(8,128)(2,1)S(1)}, bf16[64,128]{1,0:T(8,128)(2,1)S(1)}, u32[]{:S(2)}, u32[]{:S(2)}) collective-permute-start(bf16[64,128]{1,0:T(8,128)(2,1)S(1)} %get-tuple-element.71), channel_id=1, source_target_pairs={{0,8},{1,9},{2,10},{3,11},{8,16},{9,17},{10,18},{11,19},{16,24},{1... | collective-permute-start | bytes 49160 | tf_op jit(solution)/shard_map/ppermute | solution.py:636
  96.8 1.2 collective-permute-start.22
  98.5 1.3 collective-permute-done.19.refs_0_
  99.9 2.1 %collective-permute-done.20.refs_1_ = bf16[64,128]{1,0:T(8,128)(2,1)S(1)} collective-permute-done((bf16[64,128]{1,0:T(8,128)(2,1)S(1)}, bf16[64,128]{1,0:T(8,128)(2,1)S(1)}, u32[]{:S(2)}, u32[]{:S(2)}) %collective-permute-start.20) | collective-permute-done | bytes 16416 | tf_op jit(solution)/shard_map/ppermute | solution.py:636
  102.8 3.4 %collective-permute-start.26 = (bf16[144,256]{1,0:T(8,128)(2,1)S(1)}, bf16[144,256]{1,0:T(8,128)(2,1)S(1)}, u32[]{:S(2)}, u32[]{:S(2)}) collective-permute-start(bf16[144,256]{1,0:T(8,128)(2,1)S(1)} %get-tuple-element.76), channel_id=1, source_target_pairs={{0,3},{1,0},{2,1},{3,2},{8,11},{9,8},{10,9},{11,10},{16,19},{17,16... | collective-permute-start | bytes 221192 | tf_op jit(solution)/shard_map/ppermute | solution.py:628
  106.8 1.3 collective-permute-done.26.refs_1_
  108.2 4.4 %collective-permute-done.27.refs_2_ = bf16[144,256]{1,0:T(8,128)(2,1)S(1)} collective-permute-done((bf16[144,256]{1,0:T(8,128)(2,1)S(1)}, bf16[144,256]{1,0:T(8,128)(2,1)S(1)}, u32[]{:S(2)}, u32[]{:S(2)}) %collective-permute-start.27) | collective-permute-done | bytes 73760 | tf_op jit(solution)/shard_map/ppermute | solution.py:628
  113.2 2.8 %collective-permute-start.29 = (bf16[64,128]{1,0:T(8,128)(2,1)S(1)}, bf16[64,128]{1,0:T(8,128)(2,1)S(1)}, u32[]{:S(2)}, u32[]{:S(2)}) collective-permute-start(bf16[64,128]{1,0:T(8,128)(2,1)S(1)} %get-tuple-element.79), channel_id=1, source_target_pairs={{0,8},{1,9},{2,10},{3,11},{8,16},{9,17},{10,18},{11,19},{16,24},{1... | collective-permute-start | bytes 49160 | tf_op jit(solution)/shard_map/ppermute | solution.py:636
  116.0 2.1 %collective-permute-start.30 = (bf16[64,128]{1,0:T(8,128)(2,1)S(1)}, bf16[64,128]{1,0:T(8,128)(2,1)S(1)}, u32[]{:S(2)}, u32[]{:S(2)}) collective-permute-start(bf16[64,128]{1,0:T(8,128)(2,1)S(1)} %get-tuple-element.79), channel_id=1, source_target_pairs={{0,9},{1,10},{2,11},{3,8},{8,17},{9,18},{10,19},{11,16},{16,25},{1... | collective-permute-start | bytes 49160 | tf_op jit(solution)/shard_map/ppermute | solution.py:636
  118.1 1.4 collective-permute-start.31
  119.5 2.2 %collective-permute-start.32 = (bf16[64,128]{1,0:T(8,128)(2,1)S(1)}, bf16[64,128]{1,0:T(8,128)(2,1)S(1)}, u32[]{:S(2)}, u32[]{:S(2)}) collective-permute-start(bf16[64,128]{1,0:T(8,128)(2,1)S(1)} %get-tuple-element.79), channel_id=1, source_target_pairs={{0,11},{1,8},{2,9},{3,10},{8,19},{9,16},{10,17},{11,18},{16,27},{1... | collective-permute-start | bytes 49160 | tf_op jit(solution)/shard_map/ppermute | solution.py:636
  121.9 1.2 collective-permute-done.31.refs_2_
  123.1 1.7 %collective-permute-done.32.refs_3_ = bf16[64,128]{1,0:T(8,128)(2,1)S(1)} collective-permute-done((bf16[64,128]{1,0:T(8,128)(2,1)S(1)}, bf16[64,128]{1,0:T(8,128)(2,1)S(1)}, u32[]{:S(2)}, u32[]{:S(2)}) %collective-permute-start.32) | collective-permute-done | bytes 16416 | tf_op jit(solution)/shard_map/ppermute | solution.py:636
  124.8 1.4 section_slice_3.1
  126.2 3.3 %collective-permute-start.34 = (bf16[144,256]{1,0:T(8,128)(2,1)S(1)}, bf16[144,256]{1,0:T(8,128)(2,1)S(1)}, u32[]{:S(2)}, u32[]{:S(2)}) collective-permute-start(bf16[144,256]{1,0:T(8,128)(2,1)S(1)} %get-tuple-element.83), channel_id=1, source_target_pairs={{0,3},{1,0},{2,1},{3,2},{8,11},{9,8},{10,9},{11,10},{16,19},{17,16... | collective-permute-start | bytes 221192 | tf_op jit(solution)/shard_map/ppermute | solution.py:628
  130.0 1.5 collective-permute-start.42
  131.9 3.9 %collective-permute-done.35.refs_2_ = bf16[144,256]{1,0:T(8,128)(2,1)S(1)} collective-permute-done((bf16[144,256]{1,0:T(8,128)(2,1)S(1)}, bf16[144,256]{1,0:T(8,128)(2,1)S(1)}, u32[]{:S(2)}, u32[]{:S(2)}) %collective-permute-start.35) | collective-permute-done | bytes 73760 | tf_op jit(solution)/shard_map/ppermute | solution.py:628
  135.8 1.2 collective-permute-start.37
  137.0 1.2 section_3.1
  138.2 1.5 %collective-permute-start.41 = (bf16[144,256]{1,0:T(8,128)(2,1)S(1)}, bf16[144,256]{1,0:T(8,128)(2,1)S(1)}, u32[]{:S(2)}, u32[]{:S(2)}) collective-permute-start(bf16[144,256]{1,0:T(8,128)(2,1)S(1)} %get-tuple-element.90), channel_id=1, source_target_pairs={{0,4},{4,0},{8,12},{12,8},{16,20},{20,16},{24,28},{28,24},{1,5},{5... | collective-permute-start | bytes 221192 | tf_op jit(solution)/shard_map/ppermute | solution.py:644
  140.0 1.8 %collective-permute-start.39 = (bf16[64,128]{1,0:T(8,128)(2,1)}, bf16[64,128]{1,0:T(8,128)(2,1)S(1)}, u32[]{:S(2)}, u32[]{:S(2)}) collective-permute-start(bf16[64,128]{1,0:T(8,128)(2,1)} %get-tuple-element.89.refs_0_), channel_id=1, source_target_pairs={{0,2},{1,3},{2,0},{3,1},{8,10},{9,11},{10,8},{11,9},{16,18},{17,19... | collective-permute-start | bytes 49160 | tf_op jit(solution)/shard_map/ppermute | solution.py:628
  141.9 1.4 collective-permute-done.42.old_ref
  143.3 3.3 %collective-permute-start.40 = (bf16[64,128]{1,0:T(8,128)(2,1)}, bf16[64,128]{1,0:T(8,128)(2,1)S(1)}, u32[]{:S(2)}, u32[]{:S(2)}) collective-permute-start(bf16[64,128]{1,0:T(8,128)(2,1)} %get-tuple-element.89.refs_0_), channel_id=1, source_target_pairs={{0,3},{1,0},{2,1},{3,2},{8,11},{9,8},{10,9},{11,10},{16,19},{17,16... | collective-permute-start | bytes 49160 | tf_op jit(solution)/shard_map/ppermute | solution.py:628
  147.2 1.5 insert_new.1
  148.7 1.9 %section_result.1 = bf16[1,128,2048]{2,1,0:T(8,128)(2,1)} custom-call(s32[4]{0:T(128)S(1)} %pad_add_fusion.sec_ref, bf16[128,2048]{1,0:T(8,128)(2,1)S(1)} %collective-permute-done.37.back_ref, bf16[64,128]{1,0:T(8,128)(2,1)} %get-tuple-element.89.refs_0_, bf16[64,128]{1,0:T(8,128)(2,1)S(1)} %collective-permute-done.38.refs_1_, ...), custom_call_target="tpu_custom_call" | custom-call | bytes 9000000 | tf_op jit(solution)/shard_map/section_result/pallas_call | solution.py:559
  (90 shorter events, 12.2 us)
Async XLA Ops:
  0.7 24.0 %copy-start.5 = (s32[32]{0:T(128)S(1)}, s32[32]{0:T(128)}, u32[]{:S(2)}) copy-start(s32[32]{0:T(128)} %len_ref.1) | copy-start | bytes 388
  0.7 36.0 %collective-permute-start.5 = (bf16[256,2048]{1,0:T(8,128)(2,1)}, bf16[256,2048]{1,0:T(8,128)(2,1)S(1)}, u32[]{:S(2)}, u32[]{:S(2)}) collective-permute-start(bf16[256,2048]{1,0:T(8,128)(2,1)} %bitcast.14), channel_id=1, source_target_pairs={{0,4},{4,0},{8,12},{12,8},{16,20},{20,16},{24,28},{28,24},{1,5},{5... | collective-permute-start | bytes 3145736 | tf_op jit(solution)/shard_map/ppermute | solution.py:644
  3.8 30.1 %copy-start.3 = (bf16[1,4,64,2048]{3,2,1,0:T(8,128)(2,1)S(1)}, bf16[1,4,64,2048]{3,2,1,0:T(8,128)(2,1)}, u32[]{:S(2)}) copy-start(bf16[1,4,64,2048]{3,2,1,0:T(8,128)(2,1)} %param.17) | copy-start | bytes 3145732
  6.2 16.7 %collective-permute-start = (bf16[2048,128]{1,0:T(8,128)(2,1)S(1)}, bf16[2048,128]{1,0:T(8,128)(2,1)S(1)}, u32[]{:S(2)}, u32[]{:S(2)}) collective-permute-start(bf16[2048,128]{1,0:T(8,128)(2,1)S(1)} %get-tuple-element.48), channel_id=1, source_target_pairs={{0,1},{1,2},{2,3},{3,0},{8,9},{9,10},{10,11},{11,8},{16,17},{17,18... | collective-permute-start | bytes 1572872 | tf_op jit(solution)/shard_map/ppermute | solution.py:628
  7.8 24.1 %collective-permute-start.1 = (bf16[128,2048]{1,0:T(8,128)(2,1)}, bf16[128,2048]{1,0:T(8,128)(2,1)}, u32[]{:S(2)}, u32[]{:S(2)}) collective-permute-start(bf16[128,2048]{1,0:T(8,128)(2,1)} %refs_9_.1), channel_id=1, source_target_pairs={{16,18},{17,19},{18,16},{19,17},{20,22},{21,23},{22,20},{23,21}} | collective-permute-start | bytes 1572872 | tf_op jit(solution)/shard_map/ppermute | solution.py:628
  9.2 24.6 %collective-permute-start.3 = (bf16[2048,128]{1,0:T(8,128)(2,1)}, bf16[2048,128]{1,0:T(8,128)(2,1)S(1)}, u32[]{:S(2)}, u32[]{:S(2)}) collective-permute-start(bf16[2048,128]{1,0:T(8,128)(2,1)} %get-tuple-element.49), channel_id=1, source_target_pairs={{0,3},{1,0},{2,1},{3,2},{8,11},{9,8},{10,9},{11,10},{16,19},{17,16... | collective-permute-start | bytes 1572872 | tf_op jit(solution)/shard_map/ppermute | solution.py:628
  11.5 36.1 %collective-permute-start.4 = (bf16[256,1024]{1,0:T(8,128)(2,1)}, bf16[256,1024]{1,0:T(8,128)(2,1)}, u32[]{:S(2)}, u32[]{:S(2)}) collective-permute-start(bf16[256,1024]{1,0:T(8,128)(2,1)} %bitcast.7.refs_13_.refs_11_), channel_id=1, source_target_pairs={{0,4},{4,0},{8,12},{12,8},{16,20},{20,16},{24,28},{28,24},{1,5},{5... | collective-permute-start | bytes 1572872 | tf_op jit(solution)/shard_map/ppermute | solution.py:644
  22.9 36.7 %copy-start.1 = (bf16[2048,128]{1,0:T(8,128)(2,1)}, bf16[2048,128]{1,0:T(8,128)(2,1)S(1)}, u32[]{:S(2)}) copy-start(bf16[2048,128]{1,0:T(8,128)(2,1)S(1)} %collective-permute-done.refs_1_) | copy-start | bytes 1572868
  22.9 25.4 %collective-permute-start.12 = (bf16[2048,128]{1,0:T(8,128)(2,1)}, bf16[2048,128]{1,0:T(8,128)(2,1)}, u32[]{:S(2)}, u32[]{:S(2)}) collective-permute-start(bf16[2048,128]{1,0:T(8,128)(2,1)} %get-tuple-element.72), channel_id=1, source_target_pairs={{8,10},{9,11},{10,8},{11,9},{12,14},{13,15},{14,12},{15,13}} | collective-permute-start | bytes 1572872 | tf_op jit(solution)/shard_map/ppermute | solution.py:628
  31.9 27.7 %copy-start.4 = (bf16[1,8192]{1,0:T(2,128)(2,1)S(1)}, bf16[1,8192]{1,0:T(2,128)(2,1)}, u32[]{:S(2)}) copy-start(bf16[1,8192]{1,0:T(2,128)(2,1)} %refs_5_.7) | copy-start | bytes 49156
  31.9 17.6 %collective-permute-start.6 = (bf16[2048,128]{1,0:T(8,128)(2,1)S(1)}, bf16[2048,128]{1,0:T(8,128)(2,1)S(1)}, u32[]{:S(2)}, u32[]{:S(2)}) collective-permute-start(bf16[2048,128]{1,0:T(8,128)(2,1)S(1)} %collective-permute-done.refs_1_), channel_id=1, source_target_pairs={{8,12},{12,8},{16,20},{20,16},{24,28},{28,24},{9,13},{13,9},{17,21... | collective-permute-start | bytes 1572872 | tf_op jit(solution)/shard_map/ppermute | solution.py:644
  33.8 25.7 %copy-start.2 = (bf16[2048,128]{1,0:T(8,128)(2,1)}, bf16[2048,128]{1,0:T(8,128)(2,1)S(1)}, u32[]{:S(2)}) copy-start(bf16[2048,128]{1,0:T(8,128)(2,1)S(1)} %collective-permute-done.3.refs_3_) | copy-start | bytes 1572868
  33.8 35.2 %collective-permute-start.14 = (bf16[256,2048]{1,0:T(8,128)(2,1)S(1)}, bf16[256,2048]{1,0:T(8,128)(2,1)S(1)}, u32[]{:S(2)}, u32[]{:S(2)}) collective-permute-start(bf16[256,2048]{1,0:T(8,128)(2,1)S(1)} %bitcast.15), channel_id=1, source_target_pairs={{0,8},{1,9},{2,10},{3,11},{8,16},{9,17},{10,18},{11,19},{16,24},{1... | collective-permute-start | bytes 3145736 | tf_op jit(solution)/shard_map/ppermute | solution.py:636
  36.7 41.6 %collective-permute-start.15 = (bf16[256,2048]{1,0:T(8,128)(2,1)S(1)}, bf16[256,2048]{1,0:T(8,128)(2,1)S(1)}, u32[]{:S(2)}, u32[]{:S(2)}) collective-permute-start(bf16[256,2048]{1,0:T(8,128)(2,1)S(1)} %collective-permute-done.5.refs_7_), channel_id=1, source_target_pairs={{0,8},{1,9},{2,10},{3,11},{8,16},{9,17},{10,18},{11,19},{16,24},{1... | collective-permute-start | bytes 3145736 | tf_op jit(solution)/shard_map/ppermute | solution.py:636
  47.6 2.7 %collective-permute-start.7 = (bf16[2048,128]{1,0:T(8,128)(2,1)S(1)}, bf16[2048,128]{1,0:T(8,128)(2,1)S(1)}, u32[]{:S(2)}, u32[]{:S(2)}) collective-permute-start(bf16[2048,128]{1,0:T(8,128)(2,1)S(1)} %collective-permute-done.3.refs_3_), channel_id=1, source_target_pairs={{8,12},{12,8},{16,20},{20,16},{24,28},{28,24},{9,13},{13,9},{17,21... | collective-permute-start | bytes 1572872 | tf_op jit(solution)/shard_map/ppermute | solution.py:644
  48.3 11.3 %collective-permute-start.2 = (bf16[128,2048]{1,0:T(8,128)(2,1)}, bf16[128,2048]{1,0:T(8,128)(2,1)S(1)}, u32[]{:S(2)}, u32[]{:S(2)}) collective-permute-start(bf16[128,2048]{1,0:T(8,128)(2,1)} %collective-permute-done.1), channel_id=1, source_target_pairs={{16,0},{17,1},{18,2},{19,3},{20,4},{21,5},{22,6},{23,7}} | collective-permute-start | bytes 1572872 | tf_op jit(solution)/shard_map/ppermute | solution.py:636
  49.6 16.5 %collective-permute-start.13 = (bf16[2048,128]{1,0:T(8,128)(2,1)}, bf16[2048,128]{1,0:T(8,128)(2,1)S(1)}, u32[]{:S(2)}, u32[]{:S(2)}) collective-permute-start(bf16[2048,128]{1,0:T(8,128)(2,1)} %collective-permute-done.12.refs_0_), channel_id=1, source_target_pairs={{8,12},{12,8},{9,13},{13,9},{10,14},{14,10},{11,15},{15,11}} | collective-permute-start | bytes 1572872 | tf_op jit(solution)/shard_map/ppermute | solution.py:644
  50.3 34.2 %collective-permute-start.23 = (bf16[2048,128]{1,0:T(8,128)(2,1)}, bf16[2048,128]{1,0:T(8,128)(2,1)S(1)}, u32[]{:S(2)}, u32[]{:S(2)}) collective-permute-start(bf16[2048,128]{1,0:T(8,128)(2,1)} %get-tuple-element.72), channel_id=1, source_target_pairs={{16,18},{17,19},{18,16},{19,17},{24,26},{25,27},{26,24},{27,25},{2... | collective-permute-start | bytes 1572872 | tf_op jit(solution)/shard_map/ppermute | solution.py:628
  64.8 10.8 %collective-permute-start.8 = (bf16[64,128]{1,0:T(8,128)(2,1)S(1)}, bf16[64,128]{1,0:T(8,128)(2,1)S(1)}, u32[]{:S(2)}, u32[]{:S(2)}) collective-permute-start(bf16[64,128]{1,0:T(8,128)(2,1)S(1)} %get-tuple-element.61), channel_id=1, source_target_pairs={{0,8},{1,9},{2,10},{3,11},{4,12},{5,13},{6,14},{7,15}} | collective-permute-start | bytes 49160 | tf_op jit(solution)/shard_map/ppermute | solution.py:636
  66.1 12.0 %collective-permute-start.9 = (bf16[64,128]{1,0:T(8,128)(2,1)S(1)}, bf16[64,128]{1,0:T(8,128)(2,1)S(1)}, u32[]{:S(2)}, u32[]{:S(2)}) collective-permute-start(bf16[64,128]{1,0:T(8,128)(2,1)S(1)} %get-tuple-element.61), channel_id=1, source_target_pairs={{0,9},{1,10},{2,11},{3,8},{4,13},{5,14},{6,15},{7,12}} | collective-permute-start | bytes 49160 | tf_op jit(solution)/shard_map/ppermute | solution.py:636
  69.0 9.1 %collective-permute-start.10 = (bf16[64,128]{1,0:T(8,128)(2,1)S(1)}, bf16[64,128]{1,0:T(8,128)(2,1)S(1)}, u32[]{:S(2)}, u32[]{:S(2)}) collective-permute-start(bf16[64,128]{1,0:T(8,128)(2,1)S(1)} %get-tuple-element.61), channel_id=1, source_target_pairs={{0,10},{1,11},{2,8},{3,9},{4,14},{5,15},{6,12},{7,13}} | collective-permute-start | bytes 49160 | tf_op jit(solution)/shard_map/ppermute | solution.py:636
  75.6 2.7 %collective-permute-start.11 = (bf16[64,128]{1,0:T(8,128)(2,1)S(1)}, bf16[64,128]{1,0:T(8,128)(2,1)S(1)}, u32[]{:S(2)}, u32[]{:S(2)}) collective-permute-start(bf16[64,128]{1,0:T(8,128)(2,1)S(1)} %get-tuple-element.61), channel_id=1, source_target_pairs={{0,11},{1,8},{2,9},{3,10},{4,15},{5,12},{6,13},{7,14}} | collective-permute-start | bytes 49160 | tf_op jit(solution)/shard_map/ppermute | solution.py:636
  79.6 5.6 %collective-permute-start.16 = (bf16[144,256]{1,0:T(8,128)(2,1)S(1)}, bf16[144,256]{1,0:T(8,128)(2,1)S(1)}, u32[]{:S(2)}, u32[]{:S(2)}) collective-permute-start(bf16[144,256]{1,0:T(8,128)(2,1)S(1)} %get-tuple-element.67), channel_id=1, source_target_pairs={{0,3},{1,0},{2,1},{3,2},{8,11},{9,8},{10,9},{11,10},{16,19},{17,16... | collective-permute-start | bytes 221192 | tf_op jit(solution)/shard_map/ppermute | solution.py:628
  82.7 8.4 %collective-permute-start.17 = (bf16[144,256]{1,0:T(8,128)(2,1)S(1)}, bf16[144,256]{1,0:T(8,128)(2,1)S(1)}, u32[]{:S(2)}, u32[]{:S(2)}) collective-permute-start(bf16[144,256]{1,0:T(8,128)(2,1)S(1)} %get-tuple-element.68), channel_id=1, source_target_pairs={{0,2},{1,3},{2,0},{3,1},{8,10},{9,11},{10,8},{11,9},{16,18},{17,19... | collective-permute-start | bytes 221192 | tf_op jit(solution)/shard_map/ppermute | solution.py:628
  82.7 8.4 %collective-permute-start.18 = (bf16[144,256]{1,0:T(8,128)(2,1)S(1)}, bf16[144,256]{1,0:T(8,128)(2,1)S(1)}, u32[]{:S(2)}, u32[]{:S(2)}) collective-permute-start(bf16[144,256]{1,0:T(8,128)(2,1)S(1)} %get-tuple-element.69), channel_id=1, source_target_pairs={{0,1},{1,2},{2,3},{3,0},{8,9},{9,10},{10,11},{11,8},{16,17},{17,18... | collective-permute-start | bytes 221192 | tf_op jit(solution)/shard_map/ppermute | solution.py:628
  84.5 12.3 %collective-permute-start.24 = (bf16[2048,128]{1,0:T(8,128)(2,1)S(1)}, bf16[2048,128]{1,0:T(8,128)(2,1)S(1)}, u32[]{:S(2)}, u32[]{:S(2)}) collective-permute-start(bf16[2048,128]{1,0:T(8,128)(2,1)S(1)} %collective-permute-done.23.refs_0_), channel_id=1, source_target_pairs={{16,20},{20,16},{24,28},{28,24},{17,21},{21,17},{25,29},{29,25},{1... | collective-permute-start | bytes 1572872 | tf_op jit(solution)/shard_map/ppermute | solution.py:644
  91.1 11.1 %collective-permute-start.25 = (bf16[128,2048]{1,0:T(8,128)(2,1)S(1)}, bf16[128,2048]{1,0:T(8,128)(2,1)S(1)}, u32[]{:S(2)}, u32[]{:S(2)}) collective-permute-start(bf16[128,2048]{1,0:T(8,128)(2,1)S(1)} %get-tuple-element.74.refs_9_), channel_id=1, source_target_pairs={{0,8},{1,9},{2,10},{3,11},{8,16},{9,17},{10,18},{11,19},{16,24},{1... | collective-permute-start | bytes 1572872 | tf_op jit(solution)/shard_map/ppermute | solution.py:636
  92.2 7.7 %collective-permute-start.19 = (bf16[64,128]{1,0:T(8,128)(2,1)S(1)}, bf16[64,128]{1,0:T(8,128)(2,1)S(1)}, u32[]{:S(2)}, u32[]{:S(2)}) collective-permute-start(bf16[64,128]{1,0:T(8,128)(2,1)S(1)} %get-tuple-element.71), channel_id=1, source_target_pairs={{0,8},{1,9},{2,10},{3,11},{8,16},{9,17},{10,18},{11,19},{16,24},{1... | collective-permute-start | bytes 49160 | tf_op jit(solution)/shard_map/ppermute | solution.py:636
  96.1 5.9 %collective-permute-start.20 = (bf16[64,128]{1,0:T(8,128)(2,1)S(1)}, bf16[64,128]{1,0:T(8,128)(2,1)S(1)}, u32[]{:S(2)}, u32[]{:S(2)}) collective-permute-start(bf16[64,128]{1,0:T(8,128)(2,1)S(1)} %get-tuple-element.71), channel_id=1, source_target_pairs={{0,9},{1,10},{2,11},{3,8},{8,17},{9,18},{10,19},{11,16},{16,25},{1... | collective-permute-start | bytes 49160 | tf_op jit(solution)/shard_map/ppermute | solution.py:636
  96.1 5.9 %collective-permute-start.21 = (bf16[64,128]{1,0:T(8,128)(2,1)S(1)}, bf16[64,128]{1,0:T(8,128)(2,1)S(1)}, u32[]{:S(2)}, u32[]{:S(2)}) collective-permute-start(bf16[64,128]{1,0:T(8,128)(2,1)S(1)} %get-tuple-element.71), channel_id=1, source_target_pairs={{0,10},{1,11},{2,8},{3,9},{8,18},{9,19},{10,16},{11,17},{16,26},{1... | collective-permute-start | bytes 49160 | tf_op jit(solution)/shard_map/ppermute | solution.py:636
  96.8 5.4 %collective-permute-start.22 = (bf16[64,128]{1,0:T(8,128)(2,1)S(1)}, bf16[64,128]{1,0:T(8,128)(2,1)S(1)}, u32[]{:S(2)}, u32[]{:S(2)}) collective-permute-start(bf16[64,128]{1,0:T(8,128)(2,1)S(1)} %get-tuple-element.71), channel_id=1, source_target_pairs={{0,11},{1,8},{2,9},{3,10},{8,19},{9,16},{10,17},{11,18},{16,27},{1... | collective-permute-start | bytes 49160 | tf_op jit(solution)/shard_map/ppermute | solution.py:636
  102.8 5.3 %collective-permute-start.26 = (bf16[144,256]{1,0:T(8,128)(2,1)S(1)}, bf16[144,256]{1,0:T(8,128)(2,1)S(1)}, u32[]{:S(2)}, u32[]{:S(2)}) collective-permute-start(bf16[144,256]{1,0:T(8,128)(2,1)S(1)} %get-tuple-element.76), channel_id=1, source_target_pairs={{0,3},{1,0},{2,1},{3,2},{8,11},{9,8},{10,9},{11,10},{16,19},{17,16... | collective-permute-start | bytes 221192 | tf_op jit(solution)/shard_map/ppermute | solution.py:628
  106.2 6.4 %collective-permute-start.27 = (bf16[144,256]{1,0:T(8,128)(2,1)S(1)}, bf16[144,256]{1,0:T(8,128)(2,1)S(1)}, u32[]{:S(2)}, u32[]{:S(2)}) collective-permute-start(bf16[144,256]{1,0:T(8,128)(2,1)S(1)} %get-tuple-element.77), channel_id=1, source_target_pairs={{0,2},{1,3},{2,0},{3,1},{8,10},{9,11},{10,8},{11,9},{16,18},{17,19... | collective-permute-start | bytes 221192 | tf_op jit(solution)/shard_map/ppermute | solution.py:628
  106.2 6.4 %collective-permute-start.28 = (bf16[144,256]{1,0:T(8,128)(2,1)S(1)}, bf16[144,256]{1,0:T(8,128)(2,1)S(1)}, u32[]{:S(2)}, u32[]{:S(2)}) collective-permute-start(bf16[144,256]{1,0:T(8,128)(2,1)S(1)} %get-tuple-element.78), channel_id=1, source_target_pairs={{0,1},{1,2},{2,3},{3,0},{8,9},{9,10},{10,11},{11,8},{16,17},{17,18... | collective-permute-start | bytes 221192 | tf_op jit(solution)/shard_map/ppermute | solution.py:628
  112.6 12.2 %collective-permute-start.33 = (bf16[128,2048]{1,0:T(8,128)(2,1)S(1)}, bf16[128,2048]{1,0:T(8,128)(2,1)S(1)}, u32[]{:S(2)}, u32[]{:S(2)}) collective-permute-start(bf16[128,2048]{1,0:T(8,128)(2,1)S(1)} %get-tuple-element.81.refs_9_), channel_id=1, source_target_pairs={{0,8},{1,9},{2,10},{3,11},{8,16},{9,17},{10,18},{11,19},{16,24},{1... | collective-permute-start | bytes 1572872 | tf_op jit(solution)/shard_map/ppermute | solution.py:636
  113.2 8.5 %collective-permute-start.29 = (bf16[64,128]{1,0:T(8,128)(2,1)S(1)}, bf16[64,128]{1,0:T(8,128)(2,1)S(1)}, u32[]{:S(2)}, u32[]{:S(2)}) collective-permute-start(bf16[64,128]{1,0:T(8,128)(2,1)S(1)} %get-tuple-element.79), channel_id=1, source_target_pairs={{0,8},{1,9},{2,10},{3,11},{8,16},{9,17},{10,18},{11,19},{16,24},{1... | collective-permute-start | bytes 49160 | tf_op jit(solution)/shard_map/ppermute | solution.py:636
  116.0 5.9 %collective-permute-start.30 = (bf16[64,128]{1,0:T(8,128)(2,1)S(1)}, bf16[64,128]{1,0:T(8,128)(2,1)S(1)}, u32[]{:S(2)}, u32[]{:S(2)}) collective-permute-start(bf16[64,128]{1,0:T(8,128)(2,1)S(1)} %get-tuple-element.79), channel_id=1, source_target_pairs={{0,9},{1,10},{2,11},{3,8},{8,17},{9,18},{10,19},{11,16},{16,25},{1... | collective-permute-start | bytes 49160 | tf_op jit(solution)/shard_map/ppermute | solution.py:636
  118.1 5.0 %collective-permute-start.31 = (bf16[64,128]{1,0:T(8,128)(2,1)S(1)}, bf16[64,128]{1,0:T(8,128)(2,1)S(1)}, u32[]{:S(2)}, u32[]{:S(2)}) collective-permute-start(bf16[64,128]{1,0:T(8,128)(2,1)S(1)} %get-tuple-element.79), channel_id=1, source_target_pairs={{0,10},{1,11},{2,8},{3,9},{8,18},{9,19},{10,16},{11,17},{16,26},{1... | collective-permute-start | bytes 49160 | tf_op jit(solution)/shard_map/ppermute | solution.py:636
  119.5 5.3 %collective-permute-start.32 = (bf16[64,128]{1,0:T(8,128)(2,1)S(1)}, bf16[64,128]{1,0:T(8,128)(2,1)S(1)}, u32[]{:S(2)}, u32[]{:S(2)}) collective-permute-start(bf16[64,128]{1,0:T(8,128)(2,1)S(1)} %get-tuple-element.79), channel_id=1, source_target_pairs={{0,11},{1,8},{2,9},{3,10},{8,19},{9,16},{10,17},{11,18},{16,27},{1... | collective-permute-start | bytes 49160 | tf_op jit(solution)/shard_map/ppermute | solution.py:636
  126.2 5.7 %collective-permute-start.34 = (bf16[144,256]{1,0:T(8,128)(2,1)S(1)}, bf16[144,256]{1,0:T(8,128)(2,1)S(1)}, u32[]{:S(2)}, u32[]{:S(2)}) collective-permute-start(bf16[144,256]{1,0:T(8,128)(2,1)S(1)} %get-tuple-element.83), channel_id=1, source_target_pairs={{0,3},{1,0},{2,1},{3,2},{8,11},{9,8},{10,9},{11,10},{16,19},{17,16... | collective-permute-start | bytes 221192 | tf_op jit(solution)/shard_map/ppermute | solution.py:628
  129.5 6.4 %collective-permute-start.35 = (bf16[144,256]{1,0:T(8,128)(2,1)S(1)}, bf16[144,256]{1,0:T(8,128)(2,1)S(1)}, u32[]{:S(2)}, u32[]{:S(2)}) collective-permute-start(bf16[144,256]{1,0:T(8,128)(2,1)S(1)} %get-tuple-element.84), channel_id=1, source_target_pairs={{0,2},{1,3},{2,0},{3,1},{8,10},{9,11},{10,8},{11,9},{16,18},{17,19... | collective-permute-start | bytes 221192 | tf_op jit(solution)/shard_map/ppermute | solution.py:628
  129.5 6.4 %collective-permute-start.36 = (bf16[144,256]{1,0:T(8,128)(2,1)S(1)}, bf16[144,256]{1,0:T(8,128)(2,1)S(1)}, u32[]{:S(2)}, u32[]{:S(2)}) collective-permute-start(bf16[144,256]{1,0:T(8,128)(2,1)S(1)} %get-tuple-element.85), channel_id=1, source_target_pairs={{0,1},{1,2},{2,3},{3,0},{8,9},{9,10},{10,11},{11,8},{16,17},{17,18... | collective-permute-start | bytes 221192 | tf_op jit(solution)/shard_map/ppermute | solution.py:628
  130.0 13.3 %collective-permute-start.42 = (bf16[16,2,64,128]{3,2,1,0:T(8,128)(2,1)S(1)}, bf16[16,2,64,128]{3,2,1,0:T(8,128)(2,1)S(1)}, u32[]{:S(2)}, u32[]{:S(2)}) collective-permute-start(bf16[16,2,64,128]{3,2,1,0:T(8,128)(2,1)S(1)} %get-tuple-element.92), channel_id=1, source_target_pairs={{0,4},{4,0},{8,12},{12,8},{16,20},{20,16},{24,28},{28,24},{1,5},{5... | collective-permute-start | bytes 1572872 | tf_op jit(solution)/shard_map/ppermute | solution.py:644
  135.8 12.9 %collective-permute-start.37 = (bf16[128,2048]{1,0:T(8,128)(2,1)}, bf16[128,2048]{1,0:T(8,128)(2,1)S(1)}, u32[]{:S(2)}, u32[]{:S(2)}) collective-permute-start(bf16[128,2048]{1,0:T(8,128)(2,1)} %get-tuple-element.86.refs_5_), channel_id=1, source_target_pairs={{0,24},{1,25},{2,26},{3,27},{8,0},{9,1},{10,2},{11,3},{16,8},{17,9... | collective-permute-start | bytes 1572872 | tf_op jit(solution)/shard_map/ppermute | solution.py:636
  138.2 9.0 %collective-permute-start.41 = (bf16[144,256]{1,0:T(8,128)(2,1)S(1)}, bf16[144,256]{1,0:T(8,128)(2,1)S(1)}, u32[]{:S(2)}, u32[]{:S(2)}) collective-permute-start(bf16[144,256]{1,0:T(8,128)(2,1)S(1)} %get-tuple-element.90), channel_id=1, source_target_pairs={{0,4},{4,0},{8,12},{12,8},{16,20},{20,16},{24,28},{28,24},{1,5},{5... | collective-permute-start | bytes 221192 | tf_op jit(solution)/shard_map/ppermute | solution.py:644
  139.7 9.0 %collective-permute-start.38 = (bf16[64,128]{1,0:T(8,128)(2,1)}, bf16[64,128]{1,0:T(8,128)(2,1)S(1)}, u32[]{:S(2)}, u32[]{:S(2)}) collective-permute-start(bf16[64,128]{1,0:T(8,128)(2,1)} %get-tuple-element.89.refs_0_), channel_id=1, source_target_pairs={{0,1},{1,2},{2,3},{3,0},{8,9},{9,10},{10,11},{11,8},{16,17},{17,18... | collective-permute-start | bytes 49160 | tf_op jit(solution)/shard_map/ppermute | solution.py:628
  140.0 8.7 %collective-permute-start.39 = (bf16[64,128]{1,0:T(8,128)(2,1)}, bf16[64,128]{1,0:T(8,128)(2,1)S(1)}, u32[]{:S(2)}, u32[]{:S(2)}) collective-permute-start(bf16[64,128]{1,0:T(8,128)(2,1)} %get-tuple-element.89.refs_0_), channel_id=1, source_target_pairs={{0,2},{1,3},{2,0},{3,1},{8,10},{9,11},{10,8},{11,9},{16,18},{17,19... | collective-permute-start | bytes 49160 | tf_op jit(solution)/shard_map/ppermute | solution.py:628
  143.3 5.4 %collective-permute-start.40 = (bf16[64,128]{1,0:T(8,128)(2,1)}, bf16[64,128]{1,0:T(8,128)(2,1)S(1)}, u32[]{:S(2)}, u32[]{:S(2)}) collective-permute-start(bf16[64,128]{1,0:T(8,128)(2,1)} %get-tuple-element.89.refs_0_), channel_id=1, source_target_pairs={{0,3},{1,0},{2,1},{3,2},{8,11},{9,8},{10,9},{11,10},{16,19},{17,16... | collective-permute-start | bytes 49160 | tf_op jit(solution)/shard_map/ppermute | solution.py:628
  (10 other events, 153.7 us)

commit v5 on v4

--- a/solution.py
+++ b/solution.py
@@ -698,7 +698,7 @@
         "split_first",
     )
     other = {s: partner(after(mine[s], lse), later) for s in turns}
-    weights = after(weights, *other.values())
+    weights = after(weights, *other.values(), mine_late)
 
     shared = [queries[0], cos, sin, acc, lse, line, spots]
     n_a = len(a_blocks)
@@ -729,7 +729,7 @@
     )
     h_prev = h_new = hidden
     for l in later:
-        lows = [onward(low, s, 1, [0] if l == 1 else range(n_sec)) for s in range(n_tp)]
+        lows = [onward(low, s, 1, [l - 1]) for s in range(n_tp)]
         if l == 2 and paired:
             leaving = partner(after(leaving, low))
         h_new, *parts = section_slice(

time: 151 us -> 148 us (0.980); the launches traced: 151 us -> 145 us
  starting transfers between devices: 77.7 us -> 65.3 us
  waiting for transfers between devices: 42.3 us -> 48.4 us
    ppermute x18, starting transfers between devices: 43 us -> 33.5 us  [onward(): return lax.ppermute(x, ('pipe', 'tp'), pairs)]
    ppermute x18, waiting for transfers between devices: 12.6 us -> 15.8 us  [onward(): return lax.ppermute(x, ('pipe', 'tp'), pairs)]
    ppermute x17, starting transfers between devices: 25.6 us -> 22.4 us  [around(): return lax.ppermute(x, ('pipe', 'tp'), pairs)]
    ppermute x8, waiting for transfers between devices: 1.45 us -> 3.01 us  [partner(): return lax.ppermute(x, ('pipe', 'req'), pairs)]
  transfers between devices with their start and end apart: 43 -> 43, of which waited for: 16 -> 12; matrix products, arithmetic and copies ran while one was open for 1% -> 1% of each run, Pallas kernels for 16% -> 16%
where the time goes in v5:
time: 148 us; the launch traced here: 145 us
  starting transfers between devices  65.3 us (44%)
  waiting for transfers between devices  48.4 us (33%)
  Pallas kernels  28.4 us (19%)
  local copies, waits for them, and re-layouts  1.99 us (1%)
    ppermute x18, starting transfers between devices, onward(): return lax.ppermute(x, ('pipe', 'tp'), pairs)  33.5 us
    ppermute x17, waiting for transfers between devices, around(): return lax.ppermute(x, ('pipe', 'tp'), pairs)  29.7 us
    ppermute x17, starting transfers between devices, around(): return lax.ppermute(x, ('pipe', 'tp'), pairs)  22.4 us
    ppermute x18, waiting for transfers between devices, onward(): return lax.ppermute(x, ('pipe', 'tp'), pairs)  15.8 us
    ppermute x8, starting transfers between devices, partner(): return lax.ppermute(x, ('pipe', 'req'), pairs)  9.43 us
    pallas_call x4, Pallas kernels, attend_call(): pl.pallas_call(kernel, in_specs=[SM] + [VM] * (len(operands) - 1) + [ANY]...  7.53 us
    pallas_call x1, Pallas kernels, local_work(): pl.pallas_call(functools.partial(local_kernel, paired, adapters), in_spec...  7.19 us
    pallas_call x4, Pallas kernels, split_parts(): pl.pallas_call(functools.partial(split_kernel, chunks, section_of), in_sp...  4.65 us
  transfers between devices with their start and end apart: 43, of which 12 were waited for; matrix products, arithmetic and copies ran while one was open for 1% of the time, Pallas kernels for 16%

profile of v5, /device:TPU:0, one launch (start us, length us, event | category | flops | bytes accessed | tf_op | source)
XLA Modules:
  0.0 145.5 jit_solution(17096366222000178773)
XLA Ops:
  0.7 3.0 %collective-permute-start.5 = (bf16[256,2048]{1,0:T(8,128)(2,1)}, bf16[256,2048]{1,0:T(8,128)(2,1)S(1)}, u32[]{:S(2)}, u32[]{:S(2)}) collective-permute-start(bf16[256,2048]{1,0:T(8,128)(2,1)} %bitcast.14), channel_id=1, source_target_pairs={{0,4},{4,0},{8,12},{12,8},{16,20},{20,16},{24,28},{28,24},{1,5},{5... | collective-permute-start | bytes 3145736 | tf_op jit(solution)/shard_map/ppermute | solution.py:644
  3.8 2.4 %parcels.1 = (bf16[2048,128]{1,0:T(8,128)(2,1)}, bf16[2048,128]{1,0:T(8,128)(2,1)S(1)}, bf16[2048,128]{1,0:T(8,128)(2,1)}) custom-call(s32[4]{0:T(128)S(1)} %pad_add_fusion.sec_ref, bf16[128,2048]{1,0:T(8,128)(2,1)} %refs_9_.1, bf16[16384,128]{1,0:T(8,128)(2,1)} %bitcast.17), custom_call_target="tpu_custom_call" | custom-call | bytes 6000000 | tf_op jit(solution)/shard_map/parcels/pallas_call | solution.py:122
  6.2 0.8 copy-done.8
  7.0 1.6 %collective-permute-start = (bf16[2048,128]{1,0:T(8,128)(2,1)}, bf16[2048,128]{1,0:T(8,128)(2,1)S(1)}, u32[]{:S(2)}, u32[]{:S(2)}) collective-permute-start(bf16[2048,128]{1,0:T(8,128)(2,1)} %get-tuple-element.48), channel_id=1, source_target_pairs={{0,1},{1,2},{2,3},{3,0},{8,9},{9,10},{10,11},{11,8},{16,17},{17,18... | collective-permute-start | bytes 1572872 | tf_op jit(solution)/shard_map/ppermute | solution.py:628
  8.5 2.2 %collective-permute-start.3 = (bf16[2048,128]{1,0:T(8,128)(2,1)}, bf16[2048,128]{1,0:T(8,128)(2,1)S(1)}, u32[]{:S(2)}, u32[]{:S(2)}) collective-permute-start(bf16[2048,128]{1,0:T(8,128)(2,1)} %get-tuple-element.49), channel_id=1, source_target_pairs={{0,3},{1,0},{2,1},{3,2},{8,11},{9,8},{10,9},{11,10},{16,19},{17,16... | collective-permute-start | bytes 1572872 | tf_op jit(solution)/shard_map/ppermute | solution.py:628
  10.8 1.4 collective-permute-start.1
  13.0 7.2 %local_work.1 = (f32[8,128,128]{2,1,0:T(8,128)S(1)}, f32[8,128]{1,0:T(8,128)S(1)}, f32[8,128]{1,0:T(8,128)S(1)}, s32[128,128]{1,0:T(8,128)S(1)}, f32[128,128]{1,...) custom-call(s32[4]{0:T(128)S(1)} %pad_add_fusion.sec_ref, ...), custom_call_target="tpu_custom_call" | custom-call | bytes 900000 | tf_op jit(solution)/shard_map/local_work/pallas_call | solution.py:267
  20.2 3.6 %collective-permute-done.refs_1_ = bf16[2048,128]{1,0:T(8,128)(2,1)S(1)} collective-permute-done((bf16[2048,128]{1,0:T(8,128)(2,1)}, bf16[2048,128]{1,0:T(8,128)(2,1)S(1)}, u32[]{:S(2)}, u32[]{:S(2)}) %collective-permute-start) | collective-permute-done | bytes 524320 | tf_op jit(solution)/shard_map/ppermute | solution.py:628
  23.8 0.7 collective-permute-start.13
  24.5 9.7 %collective-permute-done.3.refs_3_ = bf16[2048,128]{1,0:T(8,128)(2,1)S(1)} collective-permute-done((bf16[2048,128]{1,0:T(8,128)(2,1)}, bf16[2048,128]{1,0:T(8,128)(2,1)S(1)}, u32[]{:S(2)}, u32[]{:S(2)}) %collective-permute-start.3) | collective-permute-done | bytes 524320 | tf_op jit(solution)/shard_map/ppermute | solution.py:628
  34.9 0.7 collective-permute-start.7
  35.6 3.0 %collective-permute-done.4.refs_14_.refs_12_ = bf16[256,1024]{1,0:T(8,128)(2,1)} collective-permute-done((bf16[256,1024]{1,0:T(8,128)(2,1)}, bf16[256,1024]{1,0:T(8,128)(2,1)}, u32[]{:S(2)}, u32[]{:S(2)}) %collective-permute-start.4) | collective-permute-done | bytes 524320 | tf_op jit(solution)/shard_map/ppermute | solution.py:644
  38.6 2.6 %collective-permute-start.15 = (bf16[256,2048]{1,0:T(8,128)(2,1)S(1)}, bf16[256,2048]{1,0:T(8,128)(2,1)S(1)}, u32[]{:S(2)}, u32[]{:S(2)}) collective-permute-start(bf16[256,2048]{1,0:T(8,128)(2,1)S(1)} %bitcast.15), channel_id=1, source_target_pairs={{0,8},{1,9},{2,10},{3,11},{8,16},{9,17},{10,18},{11,19},{16,24},{1... | collective-permute-start | bytes 3145736 | tf_op jit(solution)/shard_map/ppermute | solution.py:636
  41.3 12.8 %collective-permute-start.16 = (bf16[256,2048]{1,0:T(8,128)(2,1)S(1)}, bf16[256,2048]{1,0:T(8,128)(2,1)S(1)}, u32[]{:S(2)}, u32[]{:S(2)}) collective-permute-start(bf16[256,2048]{1,0:T(8,128)(2,1)S(1)} %collective-permute-done.5.refs_7_), channel_id=1, source_target_pairs={{0,8},{1,9},{2,10},{3,11},{8,16},{9,17},{10,18},{11,19},{16,24},{1... | collective-permute-start | bytes 3145736 | tf_op jit(solution)/shard_map/ppermute | solution.py:636
  54.1 0.7 collective-permute-start.8
  54.9 1.3 collective-permute-start.2
  56.2 0.7 collective-permute-start.14
  56.9 2.9 %split_first.1.refs_4_ = bf16[8192,256]{1,0:T(8,128)(2,1)S(1)} custom-call(s32[4]{0:T(128)S(1)} %pad_add_fusion.sec_ref, bf16[16384,128]{1,0:T(8,128)(2,1)} %bitcast.18), custom_call_target="tpu_custom_call" | custom-call | bytes 900000 | tf_op jit(solution)/shard_map/split_first/pallas_call | solution.py:75
  59.8 6.3 %collective-permute-done.2.refs_2_ = bf16[128,2048]{1,0:T(8,128)(2,1)S(1)} collective-permute-done((bf16[128,2048]{1,0:T(8,128)(2,1)}, bf16[128,2048]{1,0:T(8,128)(2,1)S(1)}, u32[]{:S(2)}, u32[]{:S(2)}) %collective-permute-start.2) | collective-permute-done | bytes 524320 | tf_op jit(solution)/shard_map/ppermute | solution.py:636
  66.2 5.2 %first_section.1 = (bf16[144,256]{1,0:T(8,128)(2,1)S(1)}, bf16[64,128]{1,0:T(8,128)(2,1)S(1)}) custom-call(s32[4]{0:T(128)S(1)} %pad_add_fusion.sec_ref, bf16[128,2048]{1,0:T(8,128)(2,1)} %refs_9_.1, bf16[2048,128]{1,0:T(8,128)(2,1)S(1)} %collective-permute-done.refs_1_, bf16[128,2048]{1,0:T(8,128)(2,1)S(1)} %collective-permute-done.2.refs_2_, ...), custom_call_target="tpu_custom_call" | custom-call | bytes 15000000 | tf_op jit(solution)/shard_map/first_section/pallas_call | solution.py:415
  71.4 1.3 collective-permute-start.9
  72.7 1.3 collective-permute-start.10
  74.0 1.3 collective-permute-start.11
  75.3 1.3 collective-permute-start.12
  78.0 1.3 section_slice_1.1
  79.3 1.7 %collective-permute-start.17 = (bf16[144,256]{1,0:T(8,128)(2,1)S(1)}, bf16[144,256]{1,0:T(8,128)(2,1)S(1)}, u32[]{:S(2)}, u32[]{:S(2)}) collective-permute-start(bf16[144,256]{1,0:T(8,128)(2,1)S(1)} %get-tuple-element.68), channel_id=1, source_target_pairs={{0,3},{1,0},{2,1},{3,2},{8,11},{9,8},{10,9},{11,10},{16,19},{17,16... | collective-permute-start | bytes 221192 | tf_op jit(solution)/shard_map/ppermute | solution.py:628
  81.4 1.9 %collective-permute-start.19 = (bf16[144,256]{1,0:T(8,128)(2,1)S(1)}, bf16[144,256]{1,0:T(8,128)(2,1)S(1)}, u32[]{:S(2)}, u32[]{:S(2)}) collective-permute-start(bf16[144,256]{1,0:T(8,128)(2,1)S(1)} %get-tuple-element.70), channel_id=1, source_target_pairs={{0,1},{1,2},{2,3},{3,0},{8,9},{9,10},{10,11},{11,8},{16,17},{17,18... | collective-permute-start | bytes 221192 | tf_op jit(solution)/shard_map/ppermute | solution.py:628
  84.1 6.0 %collective-permute-done.18.refs_2_ = bf16[144,256]{1,0:T(8,128)(2,1)S(1)} collective-permute-done((bf16[144,256]{1,0:T(8,128)(2,1)S(1)}, bf16[144,256]{1,0:T(8,128)(2,1)S(1)}, u32[]{:S(2)}, u32[]{:S(2)}) %collective-permute-start.18) | collective-permute-done | bytes 73760 | tf_op jit(solution)/shard_map/ppermute | solution.py:628
  91.8 0.8 collective-permute-start.21
  94.7 4.0 %collective-permute-done.25.refs_8_ = bf16[128,2048]{1,0:T(8,128)(2,1)S(1)} collective-permute-done((bf16[128,2048]{1,0:T(8,128)(2,1)S(1)}, bf16[128,2048]{1,0:T(8,128)(2,1)S(1)}, u32[]{:S(2)}, u32[]{:S(2)}) %collective-permute-start.25) | collective-permute-done | bytes 524320 | tf_op jit(solution)/shard_map/ppermute | solution.py:636
  99.7 1.4 collective-permute-start.27
  101.1 1.9 %collective-permute-start.28 = (bf16[144,256]{1,0:T(8,128)(2,1)S(1)}, bf16[144,256]{1,0:T(8,128)(2,1)S(1)}, u32[]{:S(2)}, u32[]{:S(2)}) collective-permute-start(bf16[144,256]{1,0:T(8,128)(2,1)S(1)} %get-tuple-element.78), channel_id=1, source_target_pairs={{0,1},{1,2},{2,3},{3,0},{8,9},{9,10},{10,11},{11,8},{16,17},{17,18... | collective-permute-start | bytes 221192 | tf_op jit(solution)/shard_map/ppermute | solution.py:628
  103.0 1.1 collective-permute-done.26.refs_1_
  104.2 1.4 collective-permute-done.27.refs_2_
  105.5 3.2 %collective-permute-done.28.refs_3_ = bf16[144,256]{1,0:T(8,128)(2,1)S(1)} collective-permute-done((bf16[144,256]{1,0:T(8,128)(2,1)S(1)}, bf16[144,256]{1,0:T(8,128)(2,1)S(1)}, u32[]{:S(2)}, u32[]{:S(2)}) %collective-permute-start.28) | collective-permute-done | bytes 73760 | tf_op jit(solution)/shard_map/ppermute | solution.py:628
  112.1 5.2 %collective-permute-done.33.refs_8_ = bf16[128,2048]{1,0:T(8,128)(2,1)S(1)} collective-permute-done((bf16[128,2048]{1,0:T(8,128)(2,1)S(1)}, bf16[128,2048]{1,0:T(8,128)(2,1)S(1)}, u32[]{:S(2)}, u32[]{:S(2)}) %collective-permute-start.33) | collective-permute-done | bytes 524320 | tf_op jit(solution)/shard_map/ppermute | solution.py:636
  117.3 1.4 section_slice_3.1
  118.7 1.6 %collective-permute-start.34 = (bf16[144,256]{1,0:T(8,128)(2,1)S(1)}, bf16[144,256]{1,0:T(8,128)(2,1)S(1)}, u32[]{:S(2)}, u32[]{:S(2)}) collective-permute-start(bf16[144,256]{1,0:T(8,128)(2,1)S(1)} %get-tuple-element.83), channel_id=1, source_target_pairs={{0,3},{1,0},{2,1},{3,2},{8,11},{9,8},{10,9},{11,10},{16,19},{17,16... | collective-permute-start | bytes 221192 | tf_op jit(solution)/shard_map/ppermute | solution.py:628
  120.5 2.0 %collective-permute-start.36 = (bf16[144,256]{1,0:T(8,128)(2,1)S(1)}, bf16[144,256]{1,0:T(8,128)(2,1)S(1)}, u32[]{:S(2)}, u32[]{:S(2)}) collective-permute-start(bf16[144,256]{1,0:T(8,128)(2,1)S(1)} %get-tuple-element.85), channel_id=1, source_target_pairs={{0,1},{1,2},{2,3},{3,0},{8,9},{9,10},{10,11},{11,8},{16,17},{17,18... | collective-permute-start | bytes 221192 | tf_op jit(solution)/shard_map/ppermute | solution.py:628
  122.5 2.1 %collective-permute-start.42 = (bf16[16,2,64,128]{3,2,1,0:T(8,128)(2,1)S(1)}, bf16[16,2,64,128]{3,2,1,0:T(8,128)(2,1)S(1)}, u32[]{:S(2)}, u32[]{:S(2)}) collective-permute-start(bf16[16,2,64,128]{3,2,1,0:T(8,128)(2,1)S(1)} %get-tuple-element.92), channel_id=1, source_target_pairs={{0,4},{4,0},{8,12},{12,8},{16,20},{20,16},{24,28},{28,24},{1,5},{5... | collective-permute-start | bytes 1572872 | tf_op jit(solution)/shard_map/ppermute | solution.py:644
  124.6 4.6 %collective-permute-done.35.refs_2_ = bf16[144,256]{1,0:T(8,128)(2,1)S(1)} collective-permute-done((bf16[144,256]{1,0:T(8,128)(2,1)S(1)}, bf16[144,256]{1,0:T(8,128)(2,1)S(1)}, u32[]{:S(2)}, u32[]{:S(2)}) %collective-permute-start.35) | collective-permute-done | bytes 73760 | tf_op jit(solution)/shard_map/ppermute | solution.py:628
  129.2 5.6 %collective-permute-start.37 = (bf16[128,2048]{1,0:T(8,128)(2,1)}, bf16[128,2048]{1,0:T(8,128)(2,1)S(1)}, u32[]{:S(2)}, u32[]{:S(2)}) collective-permute-start(bf16[128,2048]{1,0:T(8,128)(2,1)} %get-tuple-element.86.refs_5_), channel_id=1, source_target_pairs={{0,24},{1,25},{2,26},{3,27},{8,0},{9,1},{10,2},{11,3},{16,8},{17,9... | collective-permute-start | bytes 1572872 | tf_op jit(solution)/shard_map/ppermute | solution.py:636
  134.8 1.2 section_3.1
  136.0 1.2 collective-permute-start.41
  137.2 1.8 %collective-permute-start.39 = (bf16[64,128]{1,0:T(8,128)(2,1)}, bf16[64,128]{1,0:T(8,128)(2,1)S(1)}, u32[]{:S(2)}, u32[]{:S(2)}) collective-permute-start(bf16[64,128]{1,0:T(8,128)(2,1)} %get-tuple-element.89.refs_0_), channel_id=1, source_target_pairs={{0,2},{1,3},{2,0},{3,1},{8,10},{9,11},{10,8},{11,9},{16,18},{17,19... | collective-permute-start | bytes 49160 | tf_op jit(solution)/shard_map/ppermute | solution.py:628
  139.1 2.3 %collective-permute-start.40 = (bf16[64,128]{1,0:T(8,128)(2,1)}, bf16[64,128]{1,0:T(8,128)(2,1)S(1)}, u32[]{:S(2)}, u32[]{:S(2)}) collective-permute-start(bf16[64,128]{1,0:T(8,128)(2,1)} %get-tuple-element.89.refs_0_), channel_id=1, source_target_pairs={{0,3},{1,0},{2,1},{3,2},{8,11},{9,8},{10,9},{11,10},{16,19},{17,16... | collective-permute-start | bytes 49160 | tf_op jit(solution)/shard_map/ppermute | solution.py:628
  142.1 1.5 %insert_new.1 = bf16[1,16,2,64,128]{4,3,2,1,0:T(8,128)(2,1)} custom-call(bf16[144,256]{1,0:T(8,128)(2,1)S(1)} %collective-permute-done.41.new_ref, bf16[16,2,64,128]{3,2,1,0:T(8,128)(2,1)S(1)} %collective-permute-done.42.old_ref), custom_call_target="tpu_custom_call" | custom-call | bytes 9000000 | tf_op jit(solution)/shard_map/insert_new/pallas_call | solution.py:591
  143.6 1.9 %section_result.1 = bf16[1,128,2048]{2,1,0:T(8,128)(2,1)} custom-call(s32[4]{0:T(128)S(1)} %pad_add_fusion.sec_ref, bf16[128,2048]{1,0:T(8,128)(2,1)S(1)} %collective-permute-done.37.back_ref, bf16[64,128]{1,0:T(8,128)(2,1)} %get-tuple-element.89.refs_0_, bf16[64,128]{1,0:T(8,128)(2,1)S(1)} %collective-permute-done.38.refs_1_, ...), custom_call_target="tpu_custom_call" | custom-call | bytes 9000000 | tf_op jit(solution)/shard_map/section_result/pallas_call | solution.py:559
  (96 shorter events, 12.9 us)
Async XLA Ops:
  0.7 40.6 %collective-permute-start.5 = (bf16[256,2048]{1,0:T(8,128)(2,1)}, bf16[256,2048]{1,0:T(8,128)(2,1)S(1)}, u32[]{:S(2)}, u32[]{:S(2)}) collective-permute-start(bf16[256,2048]{1,0:T(8,128)(2,1)} %bitcast.14), channel_id=1, source_target_pairs={{0,4},{4,0},{8,12},{12,8},{16,20},{20,16},{24,28},{28,24},{1,5},{5... | collective-permute-start | bytes 3145736 | tf_op jit(solution)/shard_map/ppermute | solution.py:644
  3.8 34.9 %copy-start.3 = (bf16[1,4,64,2048]{3,2,1,0:T(8,128)(2,1)S(1)}, bf16[1,4,64,2048]{3,2,1,0:T(8,128)(2,1)}, u32[]{:S(2)}) copy-start(bf16[1,4,64,2048]{3,2,1,0:T(8,128)(2,1)} %param.17) | copy-start | bytes 3145732
  7.0 16.9 %collective-permute-start = (bf16[2048,128]{1,0:T(8,128)(2,1)}, bf16[2048,128]{1,0:T(8,128)(2,1)S(1)}, u32[]{:S(2)}, u32[]{:S(2)}) collective-permute-start(bf16[2048,128]{1,0:T(8,128)(2,1)} %get-tuple-element.48), channel_id=1, source_target_pairs={{0,1},{1,2},{2,3},{3,0},{8,9},{9,10},{10,11},{11,8},{16,17},{17,18... | collective-permute-start | bytes 1572872 | tf_op jit(solution)/shard_map/ppermute | solution.py:628
  8.5 25.7 %collective-permute-start.3 = (bf16[2048,128]{1,0:T(8,128)(2,1)}, bf16[2048,128]{1,0:T(8,128)(2,1)S(1)}, u32[]{:S(2)}, u32[]{:S(2)}) collective-permute-start(bf16[2048,128]{1,0:T(8,128)(2,1)} %get-tuple-element.49), channel_id=1, source_target_pairs={{0,3},{1,0},{2,1},{3,2},{8,11},{9,8},{10,9},{11,10},{16,19},{17,16... | collective-permute-start | bytes 1572872 | tf_op jit(solution)/shard_map/ppermute | solution.py:628
  10.8 24.2 %collective-permute-start.1 = (bf16[128,2048]{1,0:T(8,128)(2,1)}, bf16[128,2048]{1,0:T(8,128)(2,1)}, u32[]{:S(2)}, u32[]{:S(2)}) collective-permute-start(bf16[128,2048]{1,0:T(8,128)(2,1)} %refs_9_.1), channel_id=1, source_target_pairs={{16,18},{17,19},{18,16},{19,17},{20,22},{21,23},{22,20},{23,21}} | collective-permute-start | bytes 1572872 | tf_op jit(solution)/shard_map/ppermute | solution.py:628
  12.2 26.4 %collective-permute-start.4 = (bf16[256,1024]{1,0:T(8,128)(2,1)}, bf16[256,1024]{1,0:T(8,128)(2,1)}, u32[]{:S(2)}, u32[]{:S(2)}) collective-permute-start(bf16[256,1024]{1,0:T(8,128)(2,1)} %bitcast.7.refs_13_.refs_11_), channel_id=1, source_target_pairs={{0,4},{4,0},{8,12},{12,8},{16,20},{20,16},{24,28},{28,24},{1,5},{5... | collective-permute-start | bytes 1572872 | tf_op jit(solution)/shard_map/ppermute | solution.py:644
  23.8 42.3 %copy-start.1 = (bf16[2048,128]{1,0:T(8,128)(2,1)}, bf16[2048,128]{1,0:T(8,128)(2,1)S(1)}, u32[]{:S(2)}) copy-start(bf16[2048,128]{1,0:T(8,128)(2,1)S(1)} %collective-permute-done.refs_1_) | copy-start | bytes 1572868
  23.8 30.3 %collective-permute-start.13 = (bf16[2048,128]{1,0:T(8,128)(2,1)S(1)}, bf16[2048,128]{1,0:T(8,128)(2,1)S(1)}, u32[]{:S(2)}, u32[]{:S(2)}) collective-permute-start(bf16[2048,128]{1,0:T(8,128)(2,1)S(1)} %copy-done.9), channel_id=1, source_target_pairs={{8,10},{9,11},{10,8},{11,9},{12,14},{13,15},{14,12},{15,13}} | collective-permute-start | bytes 1572872 | tf_op jit(solution)/shard_map/ppermute | solution.py:628
  24.5 41.6 %copy-start.4 = (bf16[1,8192]{1,0:T(2,128)(2,1)S(1)}, bf16[1,8192]{1,0:T(2,128)(2,1)}, u32[]{:S(2)}) copy-start(bf16[1,8192]{1,0:T(2,128)(2,1)} %refs_5_.7) | copy-start | bytes 49156
  34.2 31.9 %copy-start.2 = (bf16[2048,128]{1,0:T(8,128)(2,1)}, bf16[2048,128]{1,0:T(8,128)(2,1)S(1)}, u32[]{:S(2)}) copy-start(bf16[2048,128]{1,0:T(8,128)(2,1)S(1)} %collective-permute-done.3.refs_3_) | copy-start | bytes 1572868
  34.2 20.6 %collective-permute-start.6 = (bf16[2048,128]{1,0:T(8,128)(2,1)S(1)}, bf16[2048,128]{1,0:T(8,128)(2,1)S(1)}, u32[]{:S(2)}, u32[]{:S(2)}) collective-permute-start(bf16[2048,128]{1,0:T(8,128)(2,1)S(1)} %collective-permute-done.refs_1_), channel_id=1, source_target_pairs={{8,12},{12,8},{16,20},{20,16},{24,28},{28,24},{9,13},{13,9},{17,21... | collective-permute-start | bytes 1572872 | tf_op jit(solution)/shard_map/ppermute | solution.py:644
  34.9 21.2 %collective-permute-start.7 = (bf16[2048,128]{1,0:T(8,128)(2,1)S(1)}, bf16[2048,128]{1,0:T(8,128)(2,1)S(1)}, u32[]{:S(2)}, u32[]{:S(2)}) collective-permute-start(bf16[2048,128]{1,0:T(8,128)(2,1)S(1)} %collective-permute-done.3.refs_3_), channel_id=1, source_target_pairs={{8,12},{12,8},{16,20},{20,16},{24,28},{28,24},{9,13},{13,9},{17,21... | collective-permute-start | bytes 1572872 | tf_op jit(solution)/shard_map/ppermute | solution.py:644
  38.6 36.6 %collective-permute-start.15 = (bf16[256,2048]{1,0:T(8,128)(2,1)S(1)}, bf16[256,2048]{1,0:T(8,128)(2,1)S(1)}, u32[]{:S(2)}, u32[]{:S(2)}) collective-permute-start(bf16[256,2048]{1,0:T(8,128)(2,1)S(1)} %bitcast.15), channel_id=1, source_target_pairs={{0,8},{1,9},{2,10},{3,11},{8,16},{9,17},{10,18},{11,19},{16,24},{1... | collective-permute-start | bytes 3145736 | tf_op jit(solution)/shard_map/ppermute | solution.py:636
  41.3 36.7 %collective-permute-start.16 = (bf16[256,2048]{1,0:T(8,128)(2,1)S(1)}, bf16[256,2048]{1,0:T(8,128)(2,1)S(1)}, u32[]{:S(2)}, u32[]{:S(2)}) collective-permute-start(bf16[256,2048]{1,0:T(8,128)(2,1)S(1)} %collective-permute-done.5.refs_7_), channel_id=1, source_target_pairs={{0,8},{1,9},{2,10},{3,11},{8,16},{9,17},{10,18},{11,19},{16,24},{1... | collective-permute-start | bytes 3145736 | tf_op jit(solution)/shard_map/ppermute | solution.py:636
  54.1 5.7 %collective-permute-start.8 = (bf16[2048,128]{1,0:T(8,128)(2,1)S(1)}, bf16[2048,128]{1,0:T(8,128)(2,1)S(1)}, u32[]{:S(2)}, u32[]{:S(2)}) collective-permute-start(bf16[2048,128]{1,0:T(8,128)(2,1)S(1)} %copy-done.9), channel_id=1, source_target_pairs={{16,18},{17,19},{18,16},{19,17},{24,26},{25,27},{26,24},{27,25},{2... | collective-permute-start | bytes 1572872 | tf_op jit(solution)/shard_map/ppermute | solution.py:628
  54.9 11.3 %collective-permute-start.2 = (bf16[128,2048]{1,0:T(8,128)(2,1)}, bf16[128,2048]{1,0:T(8,128)(2,1)S(1)}, u32[]{:S(2)}, u32[]{:S(2)}) collective-permute-start(bf16[128,2048]{1,0:T(8,128)(2,1)} %collective-permute-done.1), channel_id=1, source_target_pairs={{16,0},{17,1},{18,2},{19,3},{20,4},{21,5},{22,6},{23,7}} | collective-permute-start | bytes 1572872 | tf_op jit(solution)/shard_map/ppermute | solution.py:636
  56.2 17.8 %collective-permute-start.14 = (bf16[2048,128]{1,0:T(8,128)(2,1)S(1)}, bf16[2048,128]{1,0:T(8,128)(2,1)S(1)}, u32[]{:S(2)}, u32[]{:S(2)}) collective-permute-start(bf16[2048,128]{1,0:T(8,128)(2,1)S(1)} %collective-permute-done.13.refs_0_), channel_id=1, source_target_pairs={{8,12},{12,8},{9,13},{13,9},{10,14},{14,10},{11,15},{15,11}} | collective-permute-start | bytes 1572872 | tf_op jit(solution)/shard_map/ppermute | solution.py:644
  59.8 23.5 %copy-start.10 = (bf16[2048,128]{1,0:T(8,128)(2,1)}, bf16[2048,128]{1,0:T(8,128)(2,1)S(1)}, u32[]{:S(2)}) copy-start(bf16[2048,128]{1,0:T(8,128)(2,1)S(1)} %collective-permute-done.8.refs_0_) | copy-start | bytes 1572868
  71.4 6.4 %collective-permute-start.9 = (bf16[64,128]{1,0:T(8,128)(2,1)S(1)}, bf16[64,128]{1,0:T(8,128)(2,1)S(1)}, u32[]{:S(2)}, u32[]{:S(2)}) collective-permute-start(bf16[64,128]{1,0:T(8,128)(2,1)S(1)} %get-tuple-element.63), channel_id=1, source_target_pairs={{0,8},{1,9},{2,10},{3,11},{4,12},{5,13},{6,14},{7,15}} | collective-permute-start | bytes 49160 | tf_op jit(solution)/shard_map/ppermute | solution.py:636
  72.7 5.1 %collective-permute-start.10 = (bf16[64,128]{1,0:T(8,128)(2,1)S(1)}, bf16[64,128]{1,0:T(8,128)(2,1)S(1)}, u32[]{:S(2)}, u32[]{:S(2)}) collective-permute-start(bf16[64,128]{1,0:T(8,128)(2,1)S(1)} %get-tuple-element.63), channel_id=1, source_target_pairs={{0,9},{1,10},{2,11},{3,8},{4,13},{5,14},{6,15},{7,12}} | collective-permute-start | bytes 49160 | tf_op jit(solution)/shard_map/ppermute | solution.py:636
  74.0 3.8 %collective-permute-start.11 = (bf16[64,128]{1,0:T(8,128)(2,1)S(1)}, bf16[64,128]{1,0:T(8,128)(2,1)S(1)}, u32[]{:S(2)}, u32[]{:S(2)}) collective-permute-start(bf16[64,128]{1,0:T(8,128)(2,1)S(1)} %get-tuple-element.63), channel_id=1, source_target_pairs={{0,10},{1,11},{2,8},{3,9},{4,14},{5,15},{6,12},{7,13}} | collective-permute-start | bytes 49160 | tf_op jit(solution)/shard_map/ppermute | solution.py:636
  75.3 2.7 %collective-permute-start.12 = (bf16[64,128]{1,0:T(8,128)(2,1)S(1)}, bf16[64,128]{1,0:T(8,128)(2,1)S(1)}, u32[]{:S(2)}, u32[]{:S(2)}) collective-permute-start(bf16[64,128]{1,0:T(8,128)(2,1)S(1)} %get-tuple-element.63), channel_id=1, source_target_pairs={{0,11},{1,8},{2,9},{3,10},{4,15},{5,12},{6,13},{7,14}} | collective-permute-start | bytes 49160 | tf_op jit(solution)/shard_map/ppermute | solution.py:636
  79.3 4.8 %collective-permute-start.17 = (bf16[144,256]{1,0:T(8,128)(2,1)S(1)}, bf16[144,256]{1,0:T(8,128)(2,1)S(1)}, u32[]{:S(2)}, u32[]{:S(2)}) collective-permute-start(bf16[144,256]{1,0:T(8,128)(2,1)S(1)} %get-tuple-element.68), channel_id=1, source_target_pairs={{0,3},{1,0},{2,1},{3,2},{8,11},{9,8},{10,9},{11,10},{16,19},{17,16... | collective-permute-start | bytes 221192 | tf_op jit(solution)/shard_map/ppermute | solution.py:628
  81.0 9.1 %collective-permute-start.18 = (bf16[144,256]{1,0:T(8,128)(2,1)S(1)}, bf16[144,256]{1,0:T(8,128)(2,1)S(1)}, u32[]{:S(2)}, u32[]{:S(2)}) collective-permute-start(bf16[144,256]{1,0:T(8,128)(2,1)S(1)} %get-tuple-element.69), channel_id=1, source_target_pairs={{0,2},{1,3},{2,0},{3,1},{8,10},{9,11},{10,8},{11,9},{16,18},{17,19... | collective-permute-start | bytes 221192 | tf_op jit(solution)/shard_map/ppermute | solution.py:628
  81.4 8.7 %collective-permute-start.19 = (bf16[144,256]{1,0:T(8,128)(2,1)S(1)}, bf16[144,256]{1,0:T(8,128)(2,1)S(1)}, u32[]{:S(2)}, u32[]{:S(2)}) collective-permute-start(bf16[144,256]{1,0:T(8,128)(2,1)S(1)} %get-tuple-element.70), channel_id=1, source_target_pairs={{0,1},{1,2},{2,3},{3,0},{8,9},{9,10},{10,11},{11,8},{16,17},{17,18... | collective-permute-start | bytes 221192 | tf_op jit(solution)/shard_map/ppermute | solution.py:628
  83.4 9.9 %collective-permute-start.24 = (bf16[2048,128]{1,0:T(8,128)(2,1)S(1)}, bf16[2048,128]{1,0:T(8,128)(2,1)S(1)}, u32[]{:S(2)}, u32[]{:S(2)}) collective-permute-start(bf16[2048,128]{1,0:T(8,128)(2,1)S(1)} %collective-permute-done.8.refs_0_), channel_id=1, source_target_pairs={{16,20},{20,16},{24,28},{28,24},{17,21},{21,17},{25,29},{29,25},{1... | collective-permute-start | bytes 1572872 | tf_op jit(solution)/shard_map/ppermute | solution.py:644
  90.1 8.6 %collective-permute-start.25 = (bf16[128,2048]{1,0:T(8,128)(2,1)S(1)}, bf16[128,2048]{1,0:T(8,128)(2,1)S(1)}, u32[]{:S(2)}, u32[]{:S(2)}) collective-permute-start(bf16[128,2048]{1,0:T(8,128)(2,1)S(1)} %get-tuple-element.74.refs_9_), channel_id=1, source_target_pairs={{0,8},{1,9},{2,10},{3,11},{8,16},{9,17},{10,18},{11,19},{16,24},{1... | collective-permute-start | bytes 1572872 | tf_op jit(solution)/shard_map/ppermute | solution.py:636
  91.1 3.6 %collective-permute-start.20 = (bf16[64,128]{1,0:T(8,128)(2,1)S(1)}, bf16[64,128]{1,0:T(8,128)(2,1)S(1)}, u32[]{:S(2)}, u32[]{:S(2)}) collective-permute-start(bf16[64,128]{1,0:T(8,128)(2,1)S(1)} %get-tuple-element.72), channel_id=1, source_target_pairs={{8,16},{9,17},{10,18},{11,19},{12,20},{13,21},{14,22},{15,23}} | collective-permute-start | bytes 49160 | tf_op jit(solution)/shard_map/ppermute | solution.py:636
  91.8 2.9 %collective-permute-start.21 = (bf16[64,128]{1,0:T(8,128)(2,1)S(1)}, bf16[64,128]{1,0:T(8,128)(2,1)S(1)}, u32[]{:S(2)}, u32[]{:S(2)}) collective-permute-start(bf16[64,128]{1,0:T(8,128)(2,1)S(1)} %get-tuple-element.72), channel_id=1, source_target_pairs={{8,17},{9,18},{10,19},{11,16},{12,21},{13,22},{14,23},{15,20}} | collective-permute-start | bytes 49160 | tf_op jit(solution)/shard_map/ppermute | solution.py:636
  92.6 2.1 %collective-permute-start.22 = (bf16[64,128]{1,0:T(8,128)(2,1)S(1)}, bf16[64,128]{1,0:T(8,128)(2,1)S(1)}, u32[]{:S(2)}, u32[]{:S(2)}) collective-permute-start(bf16[64,128]{1,0:T(8,128)(2,1)S(1)} %get-tuple-element.72), channel_id=1, source_target_pairs={{8,18},{9,19},{10,16},{11,17},{12,22},{13,23},{14,20},{15,21}} | collective-permute-start | bytes 49160 | tf_op jit(solution)/shard_map/ppermute | solution.py:636
  93.3 1.4 collective-permute-start.23
  99.3 4.9 %collective-permute-start.26 = (bf16[144,256]{1,0:T(8,128)(2,1)S(1)}, bf16[144,256]{1,0:T(8,128)(2,1)S(1)}, u32[]{:S(2)}, u32[]{:S(2)}) collective-permute-start(bf16[144,256]{1,0:T(8,128)(2,1)S(1)} %get-tuple-element.76), channel_id=1, source_target_pairs={{0,3},{1,0},{2,1},{3,2},{8,11},{9,8},{10,9},{11,10},{16,19},{17,16... | collective-permute-start | bytes 221192 | tf_op jit(solution)/shard_map/ppermute | solution.py:628
  99.7 5.8 %collective-permute-start.27 = (bf16[144,256]{1,0:T(8,128)(2,1)S(1)}, bf16[144,256]{1,0:T(8,128)(2,1)S(1)}, u32[]{:S(2)}, u32[]{:S(2)}) collective-permute-start(bf16[144,256]{1,0:T(8,128)(2,1)S(1)} %get-tuple-element.77), channel_id=1, source_target_pairs={{0,2},{1,3},{2,0},{3,1},{8,10},{9,11},{10,8},{11,9},{16,18},{17,19... | collective-permute-start | bytes 221192 | tf_op jit(solution)/shard_map/ppermute | solution.py:628
  101.1 7.6 %collective-permute-start.28 = (bf16[144,256]{1,0:T(8,128)(2,1)S(1)}, bf16[144,256]{1,0:T(8,128)(2,1)S(1)}, u32[]{:S(2)}, u32[]{:S(2)}) collective-permute-start(bf16[144,256]{1,0:T(8,128)(2,1)S(1)} %get-tuple-element.78), channel_id=1, source_target_pairs={{0,1},{1,2},{2,3},{3,0},{8,9},{9,10},{10,11},{11,8},{16,17},{17,18... | collective-permute-start | bytes 221192 | tf_op jit(solution)/shard_map/ppermute | solution.py:628
  108.7 8.6 %collective-permute-start.33 = (bf16[128,2048]{1,0:T(8,128)(2,1)S(1)}, bf16[128,2048]{1,0:T(8,128)(2,1)S(1)}, u32[]{:S(2)}, u32[]{:S(2)}) collective-permute-start(bf16[128,2048]{1,0:T(8,128)(2,1)S(1)} %get-tuple-element.81.refs_9_), channel_id=1, source_target_pairs={{0,8},{1,9},{2,10},{3,11},{8,16},{9,17},{10,18},{11,19},{16,24},{1... | collective-permute-start | bytes 1572872 | tf_op jit(solution)/shard_map/ppermute | solution.py:636
  109.3 2.7 %collective-permute-start.29 = (bf16[64,128]{1,0:T(8,128)(2,1)S(1)}, bf16[64,128]{1,0:T(8,128)(2,1)S(1)}, u32[]{:S(2)}, u32[]{:S(2)}) collective-permute-start(bf16[64,128]{1,0:T(8,128)(2,1)S(1)} %get-tuple-element.79), channel_id=1, source_target_pairs={{16,24},{17,25},{18,26},{19,27},{20,28},{21,29},{22,30},{23,31}} | collective-permute-start | bytes 49160 | tf_op jit(solution)/shard_map/ppermute | solution.py:636
  110.0 2.0 %collective-permute-start.30 = (bf16[64,128]{1,0:T(8,128)(2,1)S(1)}, bf16[64,128]{1,0:T(8,128)(2,1)S(1)}, u32[]{:S(2)}, u32[]{:S(2)}) collective-permute-start(bf16[64,128]{1,0:T(8,128)(2,1)S(1)} %get-tuple-element.79), channel_id=1, source_target_pairs={{16,25},{17,26},{18,27},{19,24},{20,29},{21,30},{22,31},{23,28}} | collective-permute-start | bytes 49160 | tf_op jit(solution)/shard_map/ppermute | solution.py:636
  110.7 1.4 collective-permute-start.31
  111.3 0.7 collective-permute-start.32
  118.7 6.0 %collective-permute-start.34 = (bf16[144,256]{1,0:T(8,128)(2,1)S(1)}, bf16[144,256]{1,0:T(8,128)(2,1)S(1)}, u32[]{:S(2)}, u32[]{:S(2)}) collective-permute-start(bf16[144,256]{1,0:T(8,128)(2,1)S(1)} %get-tuple-element.83), channel_id=1, source_target_pairs={{0,3},{1,0},{2,1},{3,2},{8,11},{9,8},{10,9},{11,10},{16,19},{17,16... | collective-permute-start | bytes 221192 | tf_op jit(solution)/shard_map/ppermute | solution.py:628
  120.3 9.0 %collective-permute-start.35 = (bf16[144,256]{1,0:T(8,128)(2,1)S(1)}, bf16[144,256]{1,0:T(8,128)(2,1)S(1)}, u32[]{:S(2)}, u32[]{:S(2)}) collective-permute-start(bf16[144,256]{1,0:T(8,128)(2,1)S(1)} %get-tuple-element.84), channel_id=1, source_target_pairs={{0,2},{1,3},{2,0},{3,1},{8,10},{9,11},{10,8},{11,9},{16,18},{17,19... | collective-permute-start | bytes 221192 | tf_op jit(solution)/shard_map/ppermute | solution.py:628
  120.5 8.8 %collective-permute-start.36 = (bf16[144,256]{1,0:T(8,128)(2,1)S(1)}, bf16[144,256]{1,0:T(8,128)(2,1)S(1)}, u32[]{:S(2)}, u32[]{:S(2)}) collective-permute-start(bf16[144,256]{1,0:T(8,128)(2,1)S(1)} %get-tuple-element.85), channel_id=1, source_target_pairs={{0,1},{1,2},{2,3},{3,0},{8,9},{9,10},{10,11},{11,8},{16,17},{17,18... | collective-permute-start | bytes 221192 | tf_op jit(solution)/shard_map/ppermute | solution.py:628
  122.5 16.6 %collective-permute-start.42 = (bf16[16,2,64,128]{3,2,1,0:T(8,128)(2,1)S(1)}, bf16[16,2,64,128]{3,2,1,0:T(8,128)(2,1)S(1)}, u32[]{:S(2)}, u32[]{:S(2)}) collective-permute-start(bf16[16,2,64,128]{3,2,1,0:T(8,128)(2,1)S(1)} %get-tuple-element.92), channel_id=1, source_target_pairs={{0,4},{4,0},{8,12},{12,8},{16,20},{20,16},{24,28},{28,24},{1,5},{5... | collective-permute-start | bytes 1572872 | tf_op jit(solution)/shard_map/ppermute | solution.py:644
  129.2 14.3 %collective-permute-start.37 = (bf16[128,2048]{1,0:T(8,128)(2,1)}, bf16[128,2048]{1,0:T(8,128)(2,1)S(1)}, u32[]{:S(2)}, u32[]{:S(2)}) collective-permute-start(bf16[128,2048]{1,0:T(8,128)(2,1)} %get-tuple-element.86.refs_5_), channel_id=1, source_target_pairs={{0,24},{1,25},{2,26},{3,27},{8,0},{9,1},{10,2},{11,3},{16,8},{17,9... | collective-permute-start | bytes 1572872 | tf_op jit(solution)/shard_map/ppermute | solution.py:636
  136.0 6.0 %collective-permute-start.41 = (bf16[144,256]{1,0:T(8,128)(2,1)S(1)}, bf16[144,256]{1,0:T(8,128)(2,1)S(1)}, u32[]{:S(2)}, u32[]{:S(2)}) collective-permute-start(bf16[144,256]{1,0:T(8,128)(2,1)S(1)} %get-tuple-element.90), channel_id=1, source_target_pairs={{0,4},{4,0},{8,12},{12,8},{16,20},{20,16},{24,28},{28,24},{1,5},{5... | collective-permute-start | bytes 221192 | tf_op jit(solution)/shard_map/ppermute | solution.py:644
  137.2 6.3 %collective-permute-start.38 = (bf16[64,128]{1,0:T(8,128)(2,1)}, bf16[64,128]{1,0:T(8,128)(2,1)S(1)}, u32[]{:S(2)}, u32[]{:S(2)}) collective-permute-start(bf16[64,128]{1,0:T(8,128)(2,1)} %get-tuple-element.89.refs_0_), channel_id=1, source_target_pairs={{0,1},{1,2},{2,3},{3,0},{8,9},{9,10},{10,11},{11,8},{16,17},{17,18... | collective-permute-start | bytes 49160 | tf_op jit(solution)/shard_map/ppermute | solution.py:628
  137.2 6.3 %collective-permute-start.39 = (bf16[64,128]{1,0:T(8,128)(2,1)}, bf16[64,128]{1,0:T(8,128)(2,1)S(1)}, u32[]{:S(2)}, u32[]{:S(2)}) collective-permute-start(bf16[64,128]{1,0:T(8,128)(2,1)} %get-tuple-element.89.refs_0_), channel_id=1, source_target_pairs={{0,2},{1,3},{2,0},{3,1},{8,10},{9,11},{10,8},{11,9},{16,18},{17,19... | collective-permute-start | bytes 49160 | tf_op jit(solution)/shard_map/ppermute | solution.py:628
  139.1 4.5 %collective-permute-start.40 = (bf16[64,128]{1,0:T(8,128)(2,1)}, bf16[64,128]{1,0:T(8,128)(2,1)S(1)}, u32[]{:S(2)}, u32[]{:S(2)}) collective-permute-start(bf16[64,128]{1,0:T(8,128)(2,1)} %get-tuple-element.89.refs_0_), channel_id=1, source_target_pairs={{0,3},{1,0},{2,1},{3,2},{8,11},{9,8},{10,9},{11,10},{16,19},{17,16... | collective-permute-start | bytes 49160 | tf_op jit(solution)/shard_map/ppermute | solution.py:628
  (13 other events, 103.2 us)
